TPU v7x, 32 devices: a whole 2x2x4 slice. The times are simulated.
32 devices in a mesh: replica: 2 (over x), tenant: 16 (over z, y, core).
Axes of the slice: x: 2, y: 2, z: 4, core: 2. Of those that a mesh axis runs over, the one named last changes fastest.
Arguments:
- prefill_rows: bfloat16 [8192, 8192], P(('replica', 'tenant')), parts along dimension 0, may hold values from -6 to 6
- tenant_ids: int32 [8192, 1], P(('replica', 'tenant')), parts along dimension 0, may hold values from 0 to 31; in each aligned block of 256 rows (0 to 255, 256 to 511, ...) at most 16 rows name the same one
- owner_slot: int32 [32], replicated, may hold values from 0 to 31, each once
- decode_rows: bfloat16 [256, 8192], P(('replica', 'tenant')), parts along dimension 0, may hold values from -6 to 6
- queries: bfloat16 [256, 4096], P(('replica', 'tenant')), parts along dimension 0
- key_store_cache: bfloat16 [256, 384, 512], P(('replica', 'tenant')), parts along dimension 0
- value_store_cache: bfloat16 [256, 384, 512], P(('replica', 'tenant')), parts along dimension 0, may hold values from -6 to 6
- context_len: int32 [256], P(('replica', 'tenant')), parts along dimension 0, may hold values from 96 to 384, as said below
- base_weight: bfloat16 [8192, 1024], P('tenant'), may hold values from -0.0625 to 0.0625
- adapter_down: bfloat16 [32, 32, 8192], P('tenant'), may hold values from -0.0625 to 0.0625
- adapter_up: bfloat16 [32, 32, 1024], P('tenant'), may hold values from -1 to 1
Outputs:
- projected: bfloat16 [8192, 1024], P(('replica', 'tenant')), parts along dimension 0
- attended: bfloat16 [256, 4096], P(('replica', 'tenant')), parts along dimension 0
There are 2 independent parts, one for each index of `replica`. A program takes and returns all parts, laid end to end along the dimension named above; an argument that names none is the same for every part. Nothing has to cross between parts.
Inputs may be any that keep to these rules, and one draw needn't show every extreme that they name: `tenant_ids`: the rows of one device name one tenant at most 16 times, and in some device some tenant exactly 16 times. `owner_slot`: each slot is named once. `context_len`: the first decode row of each part has 384.
All inputs are finite; a program needn't handle non-finite values.
Results may differ from a plain program's by a relative error of at most 0.0055.
Values may be sent and summed in bfloat16 or wider, within the bound.
No kernel may reach another device: no remote copies, remote signals or barrier semaphores. Data moves between devices by JAX's collectives and lax.ppermute only.
A program may use at most 128 MiB of HBM per device.

v0:
```python
import math

import jax
import jax.numpy as jnp
from jax import lax
from jax.sharding import PartitionSpec as P

HEAD_SIZE = 128


adapter_scale = 2.0


def send_back(answer):
    return lax.all_to_all(answer, "tenant", split_axis=0, concat_axis=0, tiled=True)


def body(
    prefill_rows,
    tenant_ids,
    owner_slot,
    decode_rows,
    queries,
    key_store_cache,
    value_store_cache,
    context_len,
    base_weight,
    adapter_down,
    adapter_up,
):
    peers = lax.axis_size("tenant")
    local_slots = adapter_down.shape[0]
    tenants = local_slots * peers
    row_count = prefill_rows.shape[0]
    capacity = max(2, 2 * row_count // tenants)
    width = prefill_rows.shape[1]
    out_width = base_weight.shape[1]
    half_width = out_width // 2
    decode_count = decode_rows.shape[0]
    tenant_hot = tenant_ids == jnp.arange(tenants, dtype=jnp.int32)[None, :]
    slot_index = jnp.sum(jnp.where(tenant_hot, owner_slot[None, :], 0), axis=1)
    seen = jnp.cumsum(tenant_hot.astype(jnp.int32), axis=0)
    within = jnp.sum(jnp.where(tenant_hot, seen, 0), axis=1) - 1
    target = slot_index * capacity + within
    outgoing = jnp.zeros((tenants * capacity, width), jnp.bfloat16).at[target].set(prefill_rows)
    outgoing = outgoing.reshape(peers, local_slots, capacity, width)
    piece = lax.all_gather(base_weight, "tenant", axis=0, tiled=True)
    lowered = jnp.einsum(
        "ntcd,trd->ntcr",
        lax.all_to_all(outgoing, "tenant", split_axis=0, concat_axis=0, tiled=True),
        adapter_down,
        preferred_element_type=jnp.float32,
    ).astype(jnp.bfloat16)
    delta = jnp.einsum(
        "ntcr,tre->ntce", lowered, adapter_up, preferred_element_type=jnp.float32
    ).astype(jnp.bfloat16)
    gathered_back = send_back(delta)
    flat_count = gathered_back.size // gathered_back.shape[-1]
    gathered_back = gathered_back.reshape(flat_count, gathered_back.shape[-1])[target]
    projected = (
        jnp.dot(prefill_rows, piece, preferred_element_type=jnp.float32)
        + adapter_scale * gathered_back.astype(jnp.float32)
    ).astype(jnp.bfloat16)
    recent_output = jnp.dot(decode_rows, piece, preferred_element_type=jnp.float32).astype(
        jnp.bfloat16
    )
    kv_heads = half_width // HEAD_SIZE
    query_groups = queries.shape[1] // half_width
    positions = key_store_cache.shape[1]
    newest_keys = recent_output[:, :half_width].reshape(decode_count, kv_heads, HEAD_SIZE)
    newest_values = recent_output[:, half_width:].reshape(decode_count, kv_heads, HEAD_SIZE)
    query_head_rows = queries.reshape(decode_count, kv_heads, query_groups, HEAD_SIZE)
    stored_keys = key_store_cache.reshape(decode_count, positions, kv_heads, HEAD_SIZE)
    stored_values = value_store_cache.reshape(decode_count, positions, kv_heads, HEAD_SIZE)
    reverse_permute = 1.0 / math.sqrt(HEAD_SIZE)
    scores = (
        jnp.einsum(
            "bkgd,bckd->bkgc", query_head_rows, stored_keys, preferred_element_type=jnp.float32
        )
        * reverse_permute
    )
    tenant_local = (
        jnp.einsum(
            "lemx,lex->lem", query_head_rows, newest_keys, preferred_element_type=jnp.float32
        )
        * reverse_permute
    )
    live = jnp.arange(positions, dtype=jnp.int32)[None, :] < context_len[:, None]
    scores = jnp.where(live[:, None, None, :], scores, -jnp.inf)
    top = jnp.maximum(jnp.max(scores, axis=-1), tenant_local)
    cached_weight = jnp.exp(scores - top[..., None])
    own_weight = jnp.exp(tenant_local - top)
    total = jnp.sum(cached_weight, axis=-1) + own_weight
    probs = (cached_weight / total[..., None]).astype(jnp.bfloat16)
    probs_own = (own_weight / total).astype(jnp.bfloat16)
    mixed = jnp.einsum("bkgc,bckd->bkgd", probs, stored_values, preferred_element_type=jnp.float32)
    mixed = (
        mixed
        + probs_own.astype(jnp.float32)[..., None]
        * newest_values.astype(jnp.float32)[:, :, None, :]
    )
    attended = mixed.reshape(decode_count, query_groups * kv_heads * HEAD_SIZE).astype(jnp.bfloat16)
    return (projected, attended)


def solution(mesh):
    in_specs = (
        P(("replica", "tenant"), None),
        P(("replica", "tenant"), None),
        P(),
        P(("replica", "tenant"), None),
        P(("replica", "tenant"), None),
        P(("replica", "tenant"), None, None),
        P(("replica", "tenant"), None, None),
        P(("replica", "tenant")),
        P("tenant", None),
        P("tenant", None, None),
        P("tenant", None, None),
    )
    out_specs = (P(("replica", "tenant"), None), P(("replica", "tenant"), None))
    return jax.shard_map(body, mesh=mesh, in_specs=in_specs, out_specs=out_specs, check_vma=False)
```

profile of v0, /device:TPU:0, one launch (start us, length us, event | category | flops | bytes accessed | tf_op | source)
XLA Modules:
  0.0 372.1 jit_solution(15346959289181666698)
XLA Ops:
  7.2 0.7 all-gather.2.cloned.1.call-update
  7.9 0.9 fusion.46
  8.8 0.6 reduce-window.6
  9.4 0.2 slice_reduce_fusion
  9.6 0.8 select_reduce_fusion
  10.4 12.8 %scatter_custom_fusion = bf16[512,8192]{1,0:T(8,128)(2,1)} fusion(s32[256]{0:T(256)S(1)} %bitcast.94, bf16[256,8192]{1,0:T(8,128)(2,1)} %param.11, bf16[]{:T(256)} %constant.9.clone.1), kind=kCustom, calls=%fused_computation.4 | custom fusion | bytes 8389120 | tf_op jit(solution)/shard_map/scatter | solution.py:45
  23.2 282.4 %all_to_all.10 = bf16[16,2,16,8192]{3,2,1,0:T(8,128)(2,1)} all-to-all(bf16[16,2,16,8192]{3,2,1,0:T(8,128)(2,1)} %bitcast.86), channel_id=1, replica_groups=mesh['replica'=2,'tenant'=16] {'tenant'}, dimensions={0} | all-to-all | bytes 16777216 | tf_op jit(solution)/shard_map/all_to_all | solution.py:50
  305.6 7.3 %fusion.10 = bf16[16,2,16,1024]{3,2,0,1:T(8,128)(2,1)} fusion(bf16[16,2,16,8192]{3,2,1,0:T(8,128)(2,1)} %all_to_all.10, bf16[2,32,8192]{2,1,0:T(8,128)(2,1)} %param.20, bf16[2,32,1024]{2,1,0:T(8,128)(2,1)S(1)} %copy-done.7), kind=kOutput, calls=%fused_computation.14 | convolution fusion | flops 302530560 | bytes 10616832 | tf_op jit(solution)/shard_map/ntcr,tre->ntce/dot_general | solution.py:54
  312.9 2.3 copy.38
  315.3 4.6 %all-to-all-start.1 = ((bf16[16,2,16,1024]{3,2,1,0:T(8,128)(2,1)}), bf16[16,2,16,1024]{3,2,1,0:T(8,128)(2,1)}, u32[]{:S(2)}, u32[]{:S(2)}) async-start(bf16[16,2,16,1024]{3,2,1,0:T(8,128)(2,1)} %copy.38), calls=%async_computation.1 | async-start | bytes 2097152 | tf_op jit(solution)/shard_map/all_to_all | solution.py:15
  319.8 0.6 pad_clamp_fusion
  320.4 0.1 iota_compare_fusion.2
  320.5 2.1 fusion.51
  322.6 20.2 %all-to-all-done.1 = bf16[16,2,16,1024]{3,2,1,0:T(8,128)(2,1)} async-done(((bf16[16,2,16,1024]{3,2,1,0:T(8,128)(2,1)}), bf16[16,2,16,1024]{3,2,1,0:T(8,128)(2,1)}, u32[]{:S(2)}, u32[]{:S(2)}) %all-to-all-start.1) | async-done | bytes 1048608 | tf_op jit(solution)/shard_map/all_to_all | solution.py:15
  342.8 3.8 %gather_fusion = bf16[256,1024]{1,0:T(8,128)(2,1)} fusion(bf16[512,1024]{1,0:T(8,128)(2,1)} %bitcast.12, s32[1024]{0:T(1024)} %pad_clamp_fusion), kind=kCustom, calls=%fused_computation | custom fusion | bytes 1049600 | tf_op jit(solution)/shard_map/gather | solution.py:59
  346.7 8.3 %convolution_convert_fusion.1 = bf16[8,1024]{1,0:T(8,128)(2,1)S(1)} fusion(bf16[8,8192]{1,0:T(8,128)(2,1)} %param.14, bf16[8192,1024]{1,0:T(8,128)(2,1)} %all-gather.2.cloned.1.call-done), kind=kOutput, calls=%fused_computation.23 | convolution fusion | flops 134225920 | bytes 16924672 | tf_op jit(solution)/shard_map/dot_general | solution.py:64
  355.0 0.2 fusion.41
  355.2 0.2 fusion.37
  355.4 0.7 fusion.32
  356.2 0.7 copy.89
  356.8 1.5 copy-done.1
  358.3 0.3 copy-done.2
  358.6 1.3 copy-done.5
  359.9 5.4 %fusion.11 = bf16[256,1024]{1,0:T(8,128)(2,1)} fusion(bf16[256,8192]{1,0:T(8,128)(2,1)S(1)} %copy-done.5, bf16[8192,1024]{1,0:T(8,128)(2,1)S(1)} %copy-done.1, bf16[256,1024]{1,0:T(8,128)(2,1)S(1)} %copy-done.2), kind=kOutput, calls=%fused_computation.15 | convolution fusion | flops 4296015872 | bytes 22020096 | tf_op jit(solution)/shard_map/dot_general | solution.py:61
  (23 shorter events, 0.2 us)
Async XLA Ops:
  7.2 313.4 %copy-start = (bf16[8,384,512]{2,1,0:T(8,128)(2,1)S(1)}, bf16[8,384,512]{2,1,0:T(8,128)(2,1)}, u32[]{:S(2)}) copy-start(bf16[8,384,512]{2,1,0:T(8,128)(2,1)} %param.16) | copy-start | bytes 9437188
  7.2 339.5 %all-gather.2.cloned.1.call-start = ((), (), s32[]{:S(2)}) async-start(), calls=%async_computation.2 | async-start | bytes 17825792 | tf_op jit(solution)/shard_map/all_gather | solution.py:47
  23.2 282.4 %copy-start.7 = (bf16[2,32,1024]{2,1,0:T(8,128)(2,1)S(1)}, bf16[2,32,1024]{2,1,0:T(8,128)(2,1)}, u32[]{:S(2)}) copy-start(bf16[2,32,1024]{2,1,0:T(8,128)(2,1)} %param.21) | copy-start | bytes 393220
  312.9 7.5 %copy-start.4 = (s32[8]{0:T(128)S(1)}, s32[8]{0:T(128)}, u32[]{:S(2)}) copy-start(s32[8]{0:T(128)} %param.18) | copy-start | bytes 100
  315.3 27.6 %all-to-all-start.1 = ((bf16[16,2,16,1024]{3,2,1,0:T(8,128)(2,1)}), bf16[16,2,16,1024]{3,2,1,0:T(8,128)(2,1)}, u32[]{:S(2)}, u32[]{:S(2)}) async-start(bf16[16,2,16,1024]{3,2,1,0:T(8,128)(2,1)} %copy.38), calls=%async_computation.1 | async-start | bytes 2097152 | tf_op jit(solution)/shard_map/all_to_all | solution.py:15
  346.7 8.3 %copy-start.3 = (bf16[8,4096]{1,0:T(8,128)(2,1)S(1)}, bf16[8,4096]{1,0:T(8,128)(2,1)}, u32[]{:S(2)}) copy-start(bf16[8,4096]{1,0:T(8,128)(2,1)} %param.15) | copy-start | bytes 196612
  346.7 8.8 %copy-start.6 = (bf16[8,384,512]{2,1,0:T(8,128)(2,1)S(1)}, bf16[8,384,512]{2,1,0:T(8,128)(2,1)}, u32[]{:S(2)}) copy-start(bf16[8,384,512]{2,1,0:T(8,128)(2,1)} %param.17) | copy-start | bytes 9437188
  346.7 11.6 %copy-start.1 = (bf16[8192,1024]{1,0:T(8,128)(2,1)S(1)}, bf16[8192,1024]{1,0:T(8,128)(2,1)}, u32[]{:S(2)}) copy-start(bf16[8192,1024]{1,0:T(8,128)(2,1)} %all-gather.2.cloned.1.call-done) | copy-start | bytes 50331652
  354.9 3.6 copy-start.2
  354.9 4.9 %copy-start.5 = (bf16[256,8192]{1,0:T(8,128)(2,1)S(1)}, bf16[256,8192]{1,0:T(8,128)(2,1)}, u32[]{:S(2)}) copy-start(bf16[256,8192]{1,0:T(8,128)(2,1)} %param.11) | copy-start | bytes 12582916
Sparse Core Ops, SparseCore 0:
  10.2 257.7 all-gather.1
where the time goes:
time: 374 us; the launch traced here: 372 us
  blocking collectives  282 us (75%)
  matrix products  24 us (6%)
  local copies, waits for them, and re-layouts  22.9 us (6%)
  waiting for transfers between devices  20.9 us (6%)
  between operations  14.1 us (4%)
  starting transfers between devices  4.59 us (1%)
    all_to_all x1, blocking collectives, body(): lax.all_to_all(outgoing, 'tenant', split_axis=0, concat_axis=0, tiled=True)  282 us
    all_to_all x1, waiting for transfers between devices, send_back(): lax.all_to_all(answer, 'tenant', split_axis=0, concat_axis=0, tiled=True)  20.2 us
    scatter x1, local copies, waits for them, and re-layouts, body(): jnp.zeros((tenants * capacity, width), jnp.bfloat16).at[target]  12.8 us
    dot_general x1, matrix products, body(): jnp.dot(decode_rows, piece, preferred_element_type=jnp.float32)  8.25 us
  transfers between devices with their start and end apart: 2, of which 1 were waited for; matrix products, arithmetic and copies ran while one was open for 8% of the time, Pallas kernels for 0%

commit v1 on v0

v1 whole, which is shorter than its diff:
```python
import math

import jax
import jax.numpy as jnp
from jax import lax
from jax.experimental import pallas as pl
from jax.experimental.pallas import tpu as pltpu
from jax.sharding import PartitionSpec as P

HEAD_SIZE = 128
adapter_scale = 2.0
BOTH = ("replica", "tenant")


def cost(flops, bytes_accessed):
    return pl.CostEstimate(flops=flops, bytes_accessed=bytes_accessed, transcendentals=0)


def split_columns(prefill, decode, slots_row, down, up, base, table, steps, kk, flips, rep):
    rows, dec = prefill.shape[0], decode.shape[0]
    pad = slots_row.shape[0]
    ranks = down.shape[0]
    wide = steps * kk
    out_width = up.shape[1]
    fold = wide // out_width
    tall = ranks // fold
    if kk % 128:
        stacked = jnp.concatenate([prefill, decode], axis=0)

        def pick(a, m):
            cut = a.reshape(a.shape[0], -1, kk)
            return jnp.take(cut, table[m * steps : (m + 1) * steps], axis=1).reshape(a.shape[0], wide)

        folded = jnp.concatenate(jnp.split(up, fold, axis=0), axis=1)
        return (
            [jnp.concatenate([pick(stacked, m), slots_row], axis=0) for m in range(4)],
            [jnp.concatenate([pick(down, m), folded], axis=0) for m in flips],
            lax.dynamic_slice_in_dim(base, rep * kk, kk, axis=0),
        )
    count = len(flips)
    per = out_width // kk

    def kernel(tab, *refs):
        pre, dcd, dwn = refs[0:4], refs[4:8], refs[8 : 8 + count]
        slot, upm, bas = refs[8 + count : 11 + count]
        outs = refs[11 + count :]
        for m in range(4):
            outs[m][0:rows, :] = pre[m][...]
            outs[m][rows : rows + dec + pad, :] = jnp.concatenate([dcd[m][...], slot[...]], axis=0)
        for i in range(count):
            outs[4 + i][0:ranks, :] = dwn[i][...]
            outs[4 + i][ranks : ranks + tall, :] = upm[...]
        outs[4 + count][...] = bas[...]

    def at(m):
        return lambda j, tab: (0, tab[m * steps + j])

    here = lambda j, tab: (0, j)
    base_rows = kk // steps
    outs = pl.pallas_call(
        kernel,
        grid_spec=pltpu.PrefetchScalarGridSpec(
            num_scalar_prefetch=1,
            grid=(steps,),
            in_specs=[pl.BlockSpec((rows, kk), at(m)) for m in range(4)]
            + [pl.BlockSpec((dec, kk), at(m)) for m in range(4)]
            + [pl.BlockSpec((ranks, kk), at(m)) for m in flips]
            + [
                pl.BlockSpec((pad, kk), here),
                pl.BlockSpec((tall, kk), lambda j, tab: (j // per, j % per)),
                pl.BlockSpec((base_rows, out_width), lambda j, tab: (tab[4 * steps] * steps + j, 0)),
            ],
            out_specs=[pl.BlockSpec((rows + dec + pad, kk), here)] * 4
            + [pl.BlockSpec((ranks + tall, kk), here)] * count
            + [pl.BlockSpec((base_rows, out_width), lambda j, tab: (j, 0))],
        ),
        out_shape=[jax.ShapeDtypeStruct((rows + dec + pad, wide), jnp.bfloat16)] * 4
        + [jax.ShapeDtypeStruct((ranks + tall, wide), jnp.bfloat16)] * count
        + [jax.ShapeDtypeStruct((kk, out_width), jnp.bfloat16)],
        compiler_params=pltpu.CompilerParams(vmem_limit_bytes=32 * 2**20),
        cost_estimate=cost(0, 10 * 2**20),
        name="split_columns",
    )(table, *([prefill] * 4), *([decode] * 4), *([down] * count), slots_row, up, base)
    return list(outs[:4]), list(outs[4 : 4 + count]), outs[4 + count]


def base_products(blocks, parts, spots, kinds):
    kk, out_width = parts[0].shape
    tall = blocks[0].shape[0]
    n = len(parts)
    if kk % 128:
        quarter = jnp.zeros((n * kk, out_width), jnp.bfloat16)
        for i in range(n):
            quarter = lax.dynamic_update_slice_in_dim(quarter, parts[i], spots[i] * kk, axis=0)
        return [
            jnp.dot(b, quarter, preferred_element_type=jnp.float32).astype(kind)
            for b, kind in zip(blocks, kinds)
        ]
    count = len(blocks)
    cut = 256

    def kernel(spot, *refs):
        rows, weights, outs = refs[:count], refs[count : count + n], refs[count + n :]
        for m in range(count):
            total = None
            for i in range(n):
                columns = pl.ds(pl.multiple_of(spot[i] * kk, kk), kk)
                term = jnp.dot(
                    rows[m][:, columns], weights[i][...], preferred_element_type=jnp.float32
                )
                total = term if total is None else total + term
            outs[m][...] = total.astype(kinds[m])

    return pl.pallas_call(
        kernel,
        grid_spec=pltpu.PrefetchScalarGridSpec(
            num_scalar_prefetch=1,
            grid=(out_width // cut,),
            in_specs=[pl.BlockSpec(blocks[0].shape, lambda j, s: (0, 0))] * count
            + [pl.BlockSpec((kk, cut), lambda j, s: (0, j))] * n,
            out_specs=[pl.BlockSpec((tall, cut), lambda j, s: (0, j))] * count,
        ),
        out_shape=[jax.ShapeDtypeStruct((tall, out_width), kind) for kind in kinds],
        compiler_params=pltpu.CompilerParams(vmem_limit_bytes=40 * 2**20),
        cost_estimate=cost(2 * count * tall * n * kk * out_width, (count * tall + out_width) * 2 * n * kk),
        name="base_products",
    )(spots, *blocks, *parts)


def lowered_products(blocks, pieces, columns, rows, first, ranks, earlier):
    wide = blocks[0].shape[1]
    total_ranks = len(pieces) * ranks
    count = len(blocks)
    if wide % 512 or columns.shape[1] * len(blocks) > 8192:
        sums = []
        down = jnp.concatenate([p[:ranks] for p in pieces], axis=0)
        for m, b in enumerate(blocks):
            product = lax.dot_general(
                b[:rows], down, (((1,), (1,)), ((), ())), preferred_element_type=jnp.float32
            )
            slot = b[first, :rows].astype(jnp.float32)
            kept = jnp.where(slot[:, None] == columns[:1], product, 0.0)
            kept = sum(kept[:, i : i + 128] for i in range(0, total_ranks, 128))
            sums.append(kept if earlier is None else earlier[m] + kept)
        return sums
    chunk = 512
    chunks = wide // chunk
    n = len(pieces)
    base_row = first // 16 * 16

    def kernel(*refs):
        xs, ds = refs[:count], refs[count : count + n]
        col = refs[count + n]
        before = refs[count + n + 1 : count + n + 1 + (0 if earlier is None else count)]
        outs = refs[count + n + 1 + len(before) : -2]
        acc, slot_of = refs[-2], refs[-1]
        j = pl.program_id(0)

        @pl.when(j == 0)
        def _():
            acc[...] = jnp.zeros_like(acc)
            for m in range(count):
                slot_of[m] = xs[m][base_row : base_row + 16, :rows].astype(jnp.float32)

        down = jnp.concatenate([d[...] for d in ds], axis=0)
        for m in range(count):
            acc[m] += lax.dot_general(
                xs[m][:rows], down, (((1,), (1,)), ((), ())), preferred_element_type=jnp.float32
            )

        @pl.when(j == chunks - 1)
        def _():
            for m in range(count):
                slot = jnp.transpose(slot_of[m])[:, first - base_row : first - base_row + 1]
                kept = None
                for i in range(0, total_ranks, 128):
                    part = jnp.where(slot == col[0:1, i : i + 128], acc[m, :, i : i + 128], 0.0)
                    kept = part if kept is None else kept + part
                outs[m][...] = kept if earlier is None else kept + before[m][...]

    whole = lambda j: (0, 0)
    extra = [] if earlier is None else list(earlier)
    return pl.pallas_call(
        kernel,
        grid=(chunks,),
        in_specs=[pl.BlockSpec((blocks[0].shape[0], chunk), lambda j: (0, j))] * count
        + [pl.BlockSpec((ranks, chunk), lambda j: (0, j))] * n
        + [pl.BlockSpec(columns.shape, whole)]
        + [pl.BlockSpec((rows, 128), whole)] * len(extra),
        out_specs=[pl.BlockSpec((rows, 128), whole)] * count,
        out_shape=[jax.ShapeDtypeStruct((rows, 128), jnp.float32)] * count,
        scratch_shapes=[
            pltpu.VMEM((count, rows, total_ranks), jnp.float32),
            pltpu.VMEM((count, 16, rows), jnp.float32),
        ],
        compiler_params=pltpu.CompilerParams(vmem_limit_bytes=40 * 2**20),
        cost_estimate=cost(2 * count * rows * wide * total_ranks, (count * rows + total_ranks) * 2 * wide),
        name="lowered_products",
    )(*blocks, *pieces, columns, *extra)


def finish(parts, block, pieces, columns, base, rows, first, ranks, rank):
    packed_rows = parts[0].shape[0]
    folds = rows // packed_rows
    tall = pieces[0].shape[0] - ranks
    out_width = base.shape[1]
    fold = ranks // tall
    n = len(pieces)
    base_row = first // 16 * 16
    if n > 16:
        lowered = sum(parts[1:], parts[0]).astype(jnp.bfloat16)
        lowered = jnp.concatenate(
            [lowered[:, b * rank : (b + 1) * rank] for b in range(folds)], axis=0
        )
        up = jnp.concatenate(
            [p[ranks:, i * out_width : (i + 1) * out_width] for p in pieces for i in range(fold)], axis=0
        )
        slot = block[first, :rows].astype(jnp.float32)
        spread = jnp.where(
            slot[:, None] == columns[:1], jnp.tile(lowered, (1, n * ranks // rank)), jnp.bfloat16(0)
        )
        delta = jnp.dot(spread, up, preferred_element_type=jnp.float32).astype(jnp.bfloat16)
        return (base[:rows] + adapter_scale * delta.astype(jnp.float32)).astype(jnp.bfloat16)

    def kernel(*refs):
        packs = refs[:4]
        blk, col, bas = refs[4:7]
        ups = refs[7 : 7 + n]
        out = refs[7 + n]
        slot = jnp.transpose(blk[...].astype(jnp.float32))[:, first - base_row : first - base_row + 1]
        packed = (packs[0][...] + packs[1][...]) + (packs[2][...] + packs[3][...])
        lane = lax.broadcasted_iota(jnp.int32, packed.shape, 1) // rank
        spread = []
        for b in range(folds):
            one = jnp.where(lane == b, packed, 0.0)
            one = one + pltpu.roll(one, rank, 1)
            one = one + pltpu.roll(one, 2 * rank, 1)
            spread.append(one)
        lowered = jnp.concatenate(spread, axis=0)
        wide = []
        for i in range(0, n * ranks, 128):
            wide.append(jnp.where(slot == col[0:1, i : i + 128], lowered, 0.0).astype(jnp.bfloat16))
        wide = jnp.concatenate(wide, axis=1)
        up = jnp.concatenate(
            [p[:, i * out_width : (i + 1) * out_width] for p in ups for i in range(fold)], axis=0
        )
        for i in range(0, out_width, 256):
            delta = jnp.dot(wide, up[:, i : i + 256], preferred_element_type=jnp.float32)
            delta = delta.astype(jnp.bfloat16).astype(jnp.float32)
            out[:, i : i + 256] = (bas[0:rows, i : i + 256] + adapter_scale * delta).astype(jnp.bfloat16)

    one = lambda j: (0, 0)
    return pl.pallas_call(
        kernel,
        grid=(1,),
        in_specs=[pl.BlockSpec(parts[0].shape, one)] * 4
        + [
            pl.BlockSpec((16, rows), lambda j: (base_row // 16, 0)),
            pl.BlockSpec(columns.shape, one),
            pl.BlockSpec(base.shape, one),
        ]
        + [pl.BlockSpec((tall, pieces[0].shape[1]), lambda j: (ranks // tall, 0))] * n,
        out_specs=pl.BlockSpec((rows, out_width), one),
        out_shape=jax.ShapeDtypeStruct((rows, out_width), jnp.bfloat16),
        compiler_params=pltpu.CompilerParams(vmem_limit_bytes=40 * 2**20),
        cost_estimate=cost(2 * rows * n * ranks * out_width, 4 * 2**20),
        name="finish",
    )(*parts, block, columns, base, *pieces)


def body(
    prefill_rows,
    tenant_ids,
    owner_slot,
    decode_rows,
    queries,
    key_store_cache,
    value_store_cache,
    context_len,
    base_weight,
    adapter_down,
    adapter_up,
):
    reps, peers = lax.axis_size("replica"), lax.axis_size("tenant")
    planes = reps * peers // 8
    sides = peers // (2 * planes)
    local_slots, rank, width = adapter_down.shape
    slots_all = local_slots * peers
    rows, dec = prefill_rows.shape[0], decode_rows.shape[0]
    out_width = base_weight.shape[1]
    half_width = out_width // 2
    kk = base_weight.shape[0] // reps
    steps = 2 * planes
    quarter = steps * kk
    pad = 16 - dec % 16
    r, t = lax.axis_index("replica"), lax.axis_index("tenant")
    z, y, c = t // (2 * sides), (t // 2) % sides, t % 2
    q = y * reps + r

    order = list(range(0, planes, 2)) + list(range(1, planes, 2))[::-1]
    after = {order[i]: order[(i + 1) % planes] for i in range(planes)}
    everyone = [(a, b) for a in range(reps) for b in range(peers)]

    def flip(m):
        pairs = []
        for a, b in everyone:
            other = (((b // 2) % sides) * reps + a) ^ m
            to = (b // (2 * sides) * sides + other // reps) * 2 + b % 2
            pairs.append((a * peers + b, (other % reps) * peers + to))
        return pairs

    flips = {m: flip(m) for m in (1, 2, 3)}
    ring = [
        (a * peers + b, a * peers + after[b // (2 * sides)] * 2 * sides + b % (2 * sides))
        for a, b in everyone
    ]
    cores = [(a * peers + b, a * peers + (b ^ 1)) for a, b in everyone]

    def send(value, pairs):
        return lax.ppermute(value, BOTH, pairs)

    place = jnp.where(z % 2 == 0, z // 2, planes - 1 - z // 2)

    def plane_of(k):
        spot = (place - k + planes) % planes
        return jnp.where(spot < planes // 2, 2 * spot, 2 * (planes - 1 - spot) + 1)

    j = jnp.arange(steps, dtype=jnp.int32)[None, :]
    other = q ^ jnp.arange(4, dtype=jnp.int32)[:, None]
    shard = (j // 2 * sides + other // reps) * 2 + j % 2
    table = jnp.concatenate([(shard * reps + other % reps).reshape(-1), r[None]])
    spots = plane_of(j[0] // 2) * 2 + (c ^ (j[0] % 2))

    tenant_hot = tenant_ids == jnp.arange(slots_all, dtype=jnp.int32)[None, :]
    slot_index = jnp.sum(jnp.where(tenant_hot, owner_slot[None, :], 0), axis=1)
    slots_row = jnp.broadcast_to(
        jnp.pad(slot_index.astype(jnp.bfloat16), (0, quarter - rows))[None, :], (pad, quarter)
    )
    ranks = local_slots * rank
    y_flips = [0, reps] if sides == 2 else [0]
    messages, adapters, held = split_columns(
        prefill_rows,
        decode_rows,
        slots_row,
        adapter_down.reshape(ranks, width),
        adapter_up.reshape(ranks, out_width),
        base_weight,
        table,
        steps,
        kk,
        y_flips,
        r,
    )
    blocks = [messages[0]] + [send(messages[m], flips[m]) for m in (1, 2, 3)]

    base_parts = []
    for k in range(planes):
        base_parts += [held, send(held, cores)]
        if k + 1 < planes:
            held = send(held, ring)

    chains = [adapters[0]] + [send(a, flips[reps]) for a in adapters[1:]]
    pieces = []
    for k in range(planes):
        pieces.append(chains + [send(a, cores) for a in chains])
        if k + 1 < planes:
            chains = [send(a, ring) for a in chains]

    sent = base_products(blocks[1:], base_parts, spots, [jnp.bfloat16] * 3)
    sent = [send(sent[m - 1], flips[m]) for m in (1, 2, 3)]
    (base,) = base_products(blocks[:1], base_parts, spots, [jnp.float32])
    base = base + sum(s.astype(jnp.float32) for s in sent)
    recent_output = base[rows : rows + dec].astype(jnp.bfloat16)

    group = jnp.arange(slots_all, dtype=jnp.int32)
    inner = group % local_slots
    side = (group // local_slots) % sides
    core = (group // (local_slots * sides)) % 2
    step = group // (local_slots * sides * 2)
    column_slot = ((plane_of(step) * sides + (y ^ side)) * 2 + (c ^ core)) * local_slots + inner
    columns = jnp.broadcast_to(
        jnp.repeat(column_slot, rank).astype(jnp.float32)[None, :], (8, slots_all * rank)
    )
    front = sum(pieces[:-1], [])
    cut = len(front) * ranks
    first = rows + dec
    sums = None
    if front:
        sums = lowered_products(blocks, front, columns[:, :cut], rows, first, ranks, None)
    sums = lowered_products(blocks, pieces[-1], columns[:, cut:], rows, first, ranks, sums)
    folds = 128 // rank
    packed = []
    for s in sums:
        s = sum(s[:, i * rank : (i + 1) * rank] for i in range(folds))
        packed.append(jnp.concatenate(jnp.split(s, folds, axis=0), axis=1))
    packed = [packed[0]] + [send(packed[m], flips[m]) for m in (1, 2, 3)]
    projected = finish(
        packed, blocks[0], sum(pieces, []), columns, base, rows, first, ranks, rank
    )

    kv_heads = half_width // HEAD_SIZE
    query_groups = queries.shape[1] // half_width
    positions = key_store_cache.shape[1]
    newest_keys = recent_output[:, :half_width].reshape(dec, kv_heads, HEAD_SIZE)
    newest_values = recent_output[:, half_width:].reshape(dec, kv_heads, HEAD_SIZE)
    query_head_rows = queries.reshape(dec, kv_heads, query_groups, HEAD_SIZE)
    stored_keys = key_store_cache.reshape(dec, positions, kv_heads, HEAD_SIZE)
    stored_values = value_store_cache.reshape(dec, positions, kv_heads, HEAD_SIZE)
    scale = 1.0 / math.sqrt(HEAD_SIZE)
    scores = (
        jnp.einsum(
            "bkgd,bckd->bkgc", query_head_rows, stored_keys, preferred_element_type=jnp.float32
        )
        * scale
    )
    own_score = (
        jnp.einsum(
            "bkgd,bkd->bkg", query_head_rows, newest_keys, preferred_element_type=jnp.float32
        )
        * scale
    )
    live = jnp.arange(positions, dtype=jnp.int32)[None, :] < context_len[:, None]
    scores = jnp.where(live[:, None, None, :], scores, -jnp.inf)
    top = jnp.maximum(jnp.max(scores, axis=-1), own_score)
    cached_weight = jnp.exp(scores - top[..., None])
    own_weight = jnp.exp(own_score - top)
    total = jnp.sum(cached_weight, axis=-1) + own_weight
    probs = (cached_weight / total[..., None]).astype(jnp.bfloat16)
    probs_own = (own_weight / total).astype(jnp.bfloat16)
    mixed = jnp.einsum("bkgc,bckd->bkgd", probs, stored_values, preferred_element_type=jnp.float32)
    mixed = (
        mixed
        + probs_own.astype(jnp.float32)[..., None]
        * newest_values.astype(jnp.float32)[:, :, None, :]
    )
    attended = mixed.reshape(dec, query_groups * kv_heads * HEAD_SIZE).astype(jnp.bfloat16)
    return (projected, attended)


def solution(mesh):
    in_specs = (
        P(BOTH, None),
        P(BOTH, None),
        P(),
        P(BOTH, None),
        P(BOTH, None),
        P(BOTH, None, None),
        P(BOTH, None, None),
        P(BOTH),
        P("tenant", None),
        P("tenant", None, None),
        P("tenant", None, None),
    )
    out_specs = (P(BOTH, None), P(BOTH, None))
    return jax.shard_map(body, mesh=mesh, in_specs=in_specs, out_specs=out_specs, check_vma=False)
```

time: 374 us -> 171 us (0.46)
  blocking collectives: 282 us -> 0 us
  waiting for transfers between devices: 20.9 us -> 85.8 us
  Pallas kernels: 0 us -> 30 us
  starting transfers between devices: 4.59 us -> 32.1 us
  matrix products: 24 us -> 3.13 us
  between operations: 14.1 us -> 1.12 us
  local copies, waits for them, and re-layouts: 22.9 us -> 14.6 us
    all_to_all x1 -> x0, blocking collectives: 282 us -> none  [body(): lax.all_to_all(outgoing, 'tenant', split_axis=0, concat_axis=0, tiled=True)]
    ppermute x0 -> x31, waiting for transfers between devices: none -> 85.8 us  [send(): return lax.ppermute(value, BOTH, pairs)]
    ppermute x0 -> x31, starting transfers between devices: none -> 32.1 us  [send(): return lax.ppermute(value, BOTH, pairs)]
    pallas_call x0 -> x6, Pallas kernels: none -> 30 us  [the longest x2 11.6 us: base_products(): pl.pallas_call(kernel, grid_spec=pltpu.PrefetchScalarGridSpec(num_scalar_...]
    dot_general x4 -> x1, matrix products: 21.1 us -> 0.16 us  [body(): jnp.einsum('bkgd,bkd->bkg', query_head_rows, newest_keys, preferred_eleme...]
    all_to_all x1 -> x0, waiting for transfers between devices: 20.2 us -> none  [send_back(): lax.all_to_all(answer, 'tenant', split_axis=0, concat_axis=0, tiled=True)]
    scatter x1 -> x0, local copies, waits for them, and re-layouts: 12.8 us -> none  [body(): jnp.zeros((tenants * capacity, width), jnp.bfloat16).at[target]]
    unnamed x17 -> x57, local copies, waits for them, and re-layouts: 3.75 us -> 13 us
  transfers between devices with their start and end apart: 2 -> 31, of which waited for: 1 -> 11; matrix products, arithmetic and copies ran while one was open for 8% -> 4% of each run, Pallas kernels for 0% -> 13%
where the time goes in v1:
time: 171 us; the launch traced here: 170 us
  waiting for transfers between devices  85.8 us (50%)
  starting transfers between devices  32.1 us (19%)
  Pallas kernels  30 us (18%)
  local copies, waits for them, and re-layouts  14.6 us (9%)
  other arithmetic  3.46 us (2%)
  matrix products  3.13 us (2%)
    ppermute x31, waiting for transfers between devices, send(): return lax.ppermute(value, BOTH, pairs)  85.8 us
    ppermute x31, starting transfers between devices, send(): return lax.ppermute(value, BOTH, pairs)  32.1 us
    unnamed x57, local copies, waits for them, and re-layouts  13 us
    pallas_call x2, Pallas kernels, base_products(): pl.pallas_call(kernel, grid_spec=pltpu.PrefetchScalarGridSpec(num_scalar_...  11.6 us
    pallas_call x2, Pallas kernels, lowered_products(): pl.pallas_call(kernel, grid=(chunks,), in_specs=[pl.BlockSpec((blocks[0]....  10.7 us
    pallas_call x1, Pallas kernels, split_columns(): pl.pallas_call(kernel, grid_spec=pltpu.PrefetchScalarGridSpec(num_scalar_...  4.92 us
  transfers between devices with their start and end apart: 31, of which 11 were waited for; matrix products, arithmetic and copies ran while one was open for 4% of the time, Pallas kernels for 13%

profile of v1, /device:TPU:0, one launch (start us, length us, event | category | flops | bytes accessed | tf_op | source)
XLA Modules:
  0.0 170.2 jit_solution(15243187121339866830)
XLA Ops:
  1.9 2.2 %copy-done.1 = bf16[256,8192]{1,0:T(8,128)(2,1)S(1)} copy-done((bf16[256,8192]{1,0:T(8,128)(2,1)S(1)}, bf16[256,8192]{1,0:T(8,128)(2,1)}, u32[]{:S(2)}) %copy-start.1) | copy-done | bytes 4194328
  8.4 4.9 %split_columns.1 = (bf16[272,2048]{1,0:T(8,128)(2,1)S(1)}, bf16[272,2048]{1,0:T(8,128)(2,1)}, bf16[272,2048]{1,0:T(8,128)(2,1)}, bf16[272,2048]{1,0:T(8,128)(2,1...) custom-call(s32[33]{0:T(128)S(1)} %pad_add_fusion.tab, ...), custom_call_target="tpu_custom_call" | custom-call | bytes 10485760 | tf_op jit(solution)/shard_map/split_columns/pallas_call | solution.py:60
  14.3 3.0 %collective-permute-start.6 = (bf16[96,2048]{1,0:T(8,128)(2,1)S(1)}, bf16[96,2048]{1,0:T(8,128)(2,1)S(1)}, u32[]{:S(2)}, u32[]{:S(2)}) collective-permute-start(bf16[96,2048]{1,0:T(8,128)(2,1)S(1)} %get-tuple-element.25), channel_id=1, source_target_pairs={{0,2},{1,3},{2,0},{3,1},{4,6},{5,7},{6,4},{7,5},{8,10},{9,11},{10,... | collective-permute-start | bytes 1179656 | tf_op jit(solution)/shard_map/ppermute | solution.py:320
  17.2 2.6 %collective-permute-start.22 = (bf16[256,1024]{1,0:T(8,128)(2,1)S(1)}, bf16[256,1024]{1,0:T(8,128)(2,1)}, u32[]{:S(2)}, u32[]{:S(2)}) collective-permute-start(bf16[256,1024]{1,0:T(8,128)(2,1)S(1)} %get-tuple-element.34.refs_1_.refs_3_), channel_id=1, source_target_pairs={{0,8},{1,9},{2,10},{3,11},{4,0},{5,1},{6,2},{7,3},{8,12},{9,13},{1... | collective-permute-start | bytes 1572872 | tf_op jit(solution)/shard_map/ppermute | solution.py:320
  19.8 1.6 collective-permute-start.3
  21.4 4.9 %collective-permute-done.6.refs_5_.refs_8_ = bf16[96,2048]{1,0:T(8,128)(2,1)S(1)} collective-permute-done((bf16[96,2048]{1,0:T(8,128)(2,1)S(1)}, bf16[96,2048]{1,0:T(8,128)(2,1)S(1)}, u32[]{:S(2)}, u32[]{:S(2)}) %collective-permute-start.6) | collective-permute-done | bytes 393248 | tf_op jit(solution)/shard_map/ppermute | solution.py:320
  26.4 2.8 %collective-permute-start.7 = (bf16[96,2048]{1,0:T(8,128)(2,1)S(1)}, bf16[96,2048]{1,0:T(8,128)(2,1)}, u32[]{:S(2)}, u32[]{:S(2)}) collective-permute-start(bf16[96,2048]{1,0:T(8,128)(2,1)S(1)} %collective-permute-done.6.refs_5_.refs_8_), channel_id=1, source_target_pairs={{0,8},{1,9},{2,10},{3,11},{4,0},{5,1},{6,2},{7,3},{8,12},{9,13},{1... | collective-permute-start | bytes 1179656 | tf_op jit(solution)/shard_map/ppermute | solution.py:320
  29.2 11.5 %collective-permute-done.3.refs_8_.refs_11_ = bf16[96,2048]{1,0:T(8,128)(2,1)S(1)} collective-permute-done((bf16[96,2048]{1,0:T(8,128)(2,1)S(1)}, bf16[96,2048]{1,0:T(8,128)(2,1)S(1)}, u32[]{:S(2)}, u32[]{:S(2)}) %collective-permute-start.3) | collective-permute-done | bytes 393248 | tf_op jit(solution)/shard_map/ppermute | solution.py:320
  40.6 3.4 %collective-permute-start.4 = (bf16[96,2048]{1,0:T(8,128)(2,1)S(1)}, bf16[96,2048]{1,0:T(8,128)(2,1)S(1)}, u32[]{:S(2)}, u32[]{:S(2)}) collective-permute-start(bf16[96,2048]{1,0:T(8,128)(2,1)S(1)} %collective-permute-done.3.refs_8_.refs_11_), channel_id=1, source_target_pairs={{0,8},{1,9},{2,10},{3,11},{4,0},{5,1},{6,2},{7,3},{8,12},{9,13},{1... | collective-permute-start | bytes 1179656 | tf_op jit(solution)/shard_map/ppermute | solution.py:320
  49.8 6.2 %collective-permute-done.4.refs_12_.refs_15_ = bf16[96,2048]{1,0:T(8,128)(2,1)S(1)} collective-permute-done((bf16[96,2048]{1,0:T(8,128)(2,1)S(1)}, bf16[96,2048]{1,0:T(8,128)(2,1)S(1)}, u32[]{:S(2)}, u32[]{:S(2)}) %collective-permute-start.4) | collective-permute-done | bytes 393248 | tf_op jit(solution)/shard_map/ppermute | solution.py:320
  57.6 3.4 %collective-permute-start.24 = (bf16[256,1024]{1,0:T(8,128)(2,1)}, bf16[256,1024]{1,0:T(8,128)(2,1)}, u32[]{:S(2)}, u32[]{:S(2)}) collective-permute-start(bf16[256,1024]{1,0:T(8,128)(2,1)} %collective-permute-done.22.refs_3_.refs_5_), channel_id=1, source_target_pairs={{0,8},{1,9},{2,10},{3,11},{4,0},{5,1},{6,2},{7,3},{8,12},{9,13},{1... | collective-permute-start | bytes 1572872 | tf_op jit(solution)/shard_map/ppermute | solution.py:320
  63.1 10.4 %collective-permute-done.24.refs_5_.refs_7_ = bf16[256,1024]{1,0:T(8,128)(2,1)} collective-permute-done((bf16[256,1024]{1,0:T(8,128)(2,1)}, bf16[256,1024]{1,0:T(8,128)(2,1)}, u32[]{:S(2)}, u32[]{:S(2)}) %collective-permute-start.24) | collective-permute-done | bytes 524320 | tf_op jit(solution)/shard_map/ppermute | solution.py:320
  75.5 18.0 %collective-permute-done.1.refs_2_.refs_1_ = bf16[272,2048]{1,0:T(8,128)(2,1)} collective-permute-done((bf16[272,2048]{1,0:T(8,128)(2,1)}, bf16[272,2048]{1,0:T(8,128)(2,1)}, u32[]{:S(2)}, u32[]{:S(2)}) %collective-permute-start.1) | collective-permute-done | bytes 1114144 | tf_op jit(solution)/shard_map/ppermute | solution.py:320
  95.6 2.3 %fusion.52 = (f32[8,4,8]{2,1,0:T(4,128)S(1)}, f32[8,4,8,384]{3,2,1,0:T(8,128)S(1)}) fusion(bf16[8,4,8,128]{3,0,2,1:T(8,128)(2,1)} %bitcast.55, pred[8,384]{1,0:T(8,128)(4,1)} %iota_compare_fusion.1, bf16[8,384,512]{2,1,0:T(8,128)(2,1)S(1)} %copy-done), kind=kOutput, calls=%fused_computation.102 | convolution fusion | flops 25460480 | bytes 3608576 | tf_op jit(solution)/shard_map/bkgd,bckd->bkgc/dot_general | solution.py:411
  98.2 7.3 %collective-permute-done.5.refs_4_.refs_19_ = bf16[96,2048]{1,0:T(8,128)(2,1)S(1)} collective-permute-done((bf16[96,2048]{1,0:T(8,128)(2,1)}, bf16[96,2048]{1,0:T(8,128)(2,1)S(1)}, u32[]{:S(2)}, u32[]{:S(2)}) %collective-permute-start.5) | collective-permute-done | bytes 393248 | tf_op jit(solution)/shard_map/ppermute | solution.py:320
  105.5 8.4 %collective-permute-done.9.refs_5_.refs_20_ = bf16[96,2048]{1,0:T(8,128)(2,1)S(1)} collective-permute-done((bf16[96,2048]{1,0:T(8,128)(2,1)}, bf16[96,2048]{1,0:T(8,128)(2,1)S(1)}, u32[]{:S(2)}, u32[]{:S(2)}) %collective-permute-start.9) | collective-permute-done | bytes 393248 | tf_op jit(solution)/shard_map/ppermute | solution.py:320
  115.7 6.3 %lowered_products.2 = (f32[256,128]{1,0:T(8,128)S(1)}, f32[256,128]{1,0:T(8,128)S(1)}, f32[256,128]{1,0:T(8,128)S(1)}, f32[256,128]{1,0:T(8,128)S(1)}) custom-call(bf16[272,2048]{1,0:T(8,128)(2,1)S(1)} %copy-done.3, bf16[272,2048]{1,0:T(8,128)(2,1)} %collective-permute-done.refs_1_.refs_0_, bf16[272,2048]{1,0:T(8,128)(2,1)} %collective-permute-done.1.refs_2_.refs_1_, ...), custom_call_target="tpu_custom_call" | custom-call | flops 3221225472 | bytes 7340032 | tf_op jit(solution)/shard_map/lowered_products/pallas_call | solution.py:183
  122.6 4.4 %lowered_products.3 = (f32[256,128]{1,0:T(8,128)S(1)}, f32[256,128]{1,0:T(8,128)S(1)}, f32[256,128]{1,0:T(8,128)S(1)}, f32[256,128]{1,0:T(8,128)S(1)}) custom-call(bf16[272,2048]{1,0:T(8,128)(2,1)S(1)} %copy-done.3, bf16[272,2048]{1,0:T(8,128)(2,1)} %collective-permute-done.refs_1_.refs_0_, bf16[272,2048]{1,0:T(8,128)(2,1)} %collective-permute-done.1.refs_2_.refs_1_, ...), custom_call_target="tpu_custom_call" | custom-call | flops 1073741824 | bytes 5242880 | tf_op jit(solution)/shard_map/lowered_products/pallas_call | solution.py:183
  130.1 7.4 %base_products.3 = (bf16[272,1024]{1,0:T(8,128)(2,1)S(1)}, bf16[272,1024]{1,0:T(8,128)(2,1)S(1)}, bf16[272,1024]{1,0:T(8,128)(2,1)S(1)}) custom-call(s32[8]{0:T(128)S(1)} %fusion.42.spot, bf16[272,2048]{1,0:T(8,128)(2,1)} %collective-permute-done.refs_1_.refs_0_, bf16[272,2048]{1,0:T(8,128)(2,1)} %collective-permute-done.1.refs_2_.refs_1_, ...), custom_call_target="tpu_custom_call" | custom-call | flops 3422552064 | bytes 7536640 | tf_op jit(solution)/shard_map/base_products/pallas_call | solution.py:114
  137.5 1.6 collective-permute-start.28
  141.2 4.2 %base_products.2 = f32[272,1024]{1,0:T(8,128)S(1)} custom-call(s32[8]{0:T(128)S(1)} %fusion.42.spot, bf16[272,2048]{1,0:T(8,128)(2,1)S(1)} %copy-done.3, bf16[256,1024]{1,0:T(8,128)(2,1)S(1)} %copy-done.8, bf16[256,1024]{1,0:T(8,128)(2,1)S(1)} %collective-permute-done.21.refs_2_.refs_4_, bf16[256,1024]{1,0:T(8,128)(2,1)} %collective-permute-done.22.refs_3_.refs_5_, ...), custom_call_target="tpu_custom_call" | custom-call | flops 1140850688 | bytes 5308416 | tf_op jit(solution)/shard_map/base_products/pallas_call | solution.py:114
  145.5 7.6 %collective-permute-done.28 = bf16[272,1024]{1,0:T(8,128)(2,1)S(1)} collective-permute-done((bf16[272,1024]{1,0:T(8,128)(2,1)S(1)}, bf16[272,1024]{1,0:T(8,128)(2,1)S(1)}, u32[]{:S(2)}, u32[]{:S(2)}) %collective-permute-start.28) | collective-permute-done | bytes 557088 | tf_op jit(solution)/shard_map/ppermute | solution.py:320
  154.6 9.8 %collective-permute-done.29 = bf16[272,1024]{1,0:T(8,128)(2,1)S(1)} collective-permute-done((bf16[272,1024]{1,0:T(8,128)(2,1)S(1)}, bf16[272,1024]{1,0:T(8,128)(2,1)S(1)}, u32[]{:S(2)}, u32[]{:S(2)}) %collective-permute-start.29) | collective-permute-done | bytes 557088 | tf_op jit(solution)/shard_map/ppermute | solution.py:320
  167.4 2.8 %finish.1 = bf16[256,1024]{1,0:T(8,128)(2,1)} custom-call(f32[64,128]{1,0:T(8,128)S(1)} %pad_maximum_fusion.refs_0_, f32[64,128]{1,0:T(8,128)S(1)} %collective-permute-done.18.refs_1_, f32[64,128]{1,0:T(8,128)S(1)} %collective-permute-done.19.refs_2_, f32[64,128]{1,0:T(8,128)S(1)} %collective-permute-done.20.refs_3_, bf16[272,2048]{1,0:T(8,128)(2,1)S(1)} %copy-done.3, ...), custom_call_target="tpu_custom_call" | custom-call | flops 536870912 | bytes 4194304 | tf_op jit(solution)/shard_map/finish/pallas_call | solution.py:253
  (143 shorter events, 32.2 us)
Async XLA Ops:
  17.2 29.8 %collective-permute-start.22 = (bf16[256,1024]{1,0:T(8,128)(2,1)S(1)}, bf16[256,1024]{1,0:T(8,128)(2,1)}, u32[]{:S(2)}, u32[]{:S(2)}) collective-permute-start(bf16[256,1024]{1,0:T(8,128)(2,1)S(1)} %get-tuple-element.34.refs_1_.refs_3_), channel_id=1, source_target_pairs={{0,8},{1,9},{2,10},{3,11},{4,0},{5,1},{6,2},{7,3},{8,12},{9,13},{1... | collective-permute-start | bytes 1572872 | tf_op jit(solution)/shard_map/ppermute | solution.py:320
  19.8 20.8 %collective-permute-start.3 = (bf16[96,2048]{1,0:T(8,128)(2,1)S(1)}, bf16[96,2048]{1,0:T(8,128)(2,1)S(1)}, u32[]{:S(2)}, u32[]{:S(2)}) collective-permute-start(bf16[96,2048]{1,0:T(8,128)(2,1)S(1)} %get-tuple-element.24.refs_4_.refs_7_), channel_id=1, source_target_pairs={{0,8},{1,9},{2,10},{3,11},{4,0},{5,1},{6,2},{7,3},{8,12},{9,13},{1... | collective-permute-start | bytes 1179656 | tf_op jit(solution)/shard_map/ppermute | solution.py:320
  21.4 24.1 %collective-permute-start.12 = (bf16[96,2048]{1,0:T(8,128)(2,1)S(1)}, bf16[96,2048]{1,0:T(8,128)(2,1)S(1)}, u32[]{:S(2)}, u32[]{:S(2)}) collective-permute-start(bf16[96,2048]{1,0:T(8,128)(2,1)S(1)} %get-tuple-element.24.refs_4_.refs_7_), channel_id=1, source_target_pairs={{0,1},{1,0},{2,3},{3,2},{4,5},{5,4},{6,7},{7,6},{8,9},{9,8},{10,11... | collective-permute-start | bytes 1179656 | tf_op jit(solution)/shard_map/ppermute | solution.py:320
  26.4 22.7 %collective-permute-start.7 = (bf16[96,2048]{1,0:T(8,128)(2,1)S(1)}, bf16[96,2048]{1,0:T(8,128)(2,1)}, u32[]{:S(2)}, u32[]{:S(2)}) collective-permute-start(bf16[96,2048]{1,0:T(8,128)(2,1)S(1)} %collective-permute-done.6.refs_5_.refs_8_), channel_id=1, source_target_pairs={{0,8},{1,9},{2,10},{3,11},{4,0},{5,1},{6,2},{7,3},{8,12},{9,13},{1... | collective-permute-start | bytes 1179656 | tf_op jit(solution)/shard_map/ppermute | solution.py:320
  40.6 15.4 %collective-permute-start.4 = (bf16[96,2048]{1,0:T(8,128)(2,1)S(1)}, bf16[96,2048]{1,0:T(8,128)(2,1)S(1)}, u32[]{:S(2)}, u32[]{:S(2)}) collective-permute-start(bf16[96,2048]{1,0:T(8,128)(2,1)S(1)} %collective-permute-done.3.refs_8_.refs_11_), channel_id=1, source_target_pairs={{0,8},{1,9},{2,10},{3,11},{4,0},{5,1},{6,2},{7,3},{8,12},{9,13},{1... | collective-permute-start | bytes 1179656 | tf_op jit(solution)/shard_map/ppermute | solution.py:320
  44.0 31.0 %collective-permute-start = (bf16[272,2048]{1,0:T(8,128)(2,1)}, bf16[272,2048]{1,0:T(8,128)(2,1)}, u32[]{:S(2)}, u32[]{:S(2)}) collective-permute-start(bf16[272,2048]{1,0:T(8,128)(2,1)} %get-tuple-element.21), channel_id=1, source_target_pairs={{0,16},{1,17},{2,18},{3,19},{4,20},{5,21},{6,22},{7,23},{8,24},{9,... | collective-permute-start | bytes 3342344 | tf_op jit(solution)/shard_map/ppermute | solution.py:320
  46.2 47.3 %collective-permute-start.1 = (bf16[272,2048]{1,0:T(8,128)(2,1)}, bf16[272,2048]{1,0:T(8,128)(2,1)}, u32[]{:S(2)}, u32[]{:S(2)}) collective-permute-start(bf16[272,2048]{1,0:T(8,128)(2,1)} %get-tuple-element.22), channel_id=1, source_target_pairs={{0,2},{1,3},{2,0},{3,1},{4,6},{5,7},{6,4},{7,5},{8,10},{9,11},{10,... | collective-permute-start | bytes 3342344 | tf_op jit(solution)/shard_map/ppermute | solution.py:320
  47.0 47.2 %collective-permute-start.2 = (bf16[272,2048]{1,0:T(8,128)(2,1)}, bf16[272,2048]{1,0:T(8,128)(2,1)}, u32[]{:S(2)}, u32[]{:S(2)}) collective-permute-start(bf16[272,2048]{1,0:T(8,128)(2,1)} %get-tuple-element.23), channel_id=1, source_target_pairs={{0,18},{1,19},{2,16},{3,17},{4,22},{5,23},{6,20},{7,21},{8,26},{9,... | collective-permute-start | bytes 3342344 | tf_op jit(solution)/shard_map/ppermute | solution.py:320
  57.6 15.9 %collective-permute-start.24 = (bf16[256,1024]{1,0:T(8,128)(2,1)}, bf16[256,1024]{1,0:T(8,128)(2,1)}, u32[]{:S(2)}, u32[]{:S(2)}) collective-permute-start(bf16[256,1024]{1,0:T(8,128)(2,1)} %collective-permute-done.22.refs_3_.refs_5_), channel_id=1, source_target_pairs={{0,8},{1,9},{2,10},{3,11},{4,0},{5,1},{6,2},{7,3},{8,12},{9,13},{1... | collective-permute-start | bytes 1572872 | tf_op jit(solution)/shard_map/ppermute | solution.py:320
  61.8 32.4 %collective-permute-start.8 = (bf16[96,2048]{1,0:T(8,128)(2,1)}, bf16[96,2048]{1,0:T(8,128)(2,1)}, u32[]{:S(2)}, u32[]{:S(2)}) collective-permute-start(bf16[96,2048]{1,0:T(8,128)(2,1)} %collective-permute-done.7.refs_9_.refs_12_), channel_id=1, source_target_pairs={{0,8},{1,9},{2,10},{3,11},{4,0},{5,1},{6,2},{7,3},{8,12},{9,13},{1... | collective-permute-start | bytes 1179656 | tf_op jit(solution)/shard_map/ppermute | solution.py:320
  73.5 24.3 %collective-permute-start.15 = (bf16[96,2048]{1,0:T(8,128)(2,1)}, bf16[96,2048]{1,0:T(8,128)(2,1)}, u32[]{:S(2)}, u32[]{:S(2)}) collective-permute-start(bf16[96,2048]{1,0:T(8,128)(2,1)} %collective-permute-done.7.refs_9_.refs_12_), channel_id=1, source_target_pairs={{0,1},{1,0},{2,3},{3,2},{4,5},{5,4},{6,7},{7,6},{8,9},{9,8},{10,11... | collective-permute-start | bytes 1179656 | tf_op jit(solution)/shard_map/ppermute | solution.py:320
  75.0 39.0 %collective-permute-start.16 = (bf16[96,2048]{1,0:T(8,128)(2,1)}, bf16[96,2048]{1,0:T(8,128)(2,1)S(1)}, u32[]{:S(2)}, u32[]{:S(2)}) collective-permute-start(bf16[96,2048]{1,0:T(8,128)(2,1)} %copy-done.15), channel_id=1, source_target_pairs={{0,1},{1,0},{2,3},{3,2},{4,5},{5,4},{6,7},{7,6},{8,9},{9,8},{10,11... | collective-permute-start | bytes 1179656 | tf_op jit(solution)/shard_map/ppermute | solution.py:320
  94.2 20.3 %collective-permute-start.17 = (bf16[96,2048]{1,0:T(8,128)(2,1)}, bf16[96,2048]{1,0:T(8,128)(2,1)S(1)}, u32[]{:S(2)}, u32[]{:S(2)}) collective-permute-start(bf16[96,2048]{1,0:T(8,128)(2,1)} %collective-permute-done.8.refs_13_.refs_16_), channel_id=1, source_target_pairs={{0,1},{1,0},{2,3},{3,2},{4,5},{5,4},{6,7},{7,6},{8,9},{9,8},{10,11... | collective-permute-start | bytes 1179656 | tf_op jit(solution)/shard_map/ppermute | solution.py:320
  94.2 19.7 %collective-permute-start.9 = (bf16[96,2048]{1,0:T(8,128)(2,1)}, bf16[96,2048]{1,0:T(8,128)(2,1)S(1)}, u32[]{:S(2)}, u32[]{:S(2)}) collective-permute-start(bf16[96,2048]{1,0:T(8,128)(2,1)} %collective-permute-done.8.refs_13_.refs_16_), channel_id=1, source_target_pairs={{0,8},{1,9},{2,10},{3,11},{4,0},{5,1},{6,2},{7,3},{8,12},{9,13},{1... | collective-permute-start | bytes 1179656 | tf_op jit(solution)/shard_map/ppermute | solution.py:320
  97.8 24.2 %collective-permute-start.26 = (bf16[256,1024]{1,0:T(8,128)(2,1)}, bf16[256,1024]{1,0:T(8,128)(2,1)S(1)}, u32[]{:S(2)}, u32[]{:S(2)}) collective-permute-start(bf16[256,1024]{1,0:T(8,128)(2,1)} %collective-permute-done.24.refs_5_.refs_7_), channel_id=1, source_target_pairs={{0,8},{1,9},{2,10},{3,11},{4,0},{5,1},{6,2},{7,3},{8,12},{9,13},{1... | collective-permute-start | bytes 1572872 | tf_op jit(solution)/shard_map/ppermute | solution.py:320
  105.5 17.0 %collective-permute-start.10 = (bf16[96,2048]{1,0:T(8,128)(2,1)S(1)}, bf16[96,2048]{1,0:T(8,128)(2,1)S(1)}, u32[]{:S(2)}, u32[]{:S(2)}) collective-permute-start(bf16[96,2048]{1,0:T(8,128)(2,1)S(1)} %collective-permute-done.5.refs_4_.refs_19_), channel_id=1, source_target_pairs={{0,1},{1,0},{2,3},{3,2},{4,5},{5,4},{6,7},{7,6},{8,9},{9,8},{10,11... | collective-permute-start | bytes 1179656 | tf_op jit(solution)/shard_map/ppermute | solution.py:320
  114.0 15.4 %collective-permute-start.21 = (bf16[256,1024]{1,0:T(8,128)(2,1)S(1)}, bf16[256,1024]{1,0:T(8,128)(2,1)S(1)}, u32[]{:S(2)}, u32[]{:S(2)}) collective-permute-start(bf16[256,1024]{1,0:T(8,128)(2,1)S(1)} %copy-done.8), channel_id=1, source_target_pairs={{0,1},{1,0},{2,3},{3,2},{4,5},{5,4},{6,7},{7,6},{8,9},{9,8},{10,11... | collective-permute-start | bytes 1572872 | tf_op jit(solution)/shard_map/ppermute | solution.py:320
  114.5 15.5 %collective-permute-start.23 = (bf16[256,1024]{1,0:T(8,128)(2,1)}, bf16[256,1024]{1,0:T(8,128)(2,1)S(1)}, u32[]{:S(2)}, u32[]{:S(2)}) collective-permute-start(bf16[256,1024]{1,0:T(8,128)(2,1)} %collective-permute-done.22.refs_3_.refs_5_), channel_id=1, source_target_pairs={{0,1},{1,0},{2,3},{3,2},{4,5},{5,4},{6,7},{7,6},{8,9},{9,8},{10,11... | collective-permute-start | bytes 1572872 | tf_op jit(solution)/shard_map/ppermute | solution.py:320
  127.3 40.1 %collective-permute-start.20 = (f32[64,128]{1,0:T(8,128)S(1)}, f32[64,128]{1,0:T(8,128)S(1)}, u32[]{:S(2)}, u32[]{:S(2)}) collective-permute-start(f32[64,128]{1,0:T(8,128)S(1)} %pad_maximum_fusion.3), channel_id=1, source_target_pairs={{0,18},{1,19},{2,16},{3,17},{4,22},{5,23},{6,20},{7,21},{8,26},{9,... | collective-permute-start | bytes 98312 | tf_op jit(solution)/shard_map/ppermute | solution.py:320
  129.3 38.1 %collective-permute-start.19 = (f32[64,128]{1,0:T(8,128)S(1)}, f32[64,128]{1,0:T(8,128)S(1)}, u32[]{:S(2)}, u32[]{:S(2)}) collective-permute-start(f32[64,128]{1,0:T(8,128)S(1)} %pad_maximum_fusion.2), channel_id=1, source_target_pairs={{0,2},{1,3},{2,0},{3,1},{4,6},{5,7},{6,4},{7,5},{8,10},{9,11},{10,... | collective-permute-start | bytes 98312 | tf_op jit(solution)/shard_map/ppermute | solution.py:320
  137.5 15.6 %collective-permute-start.28 = (bf16[272,1024]{1,0:T(8,128)(2,1)S(1)}, bf16[272,1024]{1,0:T(8,128)(2,1)S(1)}, u32[]{:S(2)}, u32[]{:S(2)}) collective-permute-start(bf16[272,1024]{1,0:T(8,128)(2,1)S(1)} %get-tuple-element.35), channel_id=1, source_target_pairs={{0,16},{1,17},{2,18},{3,19},{4,20},{5,21},{6,22},{7,23},{8,24},{9,... | collective-permute-start | bytes 1671176 | tf_op jit(solution)/shard_map/ppermute | solution.py:320
  139.0 25.3 %collective-permute-start.29 = (bf16[272,1024]{1,0:T(8,128)(2,1)S(1)}, bf16[272,1024]{1,0:T(8,128)(2,1)S(1)}, u32[]{:S(2)}, u32[]{:S(2)}) collective-permute-start(bf16[272,1024]{1,0:T(8,128)(2,1)S(1)} %get-tuple-element.36), channel_id=1, source_target_pairs={{0,2},{1,3},{2,0},{3,1},{4,6},{5,7},{6,4},{7,5},{8,10},{9,11},{10,... | collective-permute-start | bytes 1671176 | tf_op jit(solution)/shard_map/ppermute | solution.py:320
  140.4 24.7 %collective-permute-start.30 = (bf16[272,1024]{1,0:T(8,128)(2,1)S(1)}, bf16[272,1024]{1,0:T(8,128)(2,1)S(1)}, u32[]{:S(2)}, u32[]{:S(2)}) collective-permute-start(bf16[272,1024]{1,0:T(8,128)(2,1)S(1)} %get-tuple-element.37), channel_id=1, source_target_pairs={{0,18},{1,19},{2,16},{3,17},{4,22},{5,23},{6,20},{7,21},{8,26},{9,... | collective-permute-start | bytes 1671176 | tf_op jit(solution)/shard_map/ppermute | solution.py:320
  153.1 14.3 %collective-permute-start.18 = (f32[64,128]{1,0:T(8,128)S(1)}, f32[64,128]{1,0:T(8,128)S(1)}, u32[]{:S(2)}, u32[]{:S(2)}) collective-permute-start(f32[64,128]{1,0:T(8,128)S(1)} %pad_maximum_fusion.1), channel_id=1, source_target_pairs={{0,16},{1,17},{2,18},{3,19},{4,20},{5,21},{6,22},{7,23},{8,24},{9,... | collective-permute-start | bytes 98312 | tf_op jit(solution)/shard_map/ppermute | solution.py:320
  (36 other events, 416.4 us)

commit v2 on v1

v2 whole, which is shorter than its diff:
```python
import math

import jax
import jax.numpy as jnp
from jax import lax
from jax.experimental import pallas as pl
from jax.experimental.pallas import tpu as pltpu
from jax.sharding import PartitionSpec as P

HEAD_SIZE = 128
adapter_scale = 2.0
VMEM = 60 * 2**20
BOTH = ("replica", "tenant")


def cost(flops, bytes_accessed):
    return pl.CostEstimate(flops=flops, bytes_accessed=bytes_accessed, transcendentals=0)


def cost(flops, bytes_accessed):
    return pl.CostEstimate(flops=flops, bytes_accessed=bytes_accessed, transcendentals=0)


def split_columns(prefill, decode, tenants, owner, down, place, steps, kk, reps, sides, flips, pad):
    rows, dec = prefill.shape[0], decode.shape[0]
    ranks = down.shape[0]
    wide = steps * kk
    slots_all = owner.shape[0]

    def spot(rep, y, m, j):
        other = (y * reps + rep) ^ m
        return ((j // 2 * sides + other // reps) * 2 + j % 2) * reps + other % reps

    if kk % 128:
        stacked = jnp.concatenate([prefill, decode], axis=0)
        hot = tenants.reshape(rows, 1) == jnp.arange(slots_all, dtype=jnp.int32)[None, :]
        slots = jnp.sum(jnp.where(hot, owner[None, :], 0), axis=1).astype(jnp.bfloat16)
        slots = jnp.broadcast_to(jnp.pad(slots, (0, wide - rows))[None, :], (pad, wide))

        def pick(a, m):
            cut = a.reshape(a.shape[0], -1, kk)
            order = spot(place[0], place[1], m, jnp.arange(steps, dtype=jnp.int32))
            return jnp.take(cut, order, axis=1).reshape(a.shape[0], wide)

        return (
            [jnp.concatenate([pick(stacked, m), slots], axis=0) for m in range(4)],
            [pick(down, m) for m in flips],
        )
    count = len(flips)
    turns = 2
    each = steps // turns

    def kernel(here, own, pre, dcd, ten, dwn, *outs):
        turn = pl.program_id(0)
        slot = jnp.zeros((1, rows), jnp.float32)
        for s in range(slots_all):
            slot = jnp.where(ten[...] == s, own[s].astype(jnp.float32), slot)
        slot = jnp.broadcast_to(slot, (pad, rows)).astype(jnp.bfloat16)
        slot = jnp.concatenate([slot] + [jnp.zeros_like(slot)] * (each * kk // rows - 1), axis=1)
        for m in range(4):
            for i in range(each):
                at = spot(here[0], here[1], m, turn * each + i)
                at = pl.ds(pl.multiple_of(at * kk, kk), kk)
                to = slice(i * kk, (i + 1) * kk)
                outs[m][0:rows, to] = pre[:, at]
                below = jnp.concatenate([dcd[:, at], slot[:, to]], axis=0)
                outs[m][rows : rows + dec + pad, to] = below
                if m in flips:
                    outs[4 + flips.index(m)][:, to] = dwn[:, at]

    out = lambda j, *_: (0, j)
    whole = lambda j, *_: (0, 0)
    outs = pl.pallas_call(
        kernel,
        grid_spec=pltpu.PrefetchScalarGridSpec(
            num_scalar_prefetch=2,
            grid=(turns,),
            in_specs=[pl.BlockSpec(a.shape, whole) for a in (prefill, decode, tenants, down)],
            out_specs=[pl.BlockSpec((rows + dec + pad, each * kk), out)] * 4
            + [pl.BlockSpec((ranks, each * kk), out)] * count,
        ),
        out_shape=[jax.ShapeDtypeStruct((rows + dec + pad, wide), jnp.bfloat16)] * 4
        + [jax.ShapeDtypeStruct((ranks, wide), jnp.bfloat16)] * count,
        compiler_params=pltpu.CompilerParams(vmem_limit_bytes=VMEM),
        cost_estimate=cost(0, 10 * 2**20),
        name="split_columns",
    )(place, owner, prefill, decode, tenants, down)
    return list(outs[:4]), list(outs[4:])


def base_products(blocks, parts, spots, rows):
    kk, out_width = parts[0].shape
    tall = blocks[0].shape[0]
    n = len(parts)
    kinds = [jnp.float32] + [jnp.bfloat16] * (len(blocks) - 1)
    if kk % 128:
        quarter = jnp.zeros((n * kk, out_width), jnp.bfloat16)
        for i in range(n):
            quarter = lax.dynamic_update_slice_in_dim(quarter, parts[i], spots[i] * kk, axis=0)
        products = [jnp.dot(b, quarter, preferred_element_type=jnp.float32) for b in blocks]
        return (
            [p[:rows].astype(kind) for p, kind in zip(products, kinds)],
            [p[rows:] for p in products],
        )
    count = len(blocks)
    cut = 256

    def kernel(spot, *refs):
        xs, weights = refs[:count], refs[count : count + n]
        outs, rest = refs[count + n : 2 * count + n], refs[2 * count + n : -2]
        left, right = refs[-2:]

        @pl.when(pl.program_id(0) == 0)
        def _():
            for m in range(count):
                left[m * tall : (m + 1) * tall] = xs[m][...]

        for i in range(n):
            right[pl.ds(pl.multiple_of(spot[i] * kk, kk), kk), :] = weights[i][...]
        total = jnp.dot(left[...], right[...], preferred_element_type=jnp.float32)
        for m in range(count):
            outs[m][...] = total[m * tall : m * tall + rows].astype(kinds[m])
            rest[m][...] = total[m * tall + rows : (m + 1) * tall]

    outs = pl.pallas_call(
        kernel,
        grid_spec=pltpu.PrefetchScalarGridSpec(
            num_scalar_prefetch=1,
            grid=(out_width // cut,),
            in_specs=[pl.BlockSpec(blocks[0].shape, lambda j, s: (0, 0))] * count
            + [pl.BlockSpec((kk, cut), lambda j, s: (0, j))] * n,
            out_specs=[pl.BlockSpec((rows, cut), lambda j, s: (0, j))] * count
            + [pl.BlockSpec((tall - rows, cut), lambda j, s: (0, j))] * count,
            scratch_shapes=[
                pltpu.VMEM((count * tall, n * kk), jnp.bfloat16),
                pltpu.VMEM((n * kk, cut), jnp.bfloat16),
            ],
        ),
        out_shape=[jax.ShapeDtypeStruct((rows, out_width), kind) for kind in kinds]
        + [jax.ShapeDtypeStruct((tall - rows, out_width), jnp.float32)] * count,
        compiler_params=pltpu.CompilerParams(vmem_limit_bytes=VMEM),
        cost_estimate=cost(2 * count * tall * n * kk * out_width, (count * tall + out_width) * 2 * n * kk),
        name="base_products",
    )(spots, *blocks, *parts)
    return list(outs[:count]), list(outs[count:])


def lowered_products(blocks, pieces, columns, rows, first, rank, after):
    wide = blocks[0].shape[1]
    ranks = pieces[0].shape[0]
    total_ranks = len(pieces) * ranks
    count = len(blocks)
    folds = 128 // rank
    n = len(pieces)
    tall = rows // folds
    if n > 16:
        sums = []
        down = jnp.concatenate(pieces, axis=0)
        for b in blocks:
            product = lax.dot_general(
                b[:rows], down, (((1,), (1,)), ((), ())), preferred_element_type=jnp.float32
            )
            slot = b[first, :rows].astype(jnp.float32)
            kept = jnp.where(slot[:, None] == columns, product, 0.0)
            kept = sum(kept[:, i : i + rank] for i in range(0, total_ranks, rank))
            sums.append(jnp.concatenate(jnp.split(kept, folds, axis=0), axis=1))
        return sums
    base_row = first // 16 * 16

    def kernel(_, *refs):
        xs, ds = refs[:count], refs[count : count + n]
        col, outs, left = refs[count + n], refs[count + n + 1 : -1], refs[-1]
        slot = []
        for m in range(count):
            left[m * rows : (m + 1) * rows] = xs[m][:rows]
            slot.append(xs[m][base_row : base_row + 16, :rows].astype(jnp.float32))
        slot = [jnp.transpose(s)[:, first - base_row : first - base_row + 1] for s in slot]
        slot = jnp.broadcast_to(jnp.concatenate(slot, axis=0), (count * rows, 128))
        kept = None
        for i in range(0, n, 2):
            down = jnp.concatenate([d[...] for d in ds[i : i + 2]], axis=0)
            term = lax.dot_general(
                left[...], down, (((1,), (1,)), ((), ())), preferred_element_type=jnp.float32
            )
            for h in range(0, 2 * ranks, 128):
                at = i * ranks + h
                part = jnp.where(slot == col[0:1, at : at + 128], term[:, h : h + 128], 0.0)
                kept = part if kept is None else kept + part
        kept = kept + pltpu.roll(kept, rank, 1)
        kept = kept + pltpu.roll(kept, 2 * rank, 1)
        lane = lax.broadcasted_iota(jnp.int32, (tall, 128), 1) // rank
        for m in range(count):
            packed = jnp.zeros((tall, 128), jnp.float32)
            for b in range(folds):
                at = m * rows + b * tall
                packed = jnp.where(lane == b, kept[at : at + tall], packed)
            outs[m][...] = packed

    whole = lambda j: (0, 0)
    return pl.pallas_call(
        kernel,
        grid=(1,),
        in_specs=[pl.BlockSpec(memory_space=pl.ANY)]
        + [pl.BlockSpec(blocks[0].shape, whole)] * count
        + [pl.BlockSpec((ranks, wide), whole)] * n
        + [pl.BlockSpec(columns.shape, whole)],
        out_specs=[pl.BlockSpec((tall, 128), whole)] * count,
        out_shape=[jax.ShapeDtypeStruct((tall, 128), jnp.float32)] * count,
        scratch_shapes=[pltpu.VMEM((count * rows, wide), jnp.bfloat16)],
        compiler_params=pltpu.CompilerParams(vmem_limit_bytes=VMEM),
        cost_estimate=cost(2 * count * rows * wide * total_ranks, (count * rows + total_ranks) * 2 * wide),
        name="lowered_products",
    )(after, *blocks, *pieces, columns)


def finish(parts, block, ups, columns, bases, rows, first, rank):
    packed_rows = parts[0].shape[0]
    folds = rows // packed_rows
    out_width = bases[0].shape[1]
    n = len(ups)
    tall = ups[0].shape[0]
    base_row = first // 16 * 16
    if n * tall > 2048:
        lowered = sum(parts[1:], parts[0]).astype(jnp.bfloat16)
        lowered = jnp.concatenate(
            [lowered[:, b * rank : (b + 1) * rank] for b in range(folds)], axis=0
        )
        slot = block[first, :rows].astype(jnp.float32)
        spread = jnp.where(
            slot[:, None] == columns, jnp.tile(lowered, (1, n * tall // rank)), jnp.bfloat16(0)
        )
        up = jnp.concatenate(ups, axis=0)
        delta = jnp.dot(spread, up, preferred_element_type=jnp.float32).astype(jnp.bfloat16)
        base = sum(b.astype(jnp.float32) for b in bases)[:rows]
        return (base + adapter_scale * delta.astype(jnp.float32)).astype(jnp.bfloat16)
    cut = 256

    def kernel(*refs):
        packs = refs[:4]
        blk, col = refs[4:6]
        bas, upr = refs[6:10], refs[10 : 10 + n]
        out, wide = refs[10 + n :]

        @pl.when(pl.program_id(0) == 0)
        def _():
            slot = jnp.transpose(blk[...].astype(jnp.float32))
            slot = slot[:, first - base_row : first - base_row + 1]
            packed = (packs[0][...] + packs[1][...]) + (packs[2][...] + packs[3][...])
            lane = lax.broadcasted_iota(jnp.int32, packed.shape, 1) // rank
            spread = []
            for b in range(folds):
                one = jnp.where(lane == b, packed, 0.0)
                one = one + pltpu.roll(one, rank, 1)
                one = one + pltpu.roll(one, 2 * rank, 1)
                spread.append(one)
            lowered = jnp.concatenate(spread, axis=0)
            for i in range(0, n * tall, 128):
                kept = jnp.where(slot == col[0:1, i : i + 128], lowered, 0.0)
                wide[:, i : i + 128] = kept.astype(jnp.bfloat16)

        up = jnp.concatenate([u[...] for u in upr], axis=0)
        delta = jnp.dot(wide[...], up, preferred_element_type=jnp.float32)
        base = bas[0][0:rows]
        for b in bas[1:]:
            base = base + b[0:rows].astype(jnp.float32)
        out[...] = (base + adapter_scale * delta.astype(jnp.bfloat16).astype(jnp.float32)).astype(
            jnp.bfloat16
        )

    one = lambda j: (0, 0)
    column = lambda j: (0, j)
    return pl.pallas_call(
        kernel,
        grid=(out_width // cut,),
        in_specs=[pl.BlockSpec(parts[0].shape, one)] * 4
        + [
            pl.BlockSpec((16, rows), lambda j: (base_row // 16, 0)),
            pl.BlockSpec(columns.shape, one),
        ]
        + [pl.BlockSpec((bases[0].shape[0], cut), column)] * 4
        + [pl.BlockSpec((tall, cut), column)] * n,
        out_specs=pl.BlockSpec((rows, cut), column),
        out_shape=jax.ShapeDtypeStruct((rows, out_width), jnp.bfloat16),
        scratch_shapes=[pltpu.VMEM((rows, n * tall), jnp.bfloat16)],
        compiler_params=pltpu.CompilerParams(vmem_limit_bytes=VMEM),
        cost_estimate=cost(2 * rows * n * tall * out_width, 5 * 2**20),
        name="finish",
    )(*parts, block, columns, *bases, *ups)


def body(
    prefill_rows,
    tenant_ids,
    owner_slot,
    decode_rows,
    queries,
    key_store_cache,
    value_store_cache,
    context_len,
    base_weight,
    adapter_down,
    adapter_up,
):
    reps, peers = lax.axis_size("replica"), lax.axis_size("tenant")
    planes = reps * peers // 8
    sides = peers // (2 * planes)
    local_slots, rank, width = adapter_down.shape
    slots_all = local_slots * peers
    rows, dec = prefill_rows.shape[0], decode_rows.shape[0]
    out_width = base_weight.shape[1]
    half_width = out_width // 2
    kk = base_weight.shape[0] // reps
    steps = 2 * planes
    quarter = steps * kk
    pad = 16 - dec % 16
    r, t = lax.axis_index("replica"), lax.axis_index("tenant")
    z, y, c = t // (2 * sides), (t // 2) % sides, t % 2
    q = y * reps + r

    order = list(range(0, planes, 2)) + list(range(1, planes, 2))[::-1]
    after = {order[i]: order[(i + 1) % planes] for i in range(planes)}
    everyone = [(a, b) for a in range(reps) for b in range(peers)]

    def flip(m):
        pairs = []
        for a, b in everyone:
            other = (((b // 2) % sides) * reps + a) ^ m
            to = (b // (2 * sides) * sides + other // reps) * 2 + b % 2
            pairs.append((a * peers + b, (other % reps) * peers + to))
        return pairs

    flips = {m: flip(m) for m in (1, 2, 3)}
    ring = [
        (a * peers + b, a * peers + after[b // (2 * sides)] * 2 * sides + b % (2 * sides))
        for a, b in everyone
    ]
    cores = [(a * peers + b, a * peers + (b ^ 1)) for a, b in everyone]

    def send(value, pairs):
        return lax.ppermute(value, BOTH, pairs)

    place = jnp.where(z % 2 == 0, z // 2, planes - 1 - z // 2)

    def plane_of(k):
        spot = (place - k + planes) % planes
        return jnp.where(spot < planes // 2, 2 * spot, 2 * (planes - 1 - spot) + 1)

    spots = jnp.arange(steps, dtype=jnp.int32)
    spots = plane_of(spots // 2) * 2 + (c ^ (spots % 2))
    ranks = local_slots * rank

    def both(value):
        return [value, send(value, cores)]

    def phase(*values):
        return lax.optimization_barrier(values)

    def paired(near, far):
        return near if far is None else jnp.concatenate([near, far], axis=0)

    bases = [lax.dynamic_slice_in_dim(base_weight, r * kk, kk, axis=0)]
    bases.append(send(bases[0], ring))
    up = adapter_up.reshape(ranks, out_width)
    ups = [paired(up, send(up, flips[reps]) if sides == 2 else None)]
    ups.append(send(ups[0], ring))
    messages, downs = split_columns(
        prefill_rows,
        decode_rows,
        tenant_ids.reshape(1, rows),
        owner_slot,
        adapter_down.reshape(ranks, width),
        jnp.stack([r, y]),
        steps,
        kk,
        reps,
        sides,
        [0, reps] if sides == 2 else [0],
        pad,
    )
    near = [send(messages[m], flips[m]) for m in (1, 2)]
    down_far = send(downs[1], flips[reps]) if sides == 2 else None
    bases, ups, down_far = phase(bases, ups, down_far)

    downs = [paired(downs[0], down_far)]
    bases.append(send(bases[-1], ring))
    downs.append(send(downs[-1], ring))
    base_parts = both(bases[0]) + both(bases[1])
    near, bases, downs, base_parts, far = phase(near, bases, downs, base_parts, messages[3])

    far = send(far, flips[3])
    while len(bases) < planes:
        bases.append(send(bases[-1], ring))
    downs.append(send(downs[-1], ring))
    for held in bases[2:-1]:
        base_parts = base_parts + both(held)
    pieces = both(downs[0]) + both(downs[1])
    near, far, bases, downs, base_parts, pieces = phase(
        near, far, bases, downs, base_parts, pieces
    )

    blocks = [messages[0], *near, far]
    base_parts = base_parts + both(bases[-1])
    partials, fresh = base_products(blocks, base_parts, spots, rows)
    while len(downs) < planes:
        downs.append(send(downs[-1], ring))
    partials, fresh, downs, pieces = phase(partials, fresh, downs, pieces)

    fresh = [fresh[0]] + [send(fresh[m], flips[m]) for m in (1, 2, 3)]
    recent_output = sum(fresh[1:], fresh[0])[:dec].astype(jnp.bfloat16)
    base = [partials[0]] + [send(partials[m], flips[m]) for m in (1, 2, 3)]
    while len(ups) < planes - 1:
        ups.append(send(ups[-1], ring))
    pieces = pieces + sum([both(d) for d in downs[2:]], [])
    ups, pieces = phase(ups, pieces)
    ups.append(send(ups[-1], ring))
    up_parts = sum([both(u) for u in ups], [])

    group = jnp.arange(slots_all, dtype=jnp.int32)
    inner = group % local_slots
    side = (group // local_slots) % sides
    core = (group // (local_slots * sides)) % 2
    step = group // (local_slots * sides * 2)
    column_slot = ((plane_of(step) * sides + (y ^ side)) * 2 + (c ^ core)) * local_slots + inner
    columns = jnp.repeat(column_slot, rank).astype(jnp.float32)[None, :]
    first = rows + dec
    packed = lowered_products(blocks, pieces, columns, rows, first, rank, partials[3])
    packed = [packed[0]] + [send(packed[m], flips[m]) for m in (1, 2, 3)]
    projected = finish(packed, messages[0], up_parts, columns, base, rows, first, rank)

    kv_heads = half_width // HEAD_SIZE
    query_groups = queries.shape[1] // half_width
    positions = key_store_cache.shape[1]
    newest_keys = recent_output[:, :half_width].reshape(dec, kv_heads, HEAD_SIZE)
    newest_values = recent_output[:, half_width:].reshape(dec, kv_heads, HEAD_SIZE)
    query_head_rows = queries.reshape(dec, kv_heads, query_groups, HEAD_SIZE)
    stored_keys = key_store_cache.reshape(dec, positions, kv_heads, HEAD_SIZE)
    stored_values = value_store_cache.reshape(dec, positions, kv_heads, HEAD_SIZE)
    scale = 1.0 / math.sqrt(HEAD_SIZE)
    scores = (
        jnp.einsum(
            "bkgd,bckd->bkgc", query_head_rows, stored_keys, preferred_element_type=jnp.float32
        )
        * scale
    )
    own_score = (
        jnp.einsum(
            "bkgd,bkd->bkg", query_head_rows, newest_keys, preferred_element_type=jnp.float32
        )
        * scale
    )
    live = jnp.arange(positions, dtype=jnp.int32)[None, :] < context_len[:, None]
    scores = jnp.where(live[:, None, None, :], scores, -jnp.inf)
    top = jnp.maximum(jnp.max(scores, axis=-1), own_score)
    cached_weight = jnp.exp(scores - top[..., None])
    own_weight = jnp.exp(own_score - top)
    total = jnp.sum(cached_weight, axis=-1) + own_weight
    probs = (cached_weight / total[..., None]).astype(jnp.bfloat16)
    probs_own = (own_weight / total).astype(jnp.bfloat16)
    mixed = jnp.einsum("bkgc,bckd->bkgd", probs, stored_values, preferred_element_type=jnp.float32)
    mixed = (
        mixed
        + probs_own.astype(jnp.float32)[..., None]
        * newest_values.astype(jnp.float32)[:, :, None, :]
    )
    attended = mixed.reshape(dec, query_groups * kv_heads * HEAD_SIZE).astype(jnp.bfloat16)
    return (projected, attended)


def solution(mesh):
    in_specs = (
        P(BOTH, None),
        P(BOTH, None),
        P(),
        P(BOTH, None),
        P(BOTH, None),
        P(BOTH, None, None),
        P(BOTH, None, None),
        P(BOTH),
        P("tenant", None),
        P("tenant", None, None),
        P("tenant", None, None),
    )
    out_specs = (P(BOTH, None), P(BOTH, None))
    return jax.shard_map(body, mesh=mesh, in_specs=in_specs, out_specs=out_specs, check_vma=False)
```

time: 171 us -> 145 us (0.85)
  waiting for transfers between devices: 85.8 us -> 50.3 us
  starting transfers between devices: 32.1 us -> 41.4 us
  local copies, waits for them, and re-layouts: 14.6 us -> 11.7 us
  matrix products: 3.13 us -> 5.76 us
    ppermute x31 -> x35, waiting for transfers between devices: 85.8 us -> 50.3 us  [send(): return lax.ppermute(value, BOTH, pairs)]
    ppermute x31 -> x35, starting transfers between devices: 32.1 us -> 41.4 us  [send(): return lax.ppermute(value, BOTH, pairs)]
    unnamed x57 -> x54, local copies, waits for them, and re-layouts: 13 us -> 7.54 us
    dynamic_slice x0 -> x1, local copies, waits for them, and re-layouts: none -> 2.05 us  [body(): bases = [lax.dynamic_slice_in_dim(base_weight, r * kk, kk, axis=0)]]
    dot_general x1, matrix products: 0.71 us -> 2.6 us  [body(): jnp.einsum('bkgc,bckd->bkgd', probs, stored_values, preferred_element_typ...]
    pallas_call x2 -> x1, Pallas kernels: 11.6 us -> 10.4 us  [base_products(): pl.pallas_call(kernel, grid_spec=pltpu.PrefetchScalarGridSpec(num_scalar_...]
    pallas_call x3 -> x2, Pallas kernels: 13.5 us -> 13.8 us  [the longest x1 8.75 us: lowered_products(): pl.pallas_call(kernel, grid=(1,), in_specs=[pl.BlockSpec(memory_space=pl....]
  transfers between devices with their start and end apart: 31 -> 35, of which waited for: 11 -> 9; matrix products, arithmetic and copies ran while one was open for 4% -> 10% of each run, Pallas kernels for 13% -> 17%
where the time goes in v2:
time: 145 us
  waiting for transfers between devices  50.3 us (35%)
  starting transfers between devices  41.4 us (29%)
  Pallas kernels  30.2 us (21%)
  local copies, waits for them, and re-layouts  11.7 us (8%)
  matrix products  5.76 us (4%)
  other arithmetic  4.3 us (3%)
    ppermute x35, waiting for transfers between devices, send(): return lax.ppermute(value, BOTH, pairs)  50.3 us
    ppermute x35, starting transfers between devices, send(): return lax.ppermute(value, BOTH, pairs)  41.4 us
    pallas_call x1, Pallas kernels, base_products(): pl.pallas_call(kernel, grid_spec=pltpu.PrefetchScalarGridSpec(num_scalar_...  10.4 us
    pallas_call x1, Pallas kernels, lowered_products(): pl.pallas_call(kernel, grid=(1,), in_specs=[pl.BlockSpec(memory_space=pl....  8.75 us
    unnamed x54, local copies, waits for them, and re-layouts  7.54 us
    pallas_call x1, Pallas kernels, split_columns(): pl.pallas_call(kernel, grid_spec=pltpu.PrefetchScalarGridSpec(num_scalar_...  6.08 us
    pallas_call x1, Pallas kernels, finish(): pl.pallas_call(kernel, grid=(out_width // cut,), in_specs=[pl.BlockSpec(p...  5.04 us
  transfers between devices with their start and end apart: 35, of which 9 were waited for; matrix products, arithmetic and copies ran while one was open for 10% of the time, Pallas kernels for 17%

profile of v2, /device:TPU:0, one launch (start us, length us, event | category | flops | bytes accessed | tf_op | source)
XLA Modules:
  0.0 144.6 jit_solution(11143275617848605020)
XLA Ops:
  0.7 2.0 %constant_dynamic-slice_fusion.refs_4_ = bf16[256,1024]{1,0:T(8,128)(2,1)} fusion(bf16[512,1024]{1,0:T(8,128)(2,1)} %param.19, s32[]{:T(128)S(6)} %select_n.97), kind=kLoop, calls=%fused_computation.84 | loop fusion | bytes 1048580 | tf_op jit(solution)/shard_map/dynamic_slice | solution.py:361
  2.7 4.0 %collective-permute-start.2 = (bf16[256,1024]{1,0:T(8,128)(2,1)}, bf16[256,1024]{1,0:T(8,128)(2,1)}, u32[]{:S(2)}, u32[]{:S(2)}) collective-permute-start(bf16[256,1024]{1,0:T(8,128)(2,1)} %constant_dynamic-slice_fusion.refs_4_), channel_id=1, source_target_pairs={{0,8},{1,9},{2,10},{3,11},{4,0},{5,1},{6,2},{7,3},{8,12},{9,13},{1... | collective-permute-start | bytes 1572872 | tf_op jit(solution)/shard_map/ppermute | solution.py:340
  6.7 1.5 %collective-permute-start.3 = (bf16[64,1024]{1,0:T(8,128)(2,1)}, bf16[64,1024]{1,0:T(8,128)(2,1)S(1)}, u32[]{:S(2)}, u32[]{:S(2)}) collective-permute-start(bf16[64,1024]{1,0:T(8,128)(2,1)} %bitcast.50), channel_id=1, source_target_pairs={{0,2},{1,3},{2,0},{3,1},{4,6},{5,7},{6,4},{7,5},{8,10},{9,11},{10,... | collective-permute-start | bytes 393224 | tf_op jit(solution)/shard_map/ppermute | solution.py:340
  8.8 6.1 %split_columns.1 = (bf16[272,2048]{1,0:T(8,128)(2,1)}, bf16[272,2048]{1,0:T(8,128)(2,1)}, bf16[272,2048]{1,0:T(8,128)(2,1)}, bf16[272,2048]{1,0:T(8,128)(2,1)}, ...) custom-call(s32[2]{0:T(128)} %pad_add_fusion.here, s32[32]{0:T(128)} %own.1, bf16[256,8192]{1,0:T(8,128)(2,1)} %pre.1, ...), custom_call_target="tpu_custom_call" | custom-call | bytes 10485760 | tf_op jit(solution)/shard_map/split_columns/pallas_call | solution.py:73
  16.2 1.6 %collective-permute-start.4 = (bf16[128,1024]{1,0:T(8,128)(2,1)S(1)}, bf16[128,1024]{1,0:T(8,128)(2,1)S(1)}, u32[]{:S(2)}, u32[]{:S(2)}) collective-permute-start(bf16[128,1024]{1,0:T(8,128)(2,1)S(1)} %pad_maximum_fusion.refs_10_), channel_id=1, source_target_pairs={{0,8},{1,9},{2,10},{3,11},{4,0},{5,1},{6,2},{7,3},{8,12},{9,13},{1... | collective-permute-start | bytes 786440 | tf_op jit(solution)/shard_map/ppermute | solution.py:340
  21.7 2.6 %collective-permute-done.5 = bf16[64,2048]{1,0:T(8,128)(2,1)S(1)} collective-permute-done((bf16[64,2048]{1,0:T(8,128)(2,1)}, bf16[64,2048]{1,0:T(8,128)(2,1)S(1)}, u32[]{:S(2)}, u32[]{:S(2)}) %collective-permute-start.5) | collective-permute-done | bytes 262176 | tf_op jit(solution)/shard_map/ppermute | solution.py:340
  25.1 2.8 %collective-permute-start.7 = (bf16[128,2048]{1,0:T(8,128)(2,1)S(1)}, bf16[128,2048]{1,0:T(8,128)(2,1)S(1)}, u32[]{:S(2)}, u32[]{:S(2)}) collective-permute-start(bf16[128,2048]{1,0:T(8,128)(2,1)S(1)} %constant_dynamic-update-slice_fusion.refs_4_), channel_id=1, source_target_pairs={{0,8},{1,9},{2,10},{3,11},{4,0},{5,1},{6,2},{7,3},{8,12},{9,13},{1... | collective-permute-start | bytes 1572872 | tf_op jit(solution)/shard_map/ppermute | solution.py:340
  28.6 11.7 %collective-permute-done.7.refs_6_ = bf16[128,2048]{1,0:T(8,128)(2,1)S(1)} collective-permute-done((bf16[128,2048]{1,0:T(8,128)(2,1)S(1)}, bf16[128,2048]{1,0:T(8,128)(2,1)S(1)}, u32[]{:S(2)}, u32[]{:S(2)}) %collective-permute-start.7) | collective-permute-done | bytes 524320 | tf_op jit(solution)/shard_map/ppermute | solution.py:340
  40.3 9.3 %collective-permute-done.6.refs_8_ = bf16[256,1024]{1,0:T(8,128)(2,1)S(1)} collective-permute-done((bf16[256,1024]{1,0:T(8,128)(2,1)}, bf16[256,1024]{1,0:T(8,128)(2,1)S(1)}, u32[]{:S(2)}, u32[]{:S(2)}) %collective-permute-start.6) | collective-permute-done | bytes 524320 | tf_op jit(solution)/shard_map/ppermute | solution.py:340
  49.7 2.5 %collective-permute-start.10 = (bf16[272,2048]{1,0:T(8,128)(2,1)}, bf16[272,2048]{1,0:T(8,128)(2,1)S(1)}, u32[]{:S(2)}, u32[]{:S(2)}) collective-permute-start(bf16[272,2048]{1,0:T(8,128)(2,1)} %get-tuple-element.86), channel_id=1, source_target_pairs={{0,18},{1,19},{2,16},{3,17},{4,22},{5,23},{6,20},{7,21},{8,26},{9,... | collective-permute-start | bytes 3342344 | tf_op jit(solution)/shard_map/ppermute | solution.py:340
  52.2 3.3 %collective-permute-start.11 = (bf16[256,1024]{1,0:T(8,128)(2,1)S(1)}, bf16[256,1024]{1,0:T(8,128)(2,1)}, u32[]{:S(2)}, u32[]{:S(2)}) collective-permute-start(bf16[256,1024]{1,0:T(8,128)(2,1)S(1)} %collective-permute-done.6.refs_8_), channel_id=1, source_target_pairs={{0,8},{1,9},{2,10},{3,11},{4,0},{5,1},{6,2},{7,3},{8,12},{9,13},{1... | collective-permute-start | bytes 1572872 | tf_op jit(solution)/shard_map/ppermute | solution.py:340
  56.0 11.8 %collective-permute-done.11.refs_10_ = bf16[256,1024]{1,0:T(8,128)(2,1)} collective-permute-done((bf16[256,1024]{1,0:T(8,128)(2,1)S(1)}, bf16[256,1024]{1,0:T(8,128)(2,1)}, u32[]{:S(2)}, u32[]{:S(2)}) %collective-permute-start.11) | collective-permute-done | bytes 524320 | tf_op jit(solution)/shard_map/ppermute | solution.py:340
  67.8 8.0 %collective-permute-done.12.refs_8_ = bf16[128,2048]{1,0:T(8,128)(2,1)S(1)} collective-permute-done((bf16[128,2048]{1,0:T(8,128)(2,1)S(1)}, bf16[128,2048]{1,0:T(8,128)(2,1)S(1)}, u32[]{:S(2)}, u32[]{:S(2)}) %collective-permute-start.12) | collective-permute-done | bytes 524320 | tf_op jit(solution)/shard_map/ppermute | solution.py:340
  78.8 2.2 %fusion.50 = (f32[8,4,8]{2,1,0:T(4,128)S(1)}, f32[8,4,8,384]{3,2,1,0:T(8,128)S(1)}) fusion(bf16[8,4,8,128]{3,0,2,1:T(8,128)(2,1)} %bitcast.55, pred[8,384]{1,0:T(8,128)(4,1)} %iota_compare_fusion, bf16[8,384,512]{2,1,0:T(8,128)(2,1)S(1)} %copy-done), kind=kOutput, calls=%fused_computation.85 | convolution fusion | flops 25460480 | bytes 3608576 | tf_op jit(solution)/shard_map/bkgd,bckd->bkgc/dot_general | solution.py:440
  81.0 3.4 %collective-permute-start.17 = (bf16[128,2048]{1,0:T(8,128)(2,1)S(1)}, bf16[128,2048]{1,0:T(8,128)(2,1)}, u32[]{:S(2)}, u32[]{:S(2)}) collective-permute-start(bf16[128,2048]{1,0:T(8,128)(2,1)S(1)} %copy-done.19), channel_id=1, source_target_pairs={{0,8},{1,9},{2,10},{3,11},{4,0},{5,1},{6,2},{7,3},{8,12},{9,13},{1... | collective-permute-start | bytes 1572872 | tf_op jit(solution)/shard_map/ppermute | solution.py:340
  84.9 10.4 %base_products.1 = (f32[256,1024]{1,0:T(8,128)}, bf16[256,1024]{1,0:T(8,128)(2,1)}, bf16[256,1024]{1,0:T(8,128)(2,1)}, bf16[256,1024]{1,0:T(8,128)(2,1)}, f32[16...) custom-call(s32[8]{0:T(128)} %fusion.33.spot, ...), custom_call_target="tpu_custom_call" | custom-call | flops 4563402752 | bytes 8650752 | tf_op jit(solution)/shard_map/base_products/pallas_call | solution.py:125
  97.4 2.4 %collective-permute-start.34 = (f32[16,1024]{1,0:T(8,128)}, f32[16,1024]{1,0:T(8,128)}, u32[]{:S(2)}, u32[]{:S(2)}) collective-permute-start(f32[16,1024]{1,0:T(8,128)} %get-tuple-element.147), channel_id=1, source_target_pairs={{0,18},{1,19},{2,16},{3,17},{4,22},{5,23},{6,20},{7,21},{8,26},{9,... | collective-permute-start | bytes 196616 | tf_op jit(solution)/shard_map/ppermute | solution.py:340
  101.8 3.5 %collective-permute-start.18 = (bf16[128,1024]{1,0:T(8,128)(2,1)}, bf16[128,1024]{1,0:T(8,128)(2,1)}, u32[]{:S(2)}, u32[]{:S(2)}) collective-permute-start(bf16[128,1024]{1,0:T(8,128)(2,1)} %copy-done.3), channel_id=1, source_target_pairs={{0,8},{1,9},{2,10},{3,11},{4,0},{5,1},{6,2},{7,3},{8,12},{9,13},{1... | collective-permute-start | bytes 786440 | tf_op jit(solution)/shard_map/ppermute | solution.py:340
  110.3 1.9 %collective-permute-start.26 = (bf16[256,1024]{1,0:T(8,128)(2,1)}, bf16[256,1024]{1,0:T(8,128)(2,1)}, u32[]{:S(2)}, u32[]{:S(2)}) collective-permute-start(bf16[256,1024]{1,0:T(8,128)(2,1)} %get-tuple-element.117._), channel_id=1, source_target_pairs={{0,18},{1,19},{2,16},{3,17},{4,22},{5,23},{6,20},{7,21},{8,26},{9,... | collective-permute-start | bytes 1572872 | tf_op jit(solution)/shard_map/ppermute | solution.py:340
  112.2 2.0 %collective-permute-start.30 = (bf16[128,1024]{1,0:T(8,128)(2,1)}, bf16[128,1024]{1,0:T(8,128)(2,1)}, u32[]{:S(2)}, u32[]{:S(2)}) collective-permute-start(bf16[128,1024]{1,0:T(8,128)(2,1)} %collective-permute-done.18.refs_14_), channel_id=1, source_target_pairs={{0,8},{1,9},{2,10},{3,11},{4,0},{5,1},{6,2},{7,3},{8,12},{9,13},{1... | collective-permute-start | bytes 786440 | tf_op jit(solution)/shard_map/ppermute | solution.py:340
  114.2 8.7 %lowered_products.1 = (f32[64,128]{1,0:T(8,128)}, f32[64,128]{1,0:T(8,128)}, f32[64,128]{1,0:T(8,128)}, f32[64,128]{1,0:T(8,128)}) custom-call(bf16[256,1024]{1,0:T(8,128)(2,1)} %get-tuple-element.117._, bf16[272,2048]{1,0:T(8,128)(2,1)} %get-tuple-element.75.refs_0_.refs_4_, bf16[272,2048]{1,0:T(8,128)(2,1)} %copy-done.14, bf16[272,2048]{1,0:T(8,128)(2,1)} %copy-done.15, ...), custom_call_target="tpu_custom_call" | custom-call | flops 4294967296 | bytes 8388608 | tf_op jit(solution)/shard_map/lowered_products/pallas_call | solution.py:200
  126.6 5.1 %collective-permute-done.25.refs_8_ = bf16[256,1024]{1,0:T(8,128)(2,1)} collective-permute-done((bf16[256,1024]{1,0:T(8,128)(2,1)}, bf16[256,1024]{1,0:T(8,128)(2,1)}, u32[]{:S(2)}, u32[]{:S(2)}) %collective-permute-start.25) | collective-permute-done | bytes 524320 | tf_op jit(solution)/shard_map/ppermute | solution.py:340
  133.8 2.6 %fusion.18 = bf16[1,8,32,128]{3,2,1,0:T(8,128)(2,1)S(1)} fusion(f32[8,4,8,384]{3,2,1,0:T(8,128)S(1)} %get-tuple-element.153, f32[8,4,8]{2,1,0:T(4,128)S(1)} %get-tuple-element.149, f32[8,4,8]{2,1,0:T(4,128)S(1)} %multiply_maximum_fusion, f32[8,4,128]{2,1,0:T(4,128)S(1)} %copy.16, f32[8,4,8]{2,1,0:T(4,128)S(1)} %get-tuple-element.148, ...), kind=kOutput, calls=%fused_computation.10 | convolution fusion | flops 25559040 | bytes 3623936 | tf_op jit(solution)/shard_map/bkgc,bckd->bkgd/dot_general | solution.py:459
  139.6 5.0 %finish.1 = bf16[256,1024]{1,0:T(8,128)(2,1)} custom-call(f32[64,128]{1,0:T(8,128)} %get-tuple-element.134.refs_0_, f32[64,128]{1,0:T(8,128)} %copy-done.10, f32[64,128]{1,0:T(8,128)} %copy-done.11, f32[64,128]{1,0:T(8,128)} %copy-done.12, bf16[272,2048]{1,0:T(8,128)(2,1)} %get-tuple-element.75.refs_0_.refs_4_, ...), custom_call_target="tpu_custom_call" | custom-call | flops 536870912 | bytes 5242880 | tf_op jit(solution)/shard_map/finish/pallas_call | solution.py:272
  (122 shorter events, 29.3 us)
Async XLA Ops:
  2.7 22.4 %collective-permute-start.2 = (bf16[256,1024]{1,0:T(8,128)(2,1)}, bf16[256,1024]{1,0:T(8,128)(2,1)}, u32[]{:S(2)}, u32[]{:S(2)}) collective-permute-start(bf16[256,1024]{1,0:T(8,128)(2,1)} %constant_dynamic-slice_fusion.refs_4_), channel_id=1, source_target_pairs={{0,8},{1,9},{2,10},{3,11},{4,0},{5,1},{6,2},{7,3},{8,12},{9,13},{1... | collective-permute-start | bytes 1572872 | tf_op jit(solution)/shard_map/ppermute | solution.py:340
  6.7 8.7 %collective-permute-start.3 = (bf16[64,1024]{1,0:T(8,128)(2,1)}, bf16[64,1024]{1,0:T(8,128)(2,1)S(1)}, u32[]{:S(2)}, u32[]{:S(2)}) collective-permute-start(bf16[64,1024]{1,0:T(8,128)(2,1)} %bitcast.50), channel_id=1, source_target_pairs={{0,2},{1,3},{2,0},{3,1},{4,6},{5,7},{6,4},{7,5},{8,10},{9,11},{10,... | collective-permute-start | bytes 393224 | tf_op jit(solution)/shard_map/ppermute | solution.py:340
  14.9 9.5 %collective-permute-start.5 = (bf16[64,2048]{1,0:T(8,128)(2,1)}, bf16[64,2048]{1,0:T(8,128)(2,1)S(1)}, u32[]{:S(2)}, u32[]{:S(2)}) collective-permute-start(bf16[64,2048]{1,0:T(8,128)(2,1)} %get-tuple-element.78), channel_id=1, source_target_pairs={{0,2},{1,3},{2,0},{3,1},{4,6},{5,7},{6,4},{7,5},{8,10},{9,11},{10,... | collective-permute-start | bytes 786440 | tf_op jit(solution)/shard_map/ppermute | solution.py:340
  17.8 31.9 %collective-permute-start = (bf16[272,2048]{1,0:T(8,128)(2,1)}, bf16[272,2048]{1,0:T(8,128)(2,1)S(1)}, u32[]{:S(2)}, u32[]{:S(2)}) collective-permute-start(bf16[272,2048]{1,0:T(8,128)(2,1)} %get-tuple-element.76), channel_id=1, source_target_pairs={{0,16},{1,17},{2,18},{3,19},{4,20},{5,21},{6,22},{7,23},{8,24},{9,... | collective-permute-start | bytes 3342344 | tf_op jit(solution)/shard_map/ppermute | solution.py:340
  19.3 30.4 %collective-permute-start.1 = (bf16[272,2048]{1,0:T(8,128)(2,1)}, bf16[272,2048]{1,0:T(8,128)(2,1)S(1)}, u32[]{:S(2)}, u32[]{:S(2)}) collective-permute-start(bf16[272,2048]{1,0:T(8,128)(2,1)} %get-tuple-element.77), channel_id=1, source_target_pairs={{0,2},{1,3},{2,0},{3,1},{4,6},{5,7},{6,4},{7,5},{8,10},{9,11},{10,... | collective-permute-start | bytes 3342344 | tf_op jit(solution)/shard_map/ppermute | solution.py:340
  25.1 15.2 %collective-permute-start.7 = (bf16[128,2048]{1,0:T(8,128)(2,1)S(1)}, bf16[128,2048]{1,0:T(8,128)(2,1)S(1)}, u32[]{:S(2)}, u32[]{:S(2)}) collective-permute-start(bf16[128,2048]{1,0:T(8,128)(2,1)S(1)} %constant_dynamic-update-slice_fusion.refs_4_), channel_id=1, source_target_pairs={{0,8},{1,9},{2,10},{3,11},{4,0},{5,1},{6,2},{7,3},{8,12},{9,13},{1... | collective-permute-start | bytes 1572872 | tf_op jit(solution)/shard_map/ppermute | solution.py:340
  27.9 21.7 %collective-permute-start.6 = (bf16[256,1024]{1,0:T(8,128)(2,1)}, bf16[256,1024]{1,0:T(8,128)(2,1)S(1)}, u32[]{:S(2)}, u32[]{:S(2)}) collective-permute-start(bf16[256,1024]{1,0:T(8,128)(2,1)} %collective-permute-done.2.refs_6_), channel_id=1, source_target_pairs={{0,8},{1,9},{2,10},{3,11},{4,0},{5,1},{6,2},{7,3},{8,12},{9,13},{1... | collective-permute-start | bytes 1572872 | tf_op jit(solution)/shard_map/ppermute | solution.py:340
  28.6 21.0 %collective-permute-start.8 = (bf16[256,1024]{1,0:T(8,128)(2,1)}, bf16[256,1024]{1,0:T(8,128)(2,1)S(1)}, u32[]{:S(2)}, u32[]{:S(2)}) collective-permute-start(bf16[256,1024]{1,0:T(8,128)(2,1)} %constant_dynamic-slice_fusion.refs_4_), channel_id=1, source_target_pairs={{0,1},{1,0},{2,3},{3,2},{4,5},{5,4},{6,7},{7,6},{8,9},{9,8},{10,11... | collective-permute-start | bytes 1572872 | tf_op jit(solution)/shard_map/ppermute | solution.py:340
  40.3 9.3 %collective-permute-start.9 = (bf16[256,1024]{1,0:T(8,128)(2,1)}, bf16[256,1024]{1,0:T(8,128)(2,1)S(1)}, u32[]{:S(2)}, u32[]{:S(2)}) collective-permute-start(bf16[256,1024]{1,0:T(8,128)(2,1)} %collective-permute-done.2.refs_6_), channel_id=1, source_target_pairs={{0,1},{1,0},{2,3},{3,2},{4,5},{5,4},{6,7},{7,6},{8,9},{9,8},{10,11... | collective-permute-start | bytes 1572872 | tf_op jit(solution)/shard_map/ppermute | solution.py:340
  49.7 26.2 %collective-permute-start.10 = (bf16[272,2048]{1,0:T(8,128)(2,1)}, bf16[272,2048]{1,0:T(8,128)(2,1)S(1)}, u32[]{:S(2)}, u32[]{:S(2)}) collective-permute-start(bf16[272,2048]{1,0:T(8,128)(2,1)} %get-tuple-element.86), channel_id=1, source_target_pairs={{0,18},{1,19},{2,16},{3,17},{4,22},{5,23},{6,20},{7,21},{8,26},{9,... | collective-permute-start | bytes 3342344 | tf_op jit(solution)/shard_map/ppermute | solution.py:340
  52.2 15.7 %collective-permute-start.11 = (bf16[256,1024]{1,0:T(8,128)(2,1)S(1)}, bf16[256,1024]{1,0:T(8,128)(2,1)}, u32[]{:S(2)}, u32[]{:S(2)}) collective-permute-start(bf16[256,1024]{1,0:T(8,128)(2,1)S(1)} %collective-permute-done.6.refs_8_), channel_id=1, source_target_pairs={{0,8},{1,9},{2,10},{3,11},{4,0},{5,1},{6,2},{7,3},{8,12},{9,13},{1... | collective-permute-start | bytes 1572872 | tf_op jit(solution)/shard_map/ppermute | solution.py:340
  55.4 20.3 %collective-permute-start.13 = (bf16[256,1024]{1,0:T(8,128)(2,1)S(1)}, bf16[256,1024]{1,0:T(8,128)(2,1)S(1)}, u32[]{:S(2)}, u32[]{:S(2)}) collective-permute-start(bf16[256,1024]{1,0:T(8,128)(2,1)S(1)} %collective-permute-done.6.refs_8_), channel_id=1, source_target_pairs={{0,1},{1,0},{2,3},{3,2},{4,5},{5,4},{6,7},{7,6},{8,9},{9,8},{10,11... | collective-permute-start | bytes 1572872 | tf_op jit(solution)/shard_map/ppermute | solution.py:340
  55.5 20.3 %collective-permute-start.12 = (bf16[128,2048]{1,0:T(8,128)(2,1)S(1)}, bf16[128,2048]{1,0:T(8,128)(2,1)S(1)}, u32[]{:S(2)}, u32[]{:S(2)}) collective-permute-start(bf16[128,2048]{1,0:T(8,128)(2,1)S(1)} %collective-permute-done.7.refs_6_), channel_id=1, source_target_pairs={{0,8},{1,9},{2,10},{3,11},{4,0},{5,1},{6,2},{7,3},{8,12},{9,13},{1... | collective-permute-start | bytes 1572872 | tf_op jit(solution)/shard_map/ppermute | solution.py:340
  55.5 20.3 %collective-permute-start.14 = (bf16[128,2048]{1,0:T(8,128)(2,1)S(1)}, bf16[128,2048]{1,0:T(8,128)(2,1)S(1)}, u32[]{:S(2)}, u32[]{:S(2)}) collective-permute-start(bf16[128,2048]{1,0:T(8,128)(2,1)S(1)} %constant_dynamic-update-slice_fusion.refs_4_), channel_id=1, source_target_pairs={{0,1},{1,0},{2,3},{3,2},{4,5},{5,4},{6,7},{7,6},{8,9},{9,8},{10,11... | collective-permute-start | bytes 1572872 | tf_op jit(solution)/shard_map/ppermute | solution.py:340
  81.0 15.3 %collective-permute-start.17 = (bf16[128,2048]{1,0:T(8,128)(2,1)S(1)}, bf16[128,2048]{1,0:T(8,128)(2,1)}, u32[]{:S(2)}, u32[]{:S(2)}) collective-permute-start(bf16[128,2048]{1,0:T(8,128)(2,1)S(1)} %copy-done.19), channel_id=1, source_target_pairs={{0,8},{1,9},{2,10},{3,11},{4,0},{5,1},{6,2},{7,3},{8,12},{9,13},{1... | collective-permute-start | bytes 1572872 | tf_op jit(solution)/shard_map/ppermute | solution.py:340
  96.3 9.1 %collective-permute-start.32 = (f32[16,1024]{1,0:T(8,128)}, f32[16,1024]{1,0:T(8,128)}, u32[]{:S(2)}, u32[]{:S(2)}) collective-permute-start(f32[16,1024]{1,0:T(8,128)} %get-tuple-element.145), channel_id=1, source_target_pairs={{0,16},{1,17},{2,18},{3,19},{4,20},{5,21},{6,22},{7,23},{8,24},{9,... | collective-permute-start | bytes 196616 | tf_op jit(solution)/shard_map/ppermute | solution.py:340
  96.8 9.0 %collective-permute-start.33 = (f32[16,1024]{1,0:T(8,128)}, f32[16,1024]{1,0:T(8,128)}, u32[]{:S(2)}, u32[]{:S(2)}) collective-permute-start(f32[16,1024]{1,0:T(8,128)} %get-tuple-element.146), channel_id=1, source_target_pairs={{0,2},{1,3},{2,0},{3,1},{4,6},{5,7},{6,4},{7,5},{8,10},{9,11},{10,... | collective-permute-start | bytes 196616 | tf_op jit(solution)/shard_map/ppermute | solution.py:340
  97.4 9.0 %collective-permute-start.34 = (f32[16,1024]{1,0:T(8,128)}, f32[16,1024]{1,0:T(8,128)}, u32[]{:S(2)}, u32[]{:S(2)}) collective-permute-start(f32[16,1024]{1,0:T(8,128)} %get-tuple-element.147), channel_id=1, source_target_pairs={{0,18},{1,19},{2,16},{3,17},{4,22},{5,23},{6,20},{7,21},{8,26},{9,... | collective-permute-start | bytes 196616 | tf_op jit(solution)/shard_map/ppermute | solution.py:340
  101.8 8.4 %collective-permute-start.18 = (bf16[128,1024]{1,0:T(8,128)(2,1)}, bf16[128,1024]{1,0:T(8,128)(2,1)}, u32[]{:S(2)}, u32[]{:S(2)}) collective-permute-start(bf16[128,1024]{1,0:T(8,128)(2,1)} %copy-done.3), channel_id=1, source_target_pairs={{0,8},{1,9},{2,10},{3,11},{4,0},{5,1},{6,2},{7,3},{8,12},{9,13},{1... | collective-permute-start | bytes 786440 | tf_op jit(solution)/shard_map/ppermute | solution.py:340
  105.8 18.5 %collective-permute-start.24 = (bf16[256,1024]{1,0:T(8,128)(2,1)}, bf16[256,1024]{1,0:T(8,128)(2,1)}, u32[]{:S(2)}, u32[]{:S(2)}) collective-permute-start(bf16[256,1024]{1,0:T(8,128)(2,1)} %get-tuple-element.139), channel_id=1, source_target_pairs={{0,16},{1,17},{2,18},{3,19},{4,20},{5,21},{6,22},{7,23},{8,24},{9,... | collective-permute-start | bytes 1572872 | tf_op jit(solution)/shard_map/ppermute | solution.py:340
  106.4 25.3 %collective-permute-start.25 = (bf16[256,1024]{1,0:T(8,128)(2,1)}, bf16[256,1024]{1,0:T(8,128)(2,1)}, u32[]{:S(2)}, u32[]{:S(2)}) collective-permute-start(bf16[256,1024]{1,0:T(8,128)(2,1)} %get-tuple-element.140), channel_id=1, source_target_pairs={{0,2},{1,3},{2,0},{3,1},{4,6},{5,7},{6,4},{7,5},{8,10},{9,11},{10,... | collective-permute-start | bytes 1572872 | tf_op jit(solution)/shard_map/ppermute | solution.py:340
  110.3 21.5 %collective-permute-start.26 = (bf16[256,1024]{1,0:T(8,128)(2,1)}, bf16[256,1024]{1,0:T(8,128)(2,1)}, u32[]{:S(2)}, u32[]{:S(2)}) collective-permute-start(bf16[256,1024]{1,0:T(8,128)(2,1)} %get-tuple-element.117._), channel_id=1, source_target_pairs={{0,18},{1,19},{2,16},{3,17},{4,22},{5,23},{6,20},{7,21},{8,26},{9,... | collective-permute-start | bytes 1572872 | tf_op jit(solution)/shard_map/ppermute | solution.py:340
  112.2 21.6 %collective-permute-start.30 = (bf16[128,1024]{1,0:T(8,128)(2,1)}, bf16[128,1024]{1,0:T(8,128)(2,1)}, u32[]{:S(2)}, u32[]{:S(2)}) collective-permute-start(bf16[128,1024]{1,0:T(8,128)(2,1)} %collective-permute-done.18.refs_14_), channel_id=1, source_target_pairs={{0,8},{1,9},{2,10},{3,11},{4,0},{5,1},{6,2},{7,3},{8,12},{9,13},{1... | collective-permute-start | bytes 786440 | tf_op jit(solution)/shard_map/ppermute | solution.py:340
  123.0 9.3 %collective-permute-start.21 = (f32[64,128]{1,0:T(8,128)}, f32[64,128]{1,0:T(8,128)S(1)}, u32[]{:S(2)}, u32[]{:S(2)}) collective-permute-start(f32[64,128]{1,0:T(8,128)} %get-tuple-element.135), channel_id=1, source_target_pairs={{0,16},{1,17},{2,18},{3,19},{4,20},{5,21},{6,22},{7,23},{8,24},{9,... | collective-permute-start | bytes 98312 | tf_op jit(solution)/shard_map/ppermute | solution.py:340
  (37 other events, 451.1 us)

commit v3 on v2

--- a/solution.py
+++ b/solution.py
@@ -88,7 +88,7 @@
     return list(outs[:4]), list(outs[4:])
 
 
-def base_products(blocks, parts, spots, rows):
+def base_products(blocks, parts, spots):
     kk, out_width = parts[0].shape
     tall = blocks[0].shape[0]
     n = len(parts)
@@ -98,16 +98,13 @@
         for i in range(n):
             quarter = lax.dynamic_update_slice_in_dim(quarter, parts[i], spots[i] * kk, axis=0)
         products = [jnp.dot(b, quarter, preferred_element_type=jnp.float32) for b in blocks]
-        return (
-            [p[:rows].astype(kind) for p, kind in zip(products, kinds)],
-            [p[rows:] for p in products],
-        )
+        return [p.astype(kind) for p, kind in zip(products, kinds)]
     count = len(blocks)
     cut = 256
 
     def kernel(spot, *refs):
         xs, weights = refs[:count], refs[count : count + n]
-        outs, rest = refs[count + n : 2 * count + n], refs[2 * count + n : -2]
+        outs = refs[count + n : 2 * count + n]
         left, right = refs[-2:]
 
         @pl.when(pl.program_id(0) == 0)
@@ -119,8 +116,7 @@
             right[pl.ds(pl.multiple_of(spot[i] * kk, kk), kk), :] = weights[i][...]
         total = jnp.dot(left[...], right[...], preferred_element_type=jnp.float32)
         for m in range(count):
-            outs[m][...] = total[m * tall : m * tall + rows].astype(kinds[m])
-            rest[m][...] = total[m * tall + rows : (m + 1) * tall]
+            outs[m][...] = total[m * tall : (m + 1) * tall].astype(kinds[m])
 
     outs = pl.pallas_call(
         kernel,
@@ -129,20 +125,18 @@
             grid=(out_width // cut,),
             in_specs=[pl.BlockSpec(blocks[0].shape, lambda j, s: (0, 0))] * count
             + [pl.BlockSpec((kk, cut), lambda j, s: (0, j))] * n,
-            out_specs=[pl.BlockSpec((rows, cut), lambda j, s: (0, j))] * count
-            + [pl.BlockSpec((tall - rows, cut), lambda j, s: (0, j))] * count,
+            out_specs=[pl.BlockSpec((tall, cut), lambda j, s: (0, j))] * count,
             scratch_shapes=[
                 pltpu.VMEM((count * tall, n * kk), jnp.bfloat16),
                 pltpu.VMEM((n * kk, cut), jnp.bfloat16),
             ],
         ),
-        out_shape=[jax.ShapeDtypeStruct((rows, out_width), kind) for kind in kinds]
-        + [jax.ShapeDtypeStruct((tall - rows, out_width), jnp.float32)] * count,
-        compiler_params=pltpu.CompilerParams(vmem_limit_bytes=VMEM),
+        out_shape=[jax.ShapeDtypeStruct((tall, out_width), kind) for kind in kinds],
+        compiler_params=pltpu.CompilerParams(vmem_limit_bytes=28 * 2**20),
         cost_estimate=cost(2 * count * tall * n * kk * out_width, (count * tall + out_width) * 2 * n * kk),
         name="base_products",
     )(spots, *blocks, *parts)
-    return list(outs[:count]), list(outs[count:])
+    return list(outs)
 
 
 def lowered_products(blocks, pieces, columns, rows, first, rank, after):
@@ -207,7 +201,7 @@
         out_specs=[pl.BlockSpec((tall, 128), whole)] * count,
         out_shape=[jax.ShapeDtypeStruct((tall, 128), jnp.float32)] * count,
         scratch_shapes=[pltpu.VMEM((count * rows, wide), jnp.bfloat16)],
-        compiler_params=pltpu.CompilerParams(vmem_limit_bytes=VMEM),
+        compiler_params=pltpu.CompilerParams(vmem_limit_bytes=32 * 2**20),
         cost_estimate=cost(2 * count * rows * wide * total_ranks, (count * rows + total_ranks) * 2 * wide),
         name="lowered_products",
     )(after, *blocks, *pieces, columns)
@@ -361,8 +355,7 @@
     bases = [lax.dynamic_slice_in_dim(base_weight, r * kk, kk, axis=0)]
     bases.append(send(bases[0], ring))
     up = adapter_up.reshape(ranks, out_width)
-    ups = [paired(up, send(up, flips[reps]) if sides == 2 else None)]
-    ups.append(send(ups[0], ring))
+    up_far = send(up, flips[reps]) if sides == 2 else None
     messages, downs = split_columns(
         prefill_rows,
         decode_rows,
@@ -379,59 +372,11 @@
     )
     near = [send(messages[m], flips[m]) for m in (1, 2)]
     down_far = send(downs[1], flips[reps]) if sides == 2 else None
-    bases, ups, down_far = phase(bases, ups, down_far)
-
-    downs = [paired(downs[0], down_far)]
-    bases.append(send(bases[-1], ring))
-    downs.append(send(downs[-1], ring))
-    base_parts = both(bases[0]) + both(bases[1])
-    near, bases, downs, base_parts, far = phase(near, bases, downs, base_parts, messages[3])
-
-    far = send(far, flips[3])
-    while len(bases) < planes:
-        bases.append(send(bases[-1], ring))
-    downs.append(send(downs[-1], ring))
-    for held in bases[2:-1]:
-        base_parts = base_parts + both(held)
-    pieces = both(downs[0]) + both(downs[1])
-    near, far, bases, downs, base_parts, pieces = phase(
-        near, far, bases, downs, base_parts, pieces
-    )
-
-    blocks = [messages[0], *near, far]
-    base_parts = base_parts + both(bases[-1])
-    partials, fresh = base_products(blocks, base_parts, spots, rows)
-    while len(downs) < planes:
-        downs.append(send(downs[-1], ring))
-    partials, fresh, downs, pieces = phase(partials, fresh, downs, pieces)
-
-    fresh = [fresh[0]] + [send(fresh[m], flips[m]) for m in (1, 2, 3)]
-    recent_output = sum(fresh[1:], fresh[0])[:dec].astype(jnp.bfloat16)
-    base = [partials[0]] + [send(partials[m], flips[m]) for m in (1, 2, 3)]
-    while len(ups) < planes - 1:
-        ups.append(send(ups[-1], ring))
-    pieces = pieces + sum([both(d) for d in downs[2:]], [])
-    ups, pieces = phase(ups, pieces)
-    ups.append(send(ups[-1], ring))
-    up_parts = sum([both(u) for u in ups], [])
-
-    group = jnp.arange(slots_all, dtype=jnp.int32)
-    inner = group % local_slots
-    side = (group // local_slots) % sides
-    core = (group // (local_slots * sides)) % 2
-    step = group // (local_slots * sides * 2)
-    column_slot = ((plane_of(step) * sides + (y ^ side)) * 2 + (c ^ core)) * local_slots + inner
-    columns = jnp.repeat(column_slot, rank).astype(jnp.float32)[None, :]
-    first = rows + dec
-    packed = lowered_products(blocks, pieces, columns, rows, first, rank, partials[3])
-    packed = [packed[0]] + [send(packed[m], flips[m]) for m in (1, 2, 3)]
-    projected = finish(packed, messages[0], up_parts, columns, base, rows, first, rank)
+    bases, up_far = phase(bases, up_far)
 
     kv_heads = half_width // HEAD_SIZE
     query_groups = queries.shape[1] // half_width
     positions = key_store_cache.shape[1]
-    newest_keys = recent_output[:, :half_width].reshape(dec, kv_heads, HEAD_SIZE)
-    newest_values = recent_output[:, half_width:].reshape(dec, kv_heads, HEAD_SIZE)
     query_head_rows = queries.reshape(dec, kv_heads, query_groups, HEAD_SIZE)
     stored_keys = key_store_cache.reshape(dec, positions, kv_heads, HEAD_SIZE)
     stored_values = value_store_cache.reshape(dec, positions, kv_heads, HEAD_SIZE)
@@ -442,27 +387,104 @@
         )
         * scale
     )
+    live = jnp.arange(positions, dtype=jnp.int32)[None, :] < context_len[:, None]
+    scores = jnp.where(live[:, None, None, :], scores, -jnp.inf)
+    cached_top = jnp.max(scores, axis=-1)
+    cached_weight = jnp.exp(scores - cached_top[..., None])
+    cached_total = jnp.sum(cached_weight, axis=-1)
+    cached_mix = jnp.einsum(
+        "bkgc,bckd->bkgd",
+        cached_weight.astype(jnp.bfloat16),
+        stored_values,
+        preferred_element_type=jnp.float32,
+    )
+
+    group = jnp.arange(slots_all, dtype=jnp.int32)
+    inner = group % local_slots
+    side = (group // local_slots) % sides
+    core = (group // (local_slots * sides)) % 2
+    step = group // (local_slots * sides * 2)
+    column_slot = ((plane_of(step) * sides + (y ^ side)) * 2 + (c ^ core)) * local_slots + inner
+    columns = jnp.repeat(column_slot, rank).astype(jnp.float32)[None, :]
+
+    downs = [paired(downs[0], down_far)]
+    bases.append(send(bases[-1], ring))
+    downs.append(send(downs[-1], ring))
+    ups = [paired(up, up_far)]
+    base_parts = both(bases[0]) + both(bases[1])
+    near, bases, downs, ups, base_parts, far, cached_top, cached_total, cached_mix, columns, spots = phase(
+        near,
+        bases,
+        downs,
+        ups,
+        base_parts,
+        messages[3],
+        cached_top,
+        cached_total,
+        cached_mix,
+        columns,
+        spots,
+    )
+
+    far = send(far, flips[3])
+    while len(bases) < planes:
+        bases.append(send(bases[-1], ring))
+    downs.append(send(downs[-1], ring))
+    ups.append(send(ups[-1], ring))
+    for held in bases[2:-1]:
+        base_parts = base_parts + both(held)
+    pieces = both(downs[0]) + both(downs[1])
+    up_parts = both(ups[0])
+    near, far, bases, downs, ups, base_parts, pieces, up_parts = phase(
+        near, far, bases, downs, ups, base_parts, pieces, up_parts
+    )
+
+    blocks = [messages[0], *near, far]
+    base_parts = base_parts + both(bases[-1])
+    partials = base_products(blocks, base_parts, spots)
+    while len(downs) < planes:
+        downs.append(send(downs[-1], ring))
+    pieces = pieces + sum([both(d) for d in downs[2:-1]], [])
+    partials, downs, pieces, ups = phase(partials, downs, pieces, ups)
+
+    base = [partials[0]] + [send(partials[m], flips[m]) for m in (1, 2)]
+    while len(ups) < planes - 1:
+        ups.append(send(ups[-1], ring))
+    pieces = pieces + both(downs[-1])
+    up_parts = up_parts + both(ups[1])
+    base, ups, up_parts, pieces, last = phase(base, ups, up_parts, pieces, partials[3])
+
+    base.append(send(last, flips[3]))
+    ups.append(send(ups[-1], ring))
+    up_parts = up_parts + sum([both(u) for u in ups[2:-1]], [])
+
+    first = rows + dec
+    packed = lowered_products(blocks, pieces, columns, rows, first, rank, last)
+    packed, ups, up_parts = phase(packed, ups, up_parts)
+    packed = [packed[0]] + [send(packed[m], flips[m]) for m in (1, 2, 3)]
+    up_parts = up_parts + both(ups[-1])
+
+    recent_output = sum(b[rows : rows + dec].astype(jnp.float32) for b in base).astype(jnp.bfloat16)
+    newest_keys = recent_output[:, :half_width].reshape(dec, kv_heads, HEAD_SIZE)
+    newest_values = recent_output[:, half_width:].reshape(dec, kv_heads, HEAD_SIZE)
     own_score = (
-        jnp.einsum(
-            "bkgd,bkd->bkg", query_head_rows, newest_keys, preferred_element_type=jnp.float32
+        jnp.sum(
+            query_head_rows.astype(jnp.float32) * newest_keys.astype(jnp.float32)[:, :, None, :],
+            axis=-1,
         )
         * scale
     )
-    live = jnp.arange(positions, dtype=jnp.int32)[None, :] < context_len[:, None]
-    scores = jnp.where(live[:, None, None, :], scores, -jnp.inf)
-    top = jnp.maximum(jnp.max(scores, axis=-1), own_score)
-    cached_weight = jnp.exp(scores - top[..., None])
+    top = jnp.maximum(cached_top, own_score)
+    kept = jnp.exp(cached_top - top)
     own_weight = jnp.exp(own_score - top)
-    total = jnp.sum(cached_weight, axis=-1) + own_weight
-    probs = (cached_weight / total[..., None]).astype(jnp.bfloat16)
-    probs_own = (own_weight / total).astype(jnp.bfloat16)
-    mixed = jnp.einsum("bkgc,bckd->bkgd", probs, stored_values, preferred_element_type=jnp.float32)
+    total = kept * cached_total + own_weight
     mixed = (
-        mixed
-        + probs_own.astype(jnp.float32)[..., None]
-        * newest_values.astype(jnp.float32)[:, :, None, :]
-    )
-    attended = mixed.reshape(dec, query_groups * kv_heads * HEAD_SIZE).astype(jnp.bfloat16)
+        kept[..., None] * cached_mix
+        + own_weight[..., None] * newest_values.astype(jnp.float32)[:, :, None, :]
+    ) / total[..., None]
+    attended = mixed.reshape(dec, query_groups * half_width).astype(jnp.bfloat16)
+
+    projected = finish(packed, messages[0], up_parts, columns, base, rows, first, rank)
     return (projected, attended)
 
 

time: 145 us -> 133 us (0.917)
  local copies, waits for them, and re-layouts: 11.7 us -> 6.13 us
  waiting for transfers between devices: 50.3 us -> 54.4 us
  Pallas kernels: 30.2 us -> 26.6 us
  matrix products: 5.76 us -> 2.66 us
  other arithmetic: 4.3 us -> 2.25 us
  starting transfers between devices: 41.4 us -> 39.6 us
    unnamed x54 -> x44, local copies, waits for them, and re-layouts: 7.54 us -> 3.28 us
    ppermute x35 -> x32, waiting for transfers between devices: 50.3 us -> 54.4 us  [send(): return lax.ppermute(value, BOTH, pairs)]
    dot_general x2 -> x1, matrix products: 3.59 us -> 1.39 us  [body(): jnp.einsum('bkgc,bckd->bkgd', cached_weight.astype(jnp.bfloat16), stored_...]
    pallas_call x1, Pallas kernels: 8.75 us -> 6.58 us  [lowered_products(): pl.pallas_call(kernel, grid=(1,), in_specs=[pl.BlockSpec(memory_space=pl....]
    ppermute x35 -> x32, starting transfers between devices: 41.4 us -> 39.6 us  [send(): return lax.ppermute(value, BOTH, pairs)]
    pallas_call x1, Pallas kernels: 10.4 us -> 8.83 us  [base_products(): pl.pallas_call(kernel, grid_spec=pltpu.PrefetchScalarGridSpec(num_scalar_...]
  transfers between devices with their start and end apart: 35 -> 32, of which waited for: 9 -> 11; matrix products, arithmetic and copies ran while one was open for 10% -> 8% of each run, Pallas kernels for 17% -> 16%
where the time goes in v3:
time: 133 us
  waiting for transfers between devices  54.4 us (41%)
  starting transfers between devices  39.6 us (30%)
  Pallas kernels  26.6 us (20%)
  local copies, waits for them, and re-layouts  6.13 us (5%)
  matrix products  2.66 us (2%)
  other arithmetic  2.25 us (2%)
    ppermute x32, waiting for transfers between devices, send(): return lax.ppermute(value, BOTH, pairs)  54.4 us
    ppermute x32, starting transfers between devices, send(): return lax.ppermute(value, BOTH, pairs)  39.6 us
    pallas_call x1, Pallas kernels, base_products(): pl.pallas_call(kernel, grid_spec=pltpu.PrefetchScalarGridSpec(num_scalar_...  8.83 us
    pallas_call x1, Pallas kernels, lowered_products(): pl.pallas_call(kernel, grid=(1,), in_specs=[pl.BlockSpec(memory_space=pl....  6.58 us
    pallas_call x1, Pallas kernels, split_columns(): pl.pallas_call(kernel, grid_spec=pltpu.PrefetchScalarGridSpec(num_scalar_...  6.1 us
    pallas_call x1, Pallas kernels, finish(): pl.pallas_call(kernel, grid=(out_width // cut,), in_specs=[pl.BlockSpec(p...  5.08 us
    unnamed x44, local copies, waits for them, and re-layouts  3.28 us
  transfers between devices with their start and end apart: 32, of which 11 were waited for; matrix products, arithmetic and copies ran while one was open for 8% of the time, Pallas kernels for 16%

profile of v3, /device:TPU:0, one launch (start us, length us, event | category | flops | bytes accessed | tf_op | source)
XLA Modules:
  0.0 132.6 jit_solution(2794003480439506840)
XLA Ops:
  0.6 3.0 %collective-permute-start.3 = (bf16[64,1024]{1,0:T(8,128)(2,1)}, bf16[64,1024]{1,0:T(8,128)(2,1)}, u32[]{:S(2)}, u32[]{:S(2)}) collective-permute-start(bf16[64,1024]{1,0:T(8,128)(2,1)} %bitcast.45), channel_id=1, source_target_pairs={{0,2},{1,3},{2,0},{3,1},{4,6},{5,7},{6,4},{7,5},{8,10},{9,11},{10,... | collective-permute-start | bytes 393224 | tf_op jit(solution)/shard_map/ppermute | solution.py:334
  3.7 1.9 %constant_dynamic-slice_fusion.refs_4_ = bf16[256,1024]{1,0:T(8,128)(2,1)} fusion(bf16[512,1024]{1,0:T(8,128)(2,1)} %param.19, s32[]{:T(128)S(6)} %select_n.88), kind=kLoop, calls=%fused_computation.81 | loop fusion | bytes 1048580 | tf_op jit(solution)/shard_map/dynamic_slice | solution.py:355
  5.6 2.6 %collective-permute-start.2 = (bf16[256,1024]{1,0:T(8,128)(2,1)}, bf16[256,1024]{1,0:T(8,128)(2,1)}, u32[]{:S(2)}, u32[]{:S(2)}) collective-permute-start(bf16[256,1024]{1,0:T(8,128)(2,1)} %constant_dynamic-slice_fusion.refs_4_), channel_id=1, source_target_pairs={{0,8},{1,9},{2,10},{3,11},{4,0},{5,1},{6,2},{7,3},{8,12},{9,13},{1... | collective-permute-start | bytes 1572872 | tf_op jit(solution)/shard_map/ppermute | solution.py:334
  8.8 6.1 %split_columns.1 = (bf16[272,2048]{1,0:T(8,128)(2,1)}, bf16[272,2048]{1,0:T(8,128)(2,1)}, bf16[272,2048]{1,0:T(8,128)(2,1)}, bf16[272,2048]{1,0:T(8,128)(2,1)}, ...) custom-call(s32[2]{0:T(128)} %pad_add_fusion.here, s32[32]{0:T(128)} %own.1, bf16[256,8192]{1,0:T(8,128)(2,1)} %pre.1, ...), custom_call_target="tpu_custom_call" | custom-call | bytes 10485760 | tf_op jit(solution)/shard_map/split_columns/pallas_call | solution.py:73
  18.5 1.7 %constant_dynamic-update-slice_fusion.1 = bf16[128,2048]{1,0:T(8,128)(2,1)} fusion(bf16[64,2048]{1,0:T(8,128)(2,1)} %get-tuple-element.97), kind=kLoop, calls=%fused_computation.30 | loop fusion | bytes 524288
  20.2 4.1 %collective-permute-done.5 = bf16[64,2048]{1,0:T(8,128)(2,1)S(1)} collective-permute-done((bf16[64,2048]{1,0:T(8,128)(2,1)}, bf16[64,2048]{1,0:T(8,128)(2,1)S(1)}, u32[]{:S(2)}, u32[]{:S(2)}) %collective-permute-start.5) | collective-permute-done | bytes 262176 | tf_op jit(solution)/shard_map/ppermute | solution.py:334
  28.9 11.0 %collective-permute-done.6.refs_6_ = bf16[128,2048]{1,0:T(8,128)(2,1)} collective-permute-done((bf16[128,2048]{1,0:T(8,128)(2,1)}, bf16[128,2048]{1,0:T(8,128)(2,1)}, u32[]{:S(2)}, u32[]{:S(2)}) %collective-permute-start.6) | collective-permute-done | bytes 524320 | tf_op jit(solution)/shard_map/ppermute | solution.py:334
  42.2 4.8 %collective-permute-done.4.refs_8_ = bf16[256,1024]{1,0:T(8,128)(2,1)S(1)} collective-permute-done((bf16[256,1024]{1,0:T(8,128)(2,1)}, bf16[256,1024]{1,0:T(8,128)(2,1)S(1)}, u32[]{:S(2)}, u32[]{:S(2)}) %collective-permute-start.4) | collective-permute-done | bytes 524320 | tf_op jit(solution)/shard_map/ppermute | solution.py:334
  49.1 2.5 %collective-permute-start.12 = (bf16[128,1024]{1,0:T(8,128)(2,1)S(1)}, bf16[128,1024]{1,0:T(8,128)(2,1)S(1)}, u32[]{:S(2)}, u32[]{:S(2)}) collective-permute-start(bf16[128,1024]{1,0:T(8,128)(2,1)S(1)} %pad_maximum_fusion.refs_10_), channel_id=1, source_target_pairs={{0,8},{1,9},{2,10},{3,11},{4,0},{5,1},{6,2},{7,3},{8,12},{9,13},{1... | collective-permute-start | bytes 786440 | tf_op jit(solution)/shard_map/ppermute | solution.py:334
  53.0 5.3 %collective-permute-done.12.refs_12_ = bf16[128,1024]{1,0:T(8,128)(2,1)S(1)} collective-permute-done((bf16[128,1024]{1,0:T(8,128)(2,1)S(1)}, bf16[128,1024]{1,0:T(8,128)(2,1)S(1)}, u32[]{:S(2)}, u32[]{:S(2)}) %collective-permute-start.12) | collective-permute-done | bytes 262176 | tf_op jit(solution)/shard_map/ppermute | solution.py:334
  58.3 3.4 %collective-permute-start.11 = (bf16[128,2048]{1,0:T(8,128)(2,1)}, bf16[128,2048]{1,0:T(8,128)(2,1)S(1)}, u32[]{:S(2)}, u32[]{:S(2)}) collective-permute-start(bf16[128,2048]{1,0:T(8,128)(2,1)} %collective-permute-done.6.refs_6_), channel_id=1, source_target_pairs={{0,8},{1,9},{2,10},{3,11},{4,0},{5,1},{6,2},{7,3},{8,12},{9,13},{1... | collective-permute-start | bytes 1572872 | tf_op jit(solution)/shard_map/ppermute | solution.py:334
  61.7 7.8 %collective-permute-done.10.refs_10_ = bf16[256,1024]{1,0:T(8,128)(2,1)S(1)} collective-permute-done((bf16[256,1024]{1,0:T(8,128)(2,1)S(1)}, bf16[256,1024]{1,0:T(8,128)(2,1)S(1)}, u32[]{:S(2)}, u32[]{:S(2)}) %collective-permute-start.10) | collective-permute-done | bytes 524320 | tf_op jit(solution)/shard_map/ppermute | solution.py:334
  69.5 10.4 %collective-permute-done.11.refs_8_ = bf16[128,2048]{1,0:T(8,128)(2,1)S(1)} collective-permute-done((bf16[128,2048]{1,0:T(8,128)(2,1)}, bf16[128,2048]{1,0:T(8,128)(2,1)S(1)}, u32[]{:S(2)}, u32[]{:S(2)}) %collective-permute-start.11) | collective-permute-done | bytes 524320 | tf_op jit(solution)/shard_map/ppermute | solution.py:334
  80.4 3.3 %collective-permute-start.18 = (bf16[128,2048]{1,0:T(8,128)(2,1)S(1)}, bf16[128,2048]{1,0:T(8,128)(2,1)S(1)}, u32[]{:S(2)}, u32[]{:S(2)}) collective-permute-start(bf16[128,2048]{1,0:T(8,128)(2,1)S(1)} %collective-permute-done.11.refs_8_), channel_id=1, source_target_pairs={{0,8},{1,9},{2,10},{3,11},{4,0},{5,1},{6,2},{7,3},{8,12},{9,13},{1... | collective-permute-start | bytes 1572872 | tf_op jit(solution)/shard_map/ppermute | solution.py:334
  83.7 8.8 %base_products.1 = (f32[272,1024]{1,0:T(8,128)S(1)}, bf16[272,1024]{1,0:T(8,128)(2,1)S(1)}, bf16[272,1024]{1,0:T(8,128)(2,1)S(1)}, bf16[272,1024]{1,0:T(8,128)(2,1)S(1)}) custom-call(s32[8]{0:T(128)S(1)} %fusion.24.spot, bf16[272,2048]{1,0:T(8,128)(2,1)S(1)} %copy-done.2, bf16[272,2048]{1,0:T(8,128)(2,1)} %collective-permute-done.refs_1_, ...), custom_call_target="tpu_custom_call" | custom-call | flops 4563402752 | bytes 8650752 | tf_op jit(solution)/shard_map/base_products/pallas_call | solution.py:121
  92.5 2.5 %collective-permute-done.18.refs_10_ = bf16[128,2048]{1,0:T(8,128)(2,1)S(1)} collective-permute-done((bf16[128,2048]{1,0:T(8,128)(2,1)S(1)}, bf16[128,2048]{1,0:T(8,128)(2,1)S(1)}, u32[]{:S(2)}, u32[]{:S(2)}) %collective-permute-start.18) | collective-permute-done | bytes 524320 | tf_op jit(solution)/shard_map/ppermute | solution.py:334
  97.6 3.4 %collective-permute-start.22 = (bf16[128,1024]{1,0:T(8,128)(2,1)S(1)}, bf16[128,1024]{1,0:T(8,128)(2,1)S(1)}, u32[]{:S(2)}, u32[]{:S(2)}) collective-permute-start(bf16[128,1024]{1,0:T(8,128)(2,1)S(1)} %collective-permute-done.12.refs_12_), channel_id=1, source_target_pairs={{0,8},{1,9},{2,10},{3,11},{4,0},{5,1},{6,2},{7,3},{8,12},{9,13},{1... | collective-permute-start | bytes 786440 | tf_op jit(solution)/shard_map/ppermute | solution.py:334
  101.0 5.7 %collective-permute-done.22.refs_14_ = bf16[128,1024]{1,0:T(8,128)(2,1)S(1)} collective-permute-done((bf16[128,1024]{1,0:T(8,128)(2,1)S(1)}, bf16[128,1024]{1,0:T(8,128)(2,1)S(1)}, u32[]{:S(2)}, u32[]{:S(2)}) %collective-permute-start.22) | collective-permute-done | bytes 262176 | tf_op jit(solution)/shard_map/ppermute | solution.py:334
  106.7 2.0 %collective-permute-done.20.refs_7_ = bf16[272,1024]{1,0:T(8,128)(2,1)S(1)} collective-permute-done((bf16[272,1024]{1,0:T(8,128)(2,1)S(1)}, bf16[272,1024]{1,0:T(8,128)(2,1)S(1)}, u32[]{:S(2)}, u32[]{:S(2)}) %collective-permute-start.20) | collective-permute-done | bytes 557088 | tf_op jit(solution)/shard_map/ppermute | solution.py:334
  109.0 2.4 %collective-permute-start.30 = (bf16[272,1024]{1,0:T(8,128)(2,1)S(1)}, bf16[272,1024]{1,0:T(8,128)(2,1)S(1)}, u32[]{:S(2)}, u32[]{:S(2)}) collective-permute-start(bf16[272,1024]{1,0:T(8,128)(2,1)S(1)} %get-tuple-element.148._), channel_id=1, source_target_pairs={{0,18},{1,19},{2,16},{3,17},{4,22},{5,23},{6,20},{7,21},{8,26},{9,... | collective-permute-start | bytes 1671176 | tf_op jit(solution)/shard_map/ppermute | solution.py:334
  111.4 3.4 %collective-permute-start.25 = (bf16[128,1024]{1,0:T(8,128)(2,1)S(1)}, bf16[128,1024]{1,0:T(8,128)(2,1)}, u32[]{:S(2)}, u32[]{:S(2)}) collective-permute-start(bf16[128,1024]{1,0:T(8,128)(2,1)S(1)} %collective-permute-done.22.refs_14_), channel_id=1, source_target_pairs={{0,8},{1,9},{2,10},{3,11},{4,0},{5,1},{6,2},{7,3},{8,12},{9,13},{1... | collective-permute-start | bytes 786440 | tf_op jit(solution)/shard_map/ppermute | solution.py:334
  114.8 6.6 %lowered_products.1 = (f32[64,128]{1,0:T(8,128)S(1)}, f32[64,128]{1,0:T(8,128)S(1)}, f32[64,128]{1,0:T(8,128)S(1)}, f32[64,128]{1,0:T(8,128)S(1)}) custom-call(bf16[272,1024]{1,0:T(8,128)(2,1)S(1)} %get-tuple-element.148._, bf16[272,2048]{1,0:T(8,128)(2,1)S(1)} %copy-done.2, bf16[272,2048]{1,0:T(8,128)(2,1)} %collective-permute-done.refs_1_, ...), custom_call_target="tpu_custom_call" | custom-call | flops 4294967296 | bytes 8388608 | tf_op jit(solution)/shard_map/lowered_products/pallas_call | solution.py:194
  122.5 2.4 %collective-permute-start.29 = (f32[64,128]{1,0:T(8,128)S(1)}, f32[64,128]{1,0:T(8,128)}, u32[]{:S(2)}, u32[]{:S(2)}) collective-permute-start(f32[64,128]{1,0:T(8,128)S(1)} %get-tuple-element.170), channel_id=1, source_target_pairs={{0,18},{1,19},{2,16},{3,17},{4,22},{5,23},{6,20},{7,21},{8,26},{9,... | collective-permute-start | bytes 98312 | tf_op jit(solution)/shard_map/ppermute | solution.py:334
  127.5 5.1 %finish.1 = bf16[256,1024]{1,0:T(8,128)(2,1)} custom-call(f32[64,128]{1,0:T(8,128)} %copy-done.3, f32[64,128]{1,0:T(8,128)} %copy-done.18, f32[64,128]{1,0:T(8,128)} %collective-permute-done.28.refs_2_, f32[64,128]{1,0:T(8,128)} %collective-permute-done.29.refs_3_, bf16[272,2048]{1,0:T(8,128)(2,1)} %get-tuple-element.102.refs_0_.refs_4_, ...), custom_call_target="tpu_custom_call" | custom-call | flops 536870912 | bytes 5242880 | tf_op jit(solution)/shard_map/finish/pallas_call | solution.py:266
  (107 shorter events, 21.5 us)
Async XLA Ops:
  0.6 27.8 %collective-permute-start.3 = (bf16[64,1024]{1,0:T(8,128)(2,1)}, bf16[64,1024]{1,0:T(8,128)(2,1)}, u32[]{:S(2)}, u32[]{:S(2)}) collective-permute-start(bf16[64,1024]{1,0:T(8,128)(2,1)} %bitcast.45), channel_id=1, source_target_pairs={{0,2},{1,3},{2,0},{3,1},{4,6},{5,7},{6,4},{7,5},{8,10},{9,11},{10,... | collective-permute-start | bytes 393224 | tf_op jit(solution)/shard_map/ppermute | solution.py:334
  5.6 22.8 %collective-permute-start.2 = (bf16[256,1024]{1,0:T(8,128)(2,1)}, bf16[256,1024]{1,0:T(8,128)(2,1)}, u32[]{:S(2)}, u32[]{:S(2)}) collective-permute-start(bf16[256,1024]{1,0:T(8,128)(2,1)} %constant_dynamic-slice_fusion.refs_4_), channel_id=1, source_target_pairs={{0,8},{1,9},{2,10},{3,11},{4,0},{5,1},{6,2},{7,3},{8,12},{9,13},{1... | collective-permute-start | bytes 1572872 | tf_op jit(solution)/shard_map/ppermute | solution.py:334
  14.9 9.5 %collective-permute-start.5 = (bf16[64,2048]{1,0:T(8,128)(2,1)}, bf16[64,2048]{1,0:T(8,128)(2,1)S(1)}, u32[]{:S(2)}, u32[]{:S(2)}) collective-permute-start(bf16[64,2048]{1,0:T(8,128)(2,1)} %get-tuple-element.98), channel_id=1, source_target_pairs={{0,2},{1,3},{2,0},{3,1},{4,6},{5,7},{6,4},{7,5},{8,10},{9,11},{10,... | collective-permute-start | bytes 786440 | tf_op jit(solution)/shard_map/ppermute | solution.py:334
  15.7 31.4 %collective-permute-start = (bf16[272,2048]{1,0:T(8,128)(2,1)}, bf16[272,2048]{1,0:T(8,128)(2,1)}, u32[]{:S(2)}, u32[]{:S(2)}) collective-permute-start(bf16[272,2048]{1,0:T(8,128)(2,1)} %get-tuple-element.93), channel_id=1, source_target_pairs={{0,16},{1,17},{2,18},{3,19},{4,20},{5,21},{6,22},{7,23},{8,24},{9,... | collective-permute-start | bytes 3342344 | tf_op jit(solution)/shard_map/ppermute | solution.py:334
  17.2 29.9 %collective-permute-start.1 = (bf16[272,2048]{1,0:T(8,128)(2,1)}, bf16[272,2048]{1,0:T(8,128)(2,1)}, u32[]{:S(2)}, u32[]{:S(2)}) collective-permute-start(bf16[272,2048]{1,0:T(8,128)(2,1)} %get-tuple-element.94), channel_id=1, source_target_pairs={{0,2},{1,3},{2,0},{3,1},{4,6},{5,7},{6,4},{7,5},{8,10},{9,11},{10,... | collective-permute-start | bytes 3342344 | tf_op jit(solution)/shard_map/ppermute | solution.py:334
  25.1 14.8 %collective-permute-start.6 = (bf16[128,2048]{1,0:T(8,128)(2,1)}, bf16[128,2048]{1,0:T(8,128)(2,1)}, u32[]{:S(2)}, u32[]{:S(2)}) collective-permute-start(bf16[128,2048]{1,0:T(8,128)(2,1)} %constant_dynamic-update-slice_fusion.refs_4_), channel_id=1, source_target_pairs={{0,8},{1,9},{2,10},{3,11},{4,0},{5,1},{6,2},{7,3},{8,12},{9,13},{1... | collective-permute-start | bytes 1572872 | tf_op jit(solution)/shard_map/ppermute | solution.py:334
  28.4 13.8 %collective-permute-start.8 = (bf16[256,1024]{1,0:T(8,128)(2,1)}, bf16[256,1024]{1,0:T(8,128)(2,1)S(1)}, u32[]{:S(2)}, u32[]{:S(2)}) collective-permute-start(bf16[256,1024]{1,0:T(8,128)(2,1)} %collective-permute-done.2.refs_6_), channel_id=1, source_target_pairs={{0,1},{1,0},{2,3},{3,2},{4,5},{5,4},{6,7},{7,6},{8,9},{9,8},{10,11... | collective-permute-start | bytes 1572872 | tf_op jit(solution)/shard_map/ppermute | solution.py:334
  28.5 18.6 %collective-permute-start.4 = (bf16[256,1024]{1,0:T(8,128)(2,1)}, bf16[256,1024]{1,0:T(8,128)(2,1)S(1)}, u32[]{:S(2)}, u32[]{:S(2)}) collective-permute-start(bf16[256,1024]{1,0:T(8,128)(2,1)} %collective-permute-done.2.refs_6_), channel_id=1, source_target_pairs={{0,8},{1,9},{2,10},{3,11},{4,0},{5,1},{6,2},{7,3},{8,12},{9,13},{1... | collective-permute-start | bytes 1572872 | tf_op jit(solution)/shard_map/ppermute | solution.py:334
  47.1 32.8 %collective-permute-start.9 = (bf16[272,2048]{1,0:T(8,128)(2,1)S(1)}, bf16[272,2048]{1,0:T(8,128)(2,1)S(1)}, u32[]{:S(2)}, u32[]{:S(2)}) collective-permute-start(bf16[272,2048]{1,0:T(8,128)(2,1)S(1)} %copy-done.20), channel_id=1, source_target_pairs={{0,18},{1,19},{2,16},{3,17},{4,22},{5,23},{6,20},{7,21},{8,26},{9,... | collective-permute-start | bytes 3342344 | tf_op jit(solution)/shard_map/ppermute | solution.py:334
  48.6 9.7 %collective-permute-start.14 = (bf16[128,2048]{1,0:T(8,128)(2,1)}, bf16[128,2048]{1,0:T(8,128)(2,1)S(1)}, u32[]{:S(2)}, u32[]{:S(2)}) collective-permute-start(bf16[128,2048]{1,0:T(8,128)(2,1)} %constant_dynamic-update-slice_fusion.refs_4_), channel_id=1, source_target_pairs={{0,1},{1,0},{2,3},{3,2},{4,5},{5,4},{6,7},{7,6},{8,9},{9,8},{10,11... | collective-permute-start | bytes 1572872 | tf_op jit(solution)/shard_map/ppermute | solution.py:334
  49.1 9.2 %collective-permute-start.12 = (bf16[128,1024]{1,0:T(8,128)(2,1)S(1)}, bf16[128,1024]{1,0:T(8,128)(2,1)S(1)}, u32[]{:S(2)}, u32[]{:S(2)}) collective-permute-start(bf16[128,1024]{1,0:T(8,128)(2,1)S(1)} %pad_maximum_fusion.refs_10_), channel_id=1, source_target_pairs={{0,8},{1,9},{2,10},{3,11},{4,0},{5,1},{6,2},{7,3},{8,12},{9,13},{1... | collective-permute-start | bytes 786440 | tf_op jit(solution)/shard_map/ppermute | solution.py:334
  51.6 10.1 %collective-permute-start.13 = (bf16[256,1024]{1,0:T(8,128)(2,1)S(1)}, bf16[256,1024]{1,0:T(8,128)(2,1)S(1)}, u32[]{:S(2)}, u32[]{:S(2)}) collective-permute-start(bf16[256,1024]{1,0:T(8,128)(2,1)S(1)} %collective-permute-done.4.refs_8_), channel_id=1, source_target_pairs={{0,1},{1,0},{2,3},{3,2},{4,5},{5,4},{6,7},{7,6},{8,9},{9,8},{10,11... | collective-permute-start | bytes 1572872 | tf_op jit(solution)/shard_map/ppermute | solution.py:334
  51.6 17.9 %collective-permute-start.10 = (bf16[256,1024]{1,0:T(8,128)(2,1)S(1)}, bf16[256,1024]{1,0:T(8,128)(2,1)S(1)}, u32[]{:S(2)}, u32[]{:S(2)}) collective-permute-start(bf16[256,1024]{1,0:T(8,128)(2,1)S(1)} %collective-permute-done.4.refs_8_), channel_id=1, source_target_pairs={{0,8},{1,9},{2,10},{3,11},{4,0},{5,1},{6,2},{7,3},{8,12},{9,13},{1... | collective-permute-start | bytes 1572872 | tf_op jit(solution)/shard_map/ppermute | solution.py:334
  58.3 11.2 %collective-permute-start.15 = (bf16[128,2048]{1,0:T(8,128)(2,1)}, bf16[128,2048]{1,0:T(8,128)(2,1)S(1)}, u32[]{:S(2)}, u32[]{:S(2)}) collective-permute-start(bf16[128,2048]{1,0:T(8,128)(2,1)} %collective-permute-done.6.refs_6_), channel_id=1, source_target_pairs={{0,1},{1,0},{2,3},{3,2},{4,5},{5,4},{6,7},{7,6},{8,9},{9,8},{10,11... | collective-permute-start | bytes 1572872 | tf_op jit(solution)/shard_map/ppermute | solution.py:334
  58.3 21.6 %collective-permute-start.11 = (bf16[128,2048]{1,0:T(8,128)(2,1)}, bf16[128,2048]{1,0:T(8,128)(2,1)S(1)}, u32[]{:S(2)}, u32[]{:S(2)}) collective-permute-start(bf16[128,2048]{1,0:T(8,128)(2,1)} %collective-permute-done.6.refs_6_), channel_id=1, source_target_pairs={{0,8},{1,9},{2,10},{3,11},{4,0},{5,1},{6,2},{7,3},{8,12},{9,13},{1... | collective-permute-start | bytes 1572872 | tf_op jit(solution)/shard_map/ppermute | solution.py:334
  79.9 12.7 %collective-permute-start.19 = (bf16[128,2048]{1,0:T(8,128)(2,1)S(1)}, bf16[128,2048]{1,0:T(8,128)(2,1)S(1)}, u32[]{:S(2)}, u32[]{:S(2)}) collective-permute-start(bf16[128,2048]{1,0:T(8,128)(2,1)S(1)} %collective-permute-done.11.refs_8_), channel_id=1, source_target_pairs={{0,1},{1,0},{2,3},{3,2},{4,5},{5,4},{6,7},{7,6},{8,9},{9,8},{10,11... | collective-permute-start | bytes 1572872 | tf_op jit(solution)/shard_map/ppermute | solution.py:334
  80.4 14.6 %collective-permute-start.18 = (bf16[128,2048]{1,0:T(8,128)(2,1)S(1)}, bf16[128,2048]{1,0:T(8,128)(2,1)S(1)}, u32[]{:S(2)}, u32[]{:S(2)}) collective-permute-start(bf16[128,2048]{1,0:T(8,128)(2,1)S(1)} %collective-permute-done.11.refs_8_), channel_id=1, source_target_pairs={{0,8},{1,9},{2,10},{3,11},{4,0},{5,1},{6,2},{7,3},{8,12},{9,13},{1... | collective-permute-start | bytes 1572872 | tf_op jit(solution)/shard_map/ppermute | solution.py:334
  95.0 13.7 %collective-permute-start.20 = (bf16[272,1024]{1,0:T(8,128)(2,1)S(1)}, bf16[272,1024]{1,0:T(8,128)(2,1)S(1)}, u32[]{:S(2)}, u32[]{:S(2)}) collective-permute-start(bf16[272,1024]{1,0:T(8,128)(2,1)S(1)} %get-tuple-element.135), channel_id=1, source_target_pairs={{0,16},{1,17},{2,18},{3,19},{4,20},{5,21},{6,22},{7,23},{8,24},{9,... | collective-permute-start | bytes 1671176 | tf_op jit(solution)/shard_map/ppermute | solution.py:334
  95.5 13.4 %collective-permute-start.21 = (bf16[272,1024]{1,0:T(8,128)(2,1)S(1)}, bf16[272,1024]{1,0:T(8,128)(2,1)S(1)}, u32[]{:S(2)}, u32[]{:S(2)}) collective-permute-start(bf16[272,1024]{1,0:T(8,128)(2,1)S(1)} %get-tuple-element.136), channel_id=1, source_target_pairs={{0,2},{1,3},{2,0},{3,1},{4,6},{5,7},{6,4},{7,5},{8,10},{9,11},{10,... | collective-permute-start | bytes 1671176 | tf_op jit(solution)/shard_map/ppermute | solution.py:334
  97.1 9.6 %collective-permute-start.24 = (bf16[128,2048]{1,0:T(8,128)(2,1)S(1)}, bf16[128,2048]{1,0:T(8,128)(2,1)S(1)}, u32[]{:S(2)}, u32[]{:S(2)}) collective-permute-start(bf16[128,2048]{1,0:T(8,128)(2,1)S(1)} %collective-permute-done.18.refs_10_), channel_id=1, source_target_pairs={{0,1},{1,0},{2,3},{3,2},{4,5},{5,4},{6,7},{7,6},{8,9},{9,8},{10,11... | collective-permute-start | bytes 1572872 | tf_op jit(solution)/shard_map/ppermute | solution.py:334
  97.6 9.1 %collective-permute-start.22 = (bf16[128,1024]{1,0:T(8,128)(2,1)S(1)}, bf16[128,1024]{1,0:T(8,128)(2,1)S(1)}, u32[]{:S(2)}, u32[]{:S(2)}) collective-permute-start(bf16[128,1024]{1,0:T(8,128)(2,1)S(1)} %collective-permute-done.12.refs_12_), channel_id=1, source_target_pairs={{0,8},{1,9},{2,10},{3,11},{4,0},{5,1},{6,2},{7,3},{8,12},{9,13},{1... | collective-permute-start | bytes 786440 | tf_op jit(solution)/shard_map/ppermute | solution.py:334
  109.0 16.0 %collective-permute-start.30 = (bf16[272,1024]{1,0:T(8,128)(2,1)S(1)}, bf16[272,1024]{1,0:T(8,128)(2,1)S(1)}, u32[]{:S(2)}, u32[]{:S(2)}) collective-permute-start(bf16[272,1024]{1,0:T(8,128)(2,1)S(1)} %get-tuple-element.148._), channel_id=1, source_target_pairs={{0,18},{1,19},{2,16},{3,17},{4,22},{5,23},{6,20},{7,21},{8,26},{9,... | collective-permute-start | bytes 1671176 | tf_op jit(solution)/shard_map/ppermute | solution.py:334
  111.4 10.0 %collective-permute-start.26 = (bf16[128,1024]{1,0:T(8,128)(2,1)S(1)}, bf16[128,1024]{1,0:T(8,128)(2,1)S(1)}, u32[]{:S(2)}, u32[]{:S(2)}) collective-permute-start(bf16[128,1024]{1,0:T(8,128)(2,1)S(1)} %collective-permute-done.22.refs_14_), channel_id=1, source_target_pairs={{0,1},{1,0},{2,3},{3,2},{4,5},{5,4},{6,7},{7,6},{8,9},{9,8},{10,11... | collective-permute-start | bytes 786440 | tf_op jit(solution)/shard_map/ppermute | solution.py:334
  111.4 10.0 %collective-permute-start.25 = (bf16[128,1024]{1,0:T(8,128)(2,1)S(1)}, bf16[128,1024]{1,0:T(8,128)(2,1)}, u32[]{:S(2)}, u32[]{:S(2)}) collective-permute-start(bf16[128,1024]{1,0:T(8,128)(2,1)S(1)} %collective-permute-done.22.refs_14_), channel_id=1, source_target_pairs={{0,8},{1,9},{2,10},{3,11},{4,0},{5,1},{6,2},{7,3},{8,12},{9,13},{1... | collective-permute-start | bytes 786440 | tf_op jit(solution)/shard_map/ppermute | solution.py:334
  (29 other events, 541.9 us)

commit v4 on v3

--- a/solution.py
+++ b/solution.py
@@ -21,36 +21,67 @@
     return pl.CostEstimate(flops=flops, bytes_accessed=bytes_accessed, transcendentals=0)
 
 
-def split_columns(prefill, decode, tenants, owner, down, place, steps, kk, reps, sides, flips, pad):
-    rows, dec = prefill.shape[0], decode.shape[0]
+def column_spot(rep, y, m, j, reps, sides):
+    other = (y * reps + rep) ^ m
+    return ((j // 2 * sides + other // reps) * 2 + j % 2) * reps + other % reps
+
+
+def split_down(down, place, steps, kk, reps, sides, flips):
     ranks = down.shape[0]
     wide = steps * kk
+    if kk % 128:
+
+        def pick(m):
+            cut = down.reshape(ranks, -1, kk)
+            order = jnp.arange(steps, dtype=jnp.int32)
+            order = column_spot(place[0], place[1], m, order, reps, sides)
+            return jnp.take(cut, order, axis=1).reshape(ranks, wide)
+
+        return [pick(m) for m in flips]
+
+    def kernel(here, dwn, *outs):
+        for i, m in enumerate(flips):
+            for j in range(steps):
+                at = column_spot(here[0], here[1], m, j, reps, sides)
+                outs[i][:, j * kk : (j + 1) * kk] = dwn[:, pl.ds(pl.multiple_of(at * kk, kk), kk)]
+
+    whole = lambda j, *_: (0, 0)
+    return pl.pallas_call(
+        kernel,
+        grid_spec=pltpu.PrefetchScalarGridSpec(
+            num_scalar_prefetch=1,
+            grid=(1,),
+            in_specs=[pl.BlockSpec(down.shape, whole)],
+            out_specs=[pl.BlockSpec((ranks, wide), whole)] * len(flips),
+        ),
+        out_shape=[jax.ShapeDtypeStruct((ranks, wide), jnp.bfloat16)] * len(flips),
+        compiler_params=pltpu.CompilerParams(vmem_limit_bytes=VMEM),
+        cost_estimate=cost(0, 2 * 2**20),
+        name="split_down",
+    )(place, down)
+
+
+def split_columns(prefill, decode, tenants, owner, place, steps, kk, reps, sides, pad):
+    rows, dec = prefill.shape[0], decode.shape[0]
+    wide = steps * kk
     slots_all = owner.shape[0]
-
-    def spot(rep, y, m, j):
-        other = (y * reps + rep) ^ m
-        return ((j // 2 * sides + other // reps) * 2 + j % 2) * reps + other % reps
-
     if kk % 128:
         stacked = jnp.concatenate([prefill, decode], axis=0)
         hot = tenants.reshape(rows, 1) == jnp.arange(slots_all, dtype=jnp.int32)[None, :]
         slots = jnp.sum(jnp.where(hot, owner[None, :], 0), axis=1).astype(jnp.bfloat16)
         slots = jnp.broadcast_to(jnp.pad(slots, (0, wide - rows))[None, :], (pad, wide))
 
-        def pick(a, m):
-            cut = a.reshape(a.shape[0], -1, kk)
-            order = spot(place[0], place[1], m, jnp.arange(steps, dtype=jnp.int32))
-            return jnp.take(cut, order, axis=1).reshape(a.shape[0], wide)
-
-        return (
-            [jnp.concatenate([pick(stacked, m), slots], axis=0) for m in range(4)],
-            [pick(down, m) for m in flips],
-        )
-    count = len(flips)
+        def pick(m):
+            cut = stacked.reshape(stacked.shape[0], -1, kk)
+            order = jnp.arange(steps, dtype=jnp.int32)
+            order = column_spot(place[0], place[1], m, order, reps, sides)
+            return jnp.take(cut, order, axis=1).reshape(stacked.shape[0], wide)
+
+        return [jnp.concatenate([pick(m), slots], axis=0) for m in range(4)]
     turns = 2
     each = steps // turns
 
-    def kernel(here, own, pre, dcd, ten, dwn, *outs):
+    def kernel(here, own, pre, dcd, ten, *outs):
         turn = pl.program_id(0)
         slot = jnp.zeros((1, rows), jnp.float32)
         for s in range(slots_all):
@@ -59,40 +90,34 @@
         slot = jnp.concatenate([slot] + [jnp.zeros_like(slot)] * (each * kk // rows - 1), axis=1)
         for m in range(4):
             for i in range(each):
-                at = spot(here[0], here[1], m, turn * each + i)
+                at = column_spot(here[0], here[1], m, turn * each + i, reps, sides)
                 at = pl.ds(pl.multiple_of(at * kk, kk), kk)
                 to = slice(i * kk, (i + 1) * kk)
                 outs[m][0:rows, to] = pre[:, at]
                 below = jnp.concatenate([dcd[:, at], slot[:, to]], axis=0)
                 outs[m][rows : rows + dec + pad, to] = below
-                if m in flips:
-                    outs[4 + flips.index(m)][:, to] = dwn[:, at]
 
     out = lambda j, *_: (0, j)
     whole = lambda j, *_: (0, 0)
-    outs = pl.pallas_call(
+    return pl.pallas_call(
         kernel,
         grid_spec=pltpu.PrefetchScalarGridSpec(
             num_scalar_prefetch=2,
             grid=(turns,),
-            in_specs=[pl.BlockSpec(a.shape, whole) for a in (prefill, decode, tenants, down)],
-            out_specs=[pl.BlockSpec((rows + dec + pad, each * kk), out)] * 4
-            + [pl.BlockSpec((ranks, each * kk), out)] * count,
+            in_specs=[pl.BlockSpec(a.shape, whole) for a in (prefill, decode, tenants)],
+            out_specs=[pl.BlockSpec((rows + dec + pad, each * kk), out)] * 4,
         ),
-        out_shape=[jax.ShapeDtypeStruct((rows + dec + pad, wide), jnp.bfloat16)] * 4
-        + [jax.ShapeDtypeStruct((ranks, wide), jnp.bfloat16)] * count,
+        out_shape=[jax.ShapeDtypeStruct((rows + dec + pad, wide), jnp.bfloat16)] * 4,
         compiler_params=pltpu.CompilerParams(vmem_limit_bytes=VMEM),
-        cost_estimate=cost(0, 10 * 2**20),
+        cost_estimate=cost(0, 9 * 2**20),
         name="split_columns",
-    )(place, owner, prefill, decode, tenants, down)
-    return list(outs[:4]), list(outs[4:])
-
-
-def base_products(blocks, parts, spots):
+    )(place, owner, prefill, decode, tenants)
+
+
+def base_products(blocks, parts, spots, kinds):
     kk, out_width = parts[0].shape
     tall = blocks[0].shape[0]
     n = len(parts)
-    kinds = [jnp.float32] + [jnp.bfloat16] * (len(blocks) - 1)
     if kk % 128:
         quarter = jnp.zeros((n * kk, out_width), jnp.bfloat16)
         for i in range(n):
@@ -207,7 +232,28 @@
     )(after, *blocks, *pieces, columns)
 
 
-def finish(parts, block, ups, columns, bases, rows, first, rank):
+def own_attention(fresh, queries, tops, totals, mix):
+    dec, out_width = fresh.shape
+    heads = queries.shape[0] // dec
+    kv_heads = out_width // 2 // HEAD_SIZE
+    fresh = fresh.astype(jnp.bfloat16).astype(jnp.float32)
+    parts = [fresh[:, i * HEAD_SIZE : (i + 1) * HEAD_SIZE] for i in range(2 * kv_heads)]
+    group = heads // kv_heads
+    keys = jnp.concatenate([parts[h // group] for h in range(heads)], axis=0)
+    values = jnp.concatenate([parts[kv_heads + h // group] for h in range(heads)], axis=0)
+    own = jnp.sum(queries.astype(jnp.float32) * keys, axis=1, keepdims=True)
+    own = jnp.broadcast_to(own * (1.0 / math.sqrt(HEAD_SIZE)), mix.shape)
+    tops, totals = jnp.broadcast_to(tops, mix.shape), jnp.broadcast_to(totals, mix.shape)
+    top = jnp.maximum(tops, own)
+    kept, weight = jnp.exp(tops - top), jnp.exp(own - top)
+    mixed = (kept * mix + weight * values) / (kept * totals + weight)
+    mixed = mixed.astype(jnp.bfloat16)
+    return [mixed[h * dec : (h + 1) * dec] for h in range(heads)]
+
+
+def finish(parts, block, ups, columns, bases, rows, first, rank, cached, dec):
+    heads = cached[0].shape[0] // dec
+    shape = (dec, heads * HEAD_SIZE)
     packed_rows = parts[0].shape[0]
     folds = rows // packed_rows
     out_width = bases[0].shape[1]
@@ -225,15 +271,20 @@
         )
         up = jnp.concatenate(ups, axis=0)
         delta = jnp.dot(spread, up, preferred_element_type=jnp.float32).astype(jnp.bfloat16)
-        base = sum(b.astype(jnp.float32) for b in bases)[:rows]
-        return (base + adapter_scale * delta.astype(jnp.float32)).astype(jnp.bfloat16)
+        base = sum(b.astype(jnp.float32) for b in bases)
+        attended = own_attention(base[rows : rows + dec], *cached)
+        base = base[:rows]
+        projected = (base + adapter_scale * delta.astype(jnp.float32)).astype(jnp.bfloat16)
+        return projected, jnp.concatenate(attended, axis=1)
     cut = 256
+    below = bases[0].shape[0] - rows
 
     def kernel(*refs):
         packs = refs[:4]
         blk, col = refs[4:6]
         bas, upr = refs[6:10], refs[10 : 10 + n]
-        out, wide = refs[10 + n :]
+        own, old = refs[10 + n : 14 + n], refs[14 + n : 18 + n]
+        out, out_attended, wide = refs[18 + n :]
 
         @pl.when(pl.program_id(0) == 0)
         def _():
@@ -251,6 +302,12 @@
             for i in range(0, n * tall, 128):
                 kept = jnp.where(slot == col[0:1, i : i + 128], lowered, 0.0)
                 wide[:, i : i + 128] = kept.astype(jnp.bfloat16)
+            fresh = own[0][...]
+            for b in own[1:]:
+                fresh = fresh + b[...].astype(jnp.float32)
+            parts_own = own_attention(fresh[:dec], *[c[...] for c in old])
+            for h in range(heads):
+                out_attended[:, h * HEAD_SIZE : (h + 1) * HEAD_SIZE] = parts_own[h]
 
         up = jnp.concatenate([u[...] for u in upr], axis=0)
         delta = jnp.dot(wide[...], up, preferred_element_type=jnp.float32)
@@ -272,14 +329,19 @@
             pl.BlockSpec(columns.shape, one),
         ]
         + [pl.BlockSpec((bases[0].shape[0], cut), column)] * 4
-        + [pl.BlockSpec((tall, cut), column)] * n,
-        out_specs=pl.BlockSpec((rows, cut), column),
-        out_shape=jax.ShapeDtypeStruct((rows, out_width), jnp.bfloat16),
+        + [pl.BlockSpec((tall, cut), column)] * n
+        + [pl.BlockSpec((below, out_width), lambda j: (rows // below, 0))] * 4
+        + [pl.BlockSpec(a.shape, one) for a in cached],
+        out_specs=[pl.BlockSpec((rows, cut), column), pl.BlockSpec(shape, one)],
+        out_shape=[
+            jax.ShapeDtypeStruct((rows, out_width), jnp.bfloat16),
+            jax.ShapeDtypeStruct(shape, jnp.bfloat16),
+        ],
         scratch_shapes=[pltpu.VMEM((rows, n * tall), jnp.bfloat16)],
         compiler_params=pltpu.CompilerParams(vmem_limit_bytes=VMEM),
         cost_estimate=cost(2 * rows * n * tall * out_width, 5 * 2**20),
         name="finish",
-    )(*parts, block, columns, *bases, *ups)
+    )(*parts, block, columns, *bases, *ups, *bases, *cached)
 
 
 def body(
@@ -353,26 +415,39 @@
         return near if far is None else jnp.concatenate([near, far], axis=0)
 
     bases = [lax.dynamic_slice_in_dim(base_weight, r * kk, kk, axis=0)]
+    up = adapter_up.reshape(ranks, out_width)
+    here, bases, up = phase(jnp.stack([r, y]), bases, up)
     bases.append(send(bases[0], ring))
-    up = adapter_up.reshape(ranks, out_width)
     up_far = send(up, flips[reps]) if sides == 2 else None
-    messages, downs = split_columns(
+    y_flips = [0, reps] if sides == 2 else [0]
+    downs = split_down(adapter_down.reshape(ranks, width), here, steps, kk, reps, sides, y_flips)
+    here, downs = phase(here, downs)
+    down_far = send(downs[1], flips[reps]) if sides == 2 else None
+    messages = split_columns(
         prefill_rows,
         decode_rows,
         tenant_ids.reshape(1, rows),
         owner_slot,
-        adapter_down.reshape(ranks, width),
-        jnp.stack([r, y]),
+        here,
         steps,
         kk,
         reps,
         sides,
-        [0, reps] if sides == 2 else [0],
         pad,
     )
+    downs = [paired(downs[0], down_far)]
+    ups = [paired(up, up_far)]
+    base_parts = both(bases[0])
+    bases, downs, ups, messages, base_parts = phase(bases, downs, ups, messages, base_parts)
     near = [send(messages[m], flips[m]) for m in (1, 2)]
-    down_far = send(downs[1], flips[reps]) if sides == 2 else None
-    bases, up_far = phase(bases, up_far)
+    message = messages[0]
+
+    bases.append(send(bases[-1], ring))
+    bases, queries = phase(bases, queries)
+    while len(bases) < planes:
+        bases.append(send(bases[-1], ring))
+    for held in bases[1:2]:
+        base_parts = base_parts + both(held)
 
     kv_heads = half_width // HEAD_SIZE
     query_groups = queries.shape[1] // half_width
@@ -398,6 +473,13 @@
         stored_values,
         preferred_element_type=jnp.float32,
     )
+    tall = kv_heads * query_groups * dec
+
+    def by_head(value):
+        value = value if value.ndim == 4 else value[..., None]
+        return value.transpose(1, 2, 0, 3).reshape(tall, value.shape[3])
+
+    cached = [by_head(v) for v in (query_head_rows, cached_top, cached_total, cached_mix)]
 
     group = jnp.arange(slots_all, dtype=jnp.int32)
     inner = group % local_slots
@@ -406,86 +488,68 @@
     step = group // (local_slots * sides * 2)
     column_slot = ((plane_of(step) * sides + (y ^ side)) * 2 + (c ^ core)) * local_slots + inner
     columns = jnp.repeat(column_slot, rank).astype(jnp.float32)[None, :]
-
-    downs = [paired(downs[0], down_far)]
-    bases.append(send(bases[-1], ring))
-    downs.append(send(downs[-1], ring))
-    ups = [paired(up, up_far)]
-    base_parts = both(bases[0]) + both(bases[1])
-    near, bases, downs, ups, base_parts, far, cached_top, cached_total, cached_mix, columns, spots = phase(
-        near,
-        bases,
-        downs,
-        ups,
-        base_parts,
-        messages[3],
-        cached_top,
-        cached_total,
-        cached_mix,
-        columns,
-        spots,
+    core = group // (local_slots * sides * planes)
+    step = (group // (local_slots * sides)) % planes
+    column_slot = ((plane_of(step) * sides + (y ^ side)) * 2 + (c ^ core)) * local_slots + inner
+    up_columns = jnp.repeat(column_slot, rank).astype(jnp.float32)[None, :]
+
+    pieces = both(downs[0])
+    near, bases, ups, far, base_parts, pieces, cached, columns, up_columns, spots = phase(
+        near, bases, ups, messages[3], base_parts, pieces, cached, columns, up_columns, spots
     )
 
     far = send(far, flips[3])
-    while len(bases) < planes:
-        bases.append(send(bases[-1], ring))
-    downs.append(send(downs[-1], ring))
-    ups.append(send(ups[-1], ring))
-    for held in bases[2:-1]:
+    while len(downs) < max(2, planes - 1):
+        downs.append(send(downs[-1], ring))
+    for held in bases[2:]:
         base_parts = base_parts + both(held)
-    pieces = both(downs[0]) + both(downs[1])
-    up_parts = both(ups[0])
-    near, far, bases, downs, ups, base_parts, pieces, up_parts = phase(
-        near, far, bases, downs, ups, base_parts, pieces, up_parts
-    )
-
-    blocks = [messages[0], *near, far]
-    base_parts = base_parts + both(bases[-1])
-    partials = base_products(blocks, base_parts, spots)
+    partials = base_products(near, base_parts, spots, [jnp.bfloat16] * 2)
+    up_cores = [send(ups[0], cores)]
+    pieces = pieces + both(downs[1])
+    far, downs, ups, partials, base_parts, up_cores, pieces = phase(
+        far, downs, ups, partials, base_parts, up_cores, pieces
+    )
+
+    base = [send(partials[m - 1], flips[m]) for m in (1, 2)]
     while len(downs) < planes:
         downs.append(send(downs[-1], ring))
+    ups.append(send(ups[0], ring))
+    last, own = base_products([far, message], base_parts, spots, [jnp.bfloat16, jnp.float32])
     pieces = pieces + sum([both(d) for d in downs[2:-1]], [])
-    partials, downs, pieces, ups = phase(partials, downs, pieces, ups)
-
-    base = [partials[0]] + [send(partials[m], flips[m]) for m in (1, 2)]
-    while len(ups) < planes - 1:
-        ups.append(send(ups[-1], ring))
+    base, downs, ups, last, own, pieces, up_cores = phase(
+        base, downs, ups, last, own, pieces, up_cores
+    )
+
+    base = [own, *base, send(last, flips[3])]
+    blocks = [message, *near, far]
     pieces = pieces + both(downs[-1])
-    up_parts = up_parts + both(ups[1])
-    base, ups, up_parts, pieces, last = phase(base, ups, up_parts, pieces, partials[3])
-
-    base.append(send(last, flips[3]))
-    ups.append(send(ups[-1], ring))
-    up_parts = up_parts + sum([both(u) for u in ups[2:-1]], [])
-
+    for k in range(2, planes):
+        after_k = {order[i]: order[(i + k) % planes] for i in range(planes)}
+        pairs = []
+        for a, b in everyone:
+            to = after_k[b // (2 * sides)] * 2 * sides + b % (2 * sides)
+            pairs.append((a * peers + b, a * peers + to))
+        ups.append(send(ups[0], pairs))
     first = rows + dec
     packed = lowered_products(blocks, pieces, columns, rows, first, rank, last)
-    packed, ups, up_parts = phase(packed, ups, up_parts)
+    _, ups = phase(packed, ups)
     packed = [packed[0]] + [send(packed[m], flips[m]) for m in (1, 2, 3)]
-    up_parts = up_parts + both(ups[-1])
-
-    recent_output = sum(b[rows : rows + dec].astype(jnp.float32) for b in base).astype(jnp.bfloat16)
-    newest_keys = recent_output[:, :half_width].reshape(dec, kv_heads, HEAD_SIZE)
-    newest_values = recent_output[:, half_width:].reshape(dec, kv_heads, HEAD_SIZE)
-    own_score = (
-        jnp.sum(
-            query_head_rows.astype(jnp.float32) * newest_keys.astype(jnp.float32)[:, :, None, :],
-            axis=-1,
+    up_parts = ups + up_cores + [send(u, cores) for u in ups[1:]]
+    base, packed, up_parts = phase(base, packed, up_parts)
+    return tuple(
+        finish(
+            packed,
+            message,
+            up_parts,
+            up_columns,
+            base,
+            rows,
+            first,
+            rank,
+            cached,
+            dec,
         )
-        * scale
-    )
-    top = jnp.maximum(cached_top, own_score)
-    kept = jnp.exp(cached_top - top)
-    own_weight = jnp.exp(own_score - top)
-    total = kept * cached_total + own_weight
-    mixed = (
-        kept[..., None] * cached_mix
-        + own_weight[..., None] * newest_values.astype(jnp.float32)[:, :, None, :]
-    ) / total[..., None]
-    attended = mixed.reshape(dec, query_groups * half_width).astype(jnp.bfloat16)
-
-    projected = finish(packed, messages[0], up_parts, columns, base, rows, first, rank)
-    return (projected, attended)
+    )
 
 
 def solution(mesh):

time: 133 us -> 139 us (1.045)
  Pallas kernels: 26.6 us -> 32.7 us
  starting transfers between devices: 39.6 us -> 34 us
  local copies, waits for them, and re-layouts: 6.13 us -> 8.33 us
  waiting for transfers between devices: 54.4 us -> 56.5 us
  other arithmetic: 2.25 us -> 3.88 us
    ppermute x32, starting transfers between devices: 39.6 us -> 34 us  [send(): return lax.ppermute(value, BOTH, pairs)]
    pallas_call x1 -> x2, Pallas kernels: 8.83 us -> 12.7 us  [base_products(): pl.pallas_call(kernel, grid_spec=pltpu.PrefetchScalarGridSpec(num_scalar_...]
    pallas_call x0 -> x1, Pallas kernels: none -> 2.75 us  [split_down(): pl.pallas_call(kernel, grid_spec=pltpu.PrefetchScalarGridSpec(num_scalar_...]
    concatenate x1 -> x2, other arithmetic: 0.92 us -> 2.98 us  [paired(): return near if far is None else jnp.concatenate([near, far], axis=0)]
    ppermute x32, waiting for transfers between devices: 54.4 us -> 56.5 us  [send(): return lax.ppermute(value, BOTH, pairs)]
    optimization_barrier x0 -> x2, local copies, waits for them, and re-layouts: none -> 1.59 us  [phase(): return lax.optimization_barrier(values)]
    unnamed x44 -> x38, local copies, waits for them, and re-layouts: 3.28 us -> 3.36 us
  transfers between devices with their start and end apart: 32 -> 32, of which waited for: 11 -> 13; matrix products, arithmetic and copies ran while one was open for 8% -> 6% of each run, Pallas kernels for 16% -> 20%
where the time goes in v4:
time: 139 us; the launch traced here: 138 us
  waiting for transfers between devices  56.5 us (41%)
  starting transfers between devices  34 us (24%)
  Pallas kernels  32.7 us (24%)
  local copies, waits for them, and re-layouts  8.33 us (6%)
  other arithmetic  3.88 us (3%)
  matrix products  1.97 us (1%)
    ppermute x32, waiting for transfers between devices, send(): return lax.ppermute(value, BOTH, pairs)  56.5 us
    ppermute x32, starting transfers between devices, send(): return lax.ppermute(value, BOTH, pairs)  34 us
    pallas_call x2, Pallas kernels, base_products(): pl.pallas_call(kernel, grid_spec=pltpu.PrefetchScalarGridSpec(num_scalar_...  12.7 us
    pallas_call x1, Pallas kernels, lowered_products(): pl.pallas_call(kernel, grid=(1,), in_specs=[pl.BlockSpec(memory_space=pl....  6.43 us
    pallas_call x1, Pallas kernels, finish(): pl.pallas_call(kernel, grid=(out_width // cut,), in_specs=[pl.BlockSpec(p...  5.5 us
    pallas_call x1, Pallas kernels, split_columns(): pl.pallas_call(kernel, grid_spec=pltpu.PrefetchScalarGridSpec(num_scalar_...  5.4 us
    unnamed x38, local copies, waits for them, and re-layouts  3.36 us
    concatenate x2, other arithmetic, paired(): return near if far is None else jnp.concatenate([near, far], axis=0)  2.98 us
  transfers between devices with their start and end apart: 32, of which 13 were waited for; matrix products, arithmetic and copies ran while one was open for 6% of the time, Pallas kernels for 20%

profile of v4, /device:TPU:0, one launch (start us, length us, event | category | flops | bytes accessed | tf_op | source)
XLA Modules:
  0.0 138.3 jit_solution(1486642657711202844)
XLA Ops:
  2.6 4.1 %collective-permute-start = (bf16[256,1024]{1,0:T(8,128)(2,1)S(1)}, bf16[256,1024]{1,0:T(8,128)(2,1)}, u32[]{:S(2)}, u32[]{:S(2)}) collective-permute-start(bf16[256,1024]{1,0:T(8,128)(2,1)S(1)} %constant_dynamic-slice_fusion.refs_2_), channel_id=1, source_target_pairs={{0,8},{1,9},{2,10},{3,11},{4,0},{5,1},{6,2},{7,3},{8,12},{9,13},{1... | collective-permute-start | bytes 1572872 | tf_op jit(solution)/shard_map/ppermute | solution.py:396
  6.7 2.7 %split_down.1 = (bf16[64,2048]{1,0:T(8,128)(2,1)}, bf16[64,2048]{1,0:T(8,128)(2,1)}) custom-call(s32[2]{0:T(128)} %pad_add_fusion.here, bf16[64,8192]{1,0:T(8,128)(2,1)} %bitcast.49), custom_call_target="tpu_custom_call" | custom-call | bytes 2097152 | tf_op jit(solution)/shard_map/split_down/pallas_call | solution.py:49
  11.5 5.4 %split_columns.1 = (bf16[272,2048]{1,0:T(8,128)(2,1)}, bf16[272,2048]{1,0:T(8,128)(2,1)}, bf16[272,2048]{1,0:T(8,128)(2,1)}, bf16[272,2048]{1,0:T(8,128)(2,1)}) custom-call(s32[2]{0:T(128)} %pad_add_fusion.here, s32[32]{0:T(128)} %own.1, bf16[256,8192]{1,0:T(8,128)(2,1)} %pre.1, bf16[8,8192]{1,0:T(8,128)(2,1)} %dcd.1, s32[1,256]{1,0:T(1,128)} %bitcast.57), custom_call_target="tpu_custom_call" | custom-call | bytes 9437184 | tf_op jit(solution)/shard_map/split_columns/pallas_call | solution.py:102
  16.9 4.4 %collective-permute-done.2 = bf16[64,1024]{1,0:T(8,128)(2,1)} collective-permute-done((bf16[64,1024]{1,0:T(8,128)(2,1)}, bf16[64,1024]{1,0:T(8,128)(2,1)}, u32[]{:S(2)}, u32[]{:S(2)}) %collective-permute-start.2) | collective-permute-done | bytes 131104 | tf_op jit(solution)/shard_map/ppermute | solution.py:396
  22.3 2.0 %pad_maximum_fusion.refs_4_ = bf16[128,2048]{1,0:T(8,128)(2,1)} fusion(bf16[64,2048]{1,0:T(8,128)(2,1)} %collective-permute-done.1, bf16[64,2048]{1,0:T(8,128)(2,1)} %get-tuple-element.109), kind=kLoop, calls=%fused_computation.9 | loop fusion | flops 1048576 | bytes 1048576 | tf_op jit(solution)/shard_map/concatenate | solution.py:415
  24.3 1.6 %collective-permute-start.6 = (bf16[256,1024]{1,0:T(8,128)(2,1)}, bf16[256,1024]{1,0:T(8,128)(2,1)}, u32[]{:S(2)}, u32[]{:S(2)}) collective-permute-start(bf16[256,1024]{1,0:T(8,128)(2,1)} %collective-permute-done.refs_4_), channel_id=1, source_target_pairs={{0,8},{1,9},{2,10},{3,11},{4,0},{5,1},{6,2},{7,3},{8,12},{9,13},{1... | collective-permute-start | bytes 1572872 | tf_op jit(solution)/shard_map/ppermute | solution.py:396
  30.0 8.2 %collective-permute-done.6.refs_6_ = bf16[256,1024]{1,0:T(8,128)(2,1)} collective-permute-done((bf16[256,1024]{1,0:T(8,128)(2,1)}, bf16[256,1024]{1,0:T(8,128)(2,1)}, u32[]{:S(2)}, u32[]{:S(2)}) %collective-permute-start.6) | collective-permute-done | bytes 524320 | tf_op jit(solution)/shard_map/ppermute | solution.py:396
  38.2 2.5 %collective-permute-start.7 = (bf16[256,1024]{1,0:T(8,128)(2,1)}, bf16[256,1024]{1,0:T(8,128)(2,1)}, u32[]{:S(2)}, u32[]{:S(2)}) collective-permute-start(bf16[256,1024]{1,0:T(8,128)(2,1)} %collective-permute-done.6.refs_6_), channel_id=1, source_target_pairs={{0,8},{1,9},{2,10},{3,11},{4,0},{5,1},{6,2},{7,3},{8,12},{9,13},{1... | collective-permute-start | bytes 1572872 | tf_op jit(solution)/shard_map/ppermute | solution.py:396
  44.1 7.2 %collective-permute-done.7.refs_8_ = bf16[256,1024]{1,0:T(8,128)(2,1)} collective-permute-done((bf16[256,1024]{1,0:T(8,128)(2,1)}, bf16[256,1024]{1,0:T(8,128)(2,1)}, u32[]{:S(2)}, u32[]{:S(2)}) %collective-permute-start.7) | collective-permute-done | bytes 524320 | tf_op jit(solution)/shard_map/ppermute | solution.py:396
  54.9 2.3 %collective-permute-start.11 = (bf16[128,2048]{1,0:T(8,128)(2,1)}, bf16[128,2048]{1,0:T(8,128)(2,1)S(1)}, u32[]{:S(2)}, u32[]{:S(2)}) collective-permute-start(bf16[128,2048]{1,0:T(8,128)(2,1)} %pad_maximum_fusion.refs_4_), channel_id=1, source_target_pairs={{0,8},{1,9},{2,10},{3,11},{4,0},{5,1},{6,2},{7,3},{8,12},{9,13},{1... | collective-permute-start | bytes 1572872 | tf_op jit(solution)/shard_map/ppermute | solution.py:396
  57.7 9.5 %collective-permute-done.11.refs_6_ = bf16[128,2048]{1,0:T(8,128)(2,1)S(1)} collective-permute-done((bf16[128,2048]{1,0:T(8,128)(2,1)}, bf16[128,2048]{1,0:T(8,128)(2,1)S(1)}, u32[]{:S(2)}, u32[]{:S(2)}) %collective-permute-start.11) | collective-permute-done | bytes 524320 | tf_op jit(solution)/shard_map/ppermute | solution.py:396
  67.2 2.5 %collective-permute-start.12 = (bf16[128,2048]{1,0:T(8,128)(2,1)S(1)}, bf16[128,2048]{1,0:T(8,128)(2,1)S(1)}, u32[]{:S(2)}, u32[]{:S(2)}) collective-permute-start(bf16[128,2048]{1,0:T(8,128)(2,1)S(1)} %collective-permute-done.11.refs_6_), channel_id=1, source_target_pairs={{0,8},{1,9},{2,10},{3,11},{4,0},{5,1},{6,2},{7,3},{8,12},{9,13},{1... | collective-permute-start | bytes 1572872 | tf_op jit(solution)/shard_map/ppermute | solution.py:396
  71.3 6.4 %base_products.2 = (bf16[272,1024]{1,0:T(8,128)(2,1)S(1)}, bf16[272,1024]{1,0:T(8,128)(2,1)S(1)}) custom-call(s32[8]{0:T(128)S(1)} %fusion.21.spot, bf16[272,2048]{1,0:T(8,128)(2,1)} %collective-permute-done.4.refs_0_.refs_1_, bf16[272,2048]{1,0:T(8,128)(2,1)} %collective-permute-done.5.refs_1_.refs_2_, bf16[256,1024]{1,0:T(8,128)(2,1)S(1)} %copy-done.5, ...), custom_call_target="tpu_custom_call" | custom-call | flops 2281701376 | bytes 6422528 | tf_op jit(solution)/shard_map/base_products/pallas_call | solution.py:146
  81.3 2.3 %collective-permute-start.19 = (bf16[128,2048]{1,0:T(8,128)(2,1)S(1)}, bf16[128,2048]{1,0:T(8,128)(2,1)S(1)}, u32[]{:S(2)}, u32[]{:S(2)}) collective-permute-start(bf16[128,2048]{1,0:T(8,128)(2,1)S(1)} %collective-permute-done.12.refs_8_), channel_id=1, source_target_pairs={{0,8},{1,9},{2,10},{3,11},{4,0},{5,1},{6,2},{7,3},{8,12},{9,13},{1... | collective-permute-start | bytes 1572872 | tf_op jit(solution)/shard_map/ppermute | solution.py:396
  83.6 6.2 %base_products.3 = (bf16[272,1024]{1,0:T(8,128)(2,1)}, f32[272,1024]{1,0:T(8,128)S(1)}) custom-call(s32[8]{0:T(128)S(1)} %fusion.21.spot, bf16[272,2048]{1,0:T(8,128)(2,1)S(1)} %collective-permute-done.10.refs_0_.refs_3_, bf16[272,2048]{1,0:T(8,128)(2,1)S(1)} %copy-done.2, bf16[256,1024]{1,0:T(8,128)(2,1)S(1)} %copy-done.6, ...), custom_call_target="tpu_custom_call" | custom-call | flops 2281701376 | bytes 6422528 | tf_op jit(solution)/shard_map/base_products/pallas_call | solution.py:146
  90.9 7.0 %collective-permute-done.20.refs_11_ = bf16[128,1024]{1,0:T(8,128)(2,1)} collective-permute-done((bf16[128,1024]{1,0:T(8,128)(2,1)S(1)}, bf16[128,1024]{1,0:T(8,128)(2,1)}, u32[]{:S(2)}, u32[]{:S(2)}) %collective-permute-start.20) | collective-permute-done | bytes 262176 | tf_op jit(solution)/shard_map/ppermute | solution.py:396
  98.0 1.9 %collective-permute-start.27 = (bf16[128,1024]{1,0:T(8,128)(2,1)S(1)}, bf16[128,1024]{1,0:T(8,128)(2,1)}, u32[]{:S(2)}, u32[]{:S(2)}) collective-permute-start(bf16[128,1024]{1,0:T(8,128)(2,1)S(1)} %pad_maximum_fusion.1.refs_10_), channel_id=1, source_target_pairs={{0,12},{1,13},{2,14},{3,15},{4,8},{5,9},{6,10},{7,11},{8,4},{9,5},... | collective-permute-start | bytes 786440 | tf_op jit(solution)/shard_map/ppermute | solution.py:396
  102.3 6.4 %lowered_products.1 = (f32[64,128]{1,0:T(8,128)S(1)}, f32[64,128]{1,0:T(8,128)S(1)}, f32[64,128]{1,0:T(8,128)S(1)}, f32[64,128]{1,0:T(8,128)S(1)}) custom-call(bf16[272,1024]{1,0:T(8,128)(2,1)} %get-tuple-element.167._, bf16[272,2048]{1,0:T(8,128)(2,1)S(1)} %copy-done.2, bf16[272,2048]{1,0:T(8,128)(2,1)} %collective-permute-done.4.refs_0_.refs_1_, ...), custom_call_target="tpu_custom_call" | custom-call | flops 4294967296 | bytes 8388608 | tf_op jit(solution)/shard_map/lowered_products/pallas_call | solution.py:219
  109.4 9.5 %collective-permute-done.28.refs_13_ = bf16[128,1024]{1,0:T(8,128)(2,1)} collective-permute-done((bf16[128,1024]{1,0:T(8,128)(2,1)S(1)}, bf16[128,1024]{1,0:T(8,128)(2,1)}, u32[]{:S(2)}, u32[]{:S(2)}) %collective-permute-start.28) | collective-permute-done | bytes 262176 | tf_op jit(solution)/shard_map/ppermute | solution.py:396
  120.6 2.7 %collective-permute-done.24.refs_1_ = f32[64,128]{1,0:T(8,128)S(1)} collective-permute-done((f32[64,128]{1,0:T(8,128)S(1)}, f32[64,128]{1,0:T(8,128)S(1)}, u32[]{:S(2)}, u32[]{:S(2)}) %collective-permute-start.24) | collective-permute-done | bytes 32800 | tf_op jit(solution)/shard_map/ppermute | solution.py:396
  123.3 1.5 %collective-permute-start.25 = (f32[64,128]{1,0:T(8,128)S(1)}, f32[64,128]{1,0:T(8,128)S(1)}, u32[]{:S(2)}, u32[]{:S(2)}) collective-permute-start(f32[64,128]{1,0:T(8,128)S(1)} %get-tuple-element.178), channel_id=1, source_target_pairs={{0,2},{1,3},{2,0},{3,1},{4,6},{5,7},{6,4},{7,5},{8,10},{9,11},{10,... | collective-permute-start | bytes 98312 | tf_op jit(solution)/shard_map/ppermute | solution.py:396
  124.8 2.4 %collective-permute-done.25.refs_2_ = f32[64,128]{1,0:T(8,128)S(1)} collective-permute-done((f32[64,128]{1,0:T(8,128)S(1)}, f32[64,128]{1,0:T(8,128)S(1)}, u32[]{:S(2)}, u32[]{:S(2)}) %collective-permute-start.25) | collective-permute-done | bytes 32800 | tf_op jit(solution)/shard_map/ppermute | solution.py:396
  130.3 1.7 %collective-permute-done.26.refs_3_ = f32[64,128]{1,0:T(8,128)S(1)} collective-permute-done((f32[64,128]{1,0:T(8,128)S(1)}, f32[64,128]{1,0:T(8,128)S(1)}, u32[]{:S(2)}, u32[]{:S(2)}) %collective-permute-start.26) | collective-permute-done | bytes 32800 | tf_op jit(solution)/shard_map/ppermute | solution.py:396
  132.8 5.5 %finish.1 = (bf16[256,1024]{1,0:T(8,128)(2,1)}, bf16[8,4096]{1,0:T(8,128)(2,1)}) custom-call(f32[64,128]{1,0:T(8,128)} %copy-done.7, f32[64,128]{1,0:T(8,128)} %copy-done.15, f32[64,128]{1,0:T(8,128)} %copy-done.16, f32[64,128]{1,0:T(8,128)} %copy-done.17, bf16[272,2048]{1,0:T(8,128)(2,1)} %get-tuple-element.148.refs_1_.refs_0_.refs_4_, ...), custom_call_target="tpu_custom_call" | custom-call | flops 536870912 | bytes 5242880 | tf_op jit(solution)/shard_map/finish/pallas_call | solution.py:323
  (105 shorter events, 31.2 us)
Async XLA Ops:
  2.6 21.7 %collective-permute-start = (bf16[256,1024]{1,0:T(8,128)(2,1)S(1)}, bf16[256,1024]{1,0:T(8,128)(2,1)}, u32[]{:S(2)}, u32[]{:S(2)}) collective-permute-start(bf16[256,1024]{1,0:T(8,128)(2,1)S(1)} %constant_dynamic-slice_fusion.refs_2_), channel_id=1, source_target_pairs={{0,8},{1,9},{2,10},{3,11},{4,0},{5,1},{6,2},{7,3},{8,12},{9,13},{1... | collective-permute-start | bytes 1572872 | tf_op jit(solution)/shard_map/ppermute | solution.py:396
  6.7 17.6 %collective-permute-start.3 = (bf16[256,1024]{1,0:T(8,128)(2,1)S(1)}, bf16[256,1024]{1,0:T(8,128)(2,1)}, u32[]{:S(2)}, u32[]{:S(2)}) collective-permute-start(bf16[256,1024]{1,0:T(8,128)(2,1)S(1)} %constant_dynamic-slice_fusion.refs_2_), channel_id=1, source_target_pairs={{0,1},{1,0},{2,3},{3,2},{4,5},{5,4},{6,7},{7,6},{8,9},{9,8},{10,11... | collective-permute-start | bytes 1572872 | tf_op jit(solution)/shard_map/ppermute | solution.py:396
  9.5 12.8 %collective-permute-start.1 = (bf16[64,2048]{1,0:T(8,128)(2,1)}, bf16[64,2048]{1,0:T(8,128)(2,1)}, u32[]{:S(2)}, u32[]{:S(2)}) collective-permute-start(bf16[64,2048]{1,0:T(8,128)(2,1)} %get-tuple-element.110), channel_id=1, source_target_pairs={{0,2},{1,3},{2,0},{3,1},{4,6},{5,7},{6,4},{7,5},{8,10},{9,11},{10,... | collective-permute-start | bytes 786440 | tf_op jit(solution)/shard_map/ppermute | solution.py:396
  24.3 13.9 %collective-permute-start.6 = (bf16[256,1024]{1,0:T(8,128)(2,1)}, bf16[256,1024]{1,0:T(8,128)(2,1)}, u32[]{:S(2)}, u32[]{:S(2)}) collective-permute-start(bf16[256,1024]{1,0:T(8,128)(2,1)} %collective-permute-done.refs_4_), channel_id=1, source_target_pairs={{0,8},{1,9},{2,10},{3,11},{4,0},{5,1},{6,2},{7,3},{8,12},{9,13},{1... | collective-permute-start | bytes 1572872 | tf_op jit(solution)/shard_map/ppermute | solution.py:396
  26.0 26.2 %collective-permute-start.4 = (bf16[272,2048]{1,0:T(8,128)(2,1)}, bf16[272,2048]{1,0:T(8,128)(2,1)}, u32[]{:S(2)}, u32[]{:S(2)}) collective-permute-start(bf16[272,2048]{1,0:T(8,128)(2,1)} %get-tuple-element.117), channel_id=1, source_target_pairs={{0,16},{1,17},{2,18},{3,19},{4,20},{5,21},{6,22},{7,23},{8,24},{9,... | collective-permute-start | bytes 3342344 | tf_op jit(solution)/shard_map/ppermute | solution.py:396
  27.4 25.9 %collective-permute-start.5 = (bf16[272,2048]{1,0:T(8,128)(2,1)}, bf16[272,2048]{1,0:T(8,128)(2,1)}, u32[]{:S(2)}, u32[]{:S(2)}) collective-permute-start(bf16[272,2048]{1,0:T(8,128)(2,1)} %get-tuple-element.118), channel_id=1, source_target_pairs={{0,2},{1,3},{2,0},{3,1},{4,6},{5,7},{6,4},{7,5},{8,10},{9,11},{10,... | collective-permute-start | bytes 3342344 | tf_op jit(solution)/shard_map/ppermute | solution.py:396
  30.0 14.1 %collective-permute-start.9 = (bf16[128,2048]{1,0:T(8,128)(2,1)}, bf16[128,2048]{1,0:T(8,128)(2,1)}, u32[]{:S(2)}, u32[]{:S(2)}) collective-permute-start(bf16[128,2048]{1,0:T(8,128)(2,1)} %pad_maximum_fusion.refs_4_), channel_id=1, source_target_pairs={{0,1},{1,0},{2,3},{3,2},{4,5},{5,4},{6,7},{7,6},{8,9},{9,8},{10,11... | collective-permute-start | bytes 1572872 | tf_op jit(solution)/shard_map/ppermute | solution.py:396
  38.2 13.0 %collective-permute-start.7 = (bf16[256,1024]{1,0:T(8,128)(2,1)}, bf16[256,1024]{1,0:T(8,128)(2,1)}, u32[]{:S(2)}, u32[]{:S(2)}) collective-permute-start(bf16[256,1024]{1,0:T(8,128)(2,1)} %collective-permute-done.6.refs_6_), channel_id=1, source_target_pairs={{0,8},{1,9},{2,10},{3,11},{4,0},{5,1},{6,2},{7,3},{8,12},{9,13},{1... | collective-permute-start | bytes 1572872 | tf_op jit(solution)/shard_map/ppermute | solution.py:396
  53.4 25.8 %collective-permute-start.10 = (bf16[272,2048]{1,0:T(8,128)(2,1)}, bf16[272,2048]{1,0:T(8,128)(2,1)S(1)}, u32[]{:S(2)}, u32[]{:S(2)}) collective-permute-start(bf16[272,2048]{1,0:T(8,128)(2,1)} %get-tuple-element.128), channel_id=1, source_target_pairs={{0,18},{1,19},{2,16},{3,17},{4,22},{5,23},{6,20},{7,21},{8,26},{9,... | collective-permute-start | bytes 3342344 | tf_op jit(solution)/shard_map/ppermute | solution.py:396
  54.9 12.3 %collective-permute-start.11 = (bf16[128,2048]{1,0:T(8,128)(2,1)}, bf16[128,2048]{1,0:T(8,128)(2,1)S(1)}, u32[]{:S(2)}, u32[]{:S(2)}) collective-permute-start(bf16[128,2048]{1,0:T(8,128)(2,1)} %pad_maximum_fusion.refs_4_), channel_id=1, source_target_pairs={{0,8},{1,9},{2,10},{3,11},{4,0},{5,1},{6,2},{7,3},{8,12},{9,13},{1... | collective-permute-start | bytes 1572872 | tf_op jit(solution)/shard_map/ppermute | solution.py:396
  57.1 12.6 %collective-permute-start.13 = (bf16[256,1024]{1,0:T(8,128)(2,1)}, bf16[256,1024]{1,0:T(8,128)(2,1)S(1)}, u32[]{:S(2)}, u32[]{:S(2)}) collective-permute-start(bf16[256,1024]{1,0:T(8,128)(2,1)} %collective-permute-done.6.refs_6_), channel_id=1, source_target_pairs={{0,1},{1,0},{2,3},{3,2},{4,5},{5,4},{6,7},{7,6},{8,9},{9,8},{10,11... | collective-permute-start | bytes 1572872 | tf_op jit(solution)/shard_map/ppermute | solution.py:396
  57.1 13.1 %collective-permute-start.14 = (bf16[256,1024]{1,0:T(8,128)(2,1)}, bf16[256,1024]{1,0:T(8,128)(2,1)S(1)}, u32[]{:S(2)}, u32[]{:S(2)}) collective-permute-start(bf16[256,1024]{1,0:T(8,128)(2,1)} %collective-permute-done.7.refs_8_), channel_id=1, source_target_pairs={{0,1},{1,0},{2,3},{3,2},{4,5},{5,4},{6,7},{7,6},{8,9},{9,8},{10,11... | collective-permute-start | bytes 1572872 | tf_op jit(solution)/shard_map/ppermute | solution.py:396
  67.2 11.0 %collective-permute-start.12 = (bf16[128,2048]{1,0:T(8,128)(2,1)S(1)}, bf16[128,2048]{1,0:T(8,128)(2,1)S(1)}, u32[]{:S(2)}, u32[]{:S(2)}) collective-permute-start(bf16[128,2048]{1,0:T(8,128)(2,1)S(1)} %collective-permute-done.11.refs_6_), channel_id=1, source_target_pairs={{0,8},{1,9},{2,10},{3,11},{4,0},{5,1},{6,2},{7,3},{8,12},{9,13},{1... | collective-permute-start | bytes 1572872 | tf_op jit(solution)/shard_map/ppermute | solution.py:396
  79.2 18.7 %collective-permute-start.17 = (bf16[272,1024]{1,0:T(8,128)(2,1)S(1)}, bf16[272,1024]{1,0:T(8,128)(2,1)S(1)}, u32[]{:S(2)}, u32[]{:S(2)}) collective-permute-start(bf16[272,1024]{1,0:T(8,128)(2,1)S(1)} %get-tuple-element.143), channel_id=1, source_target_pairs={{0,16},{1,17},{2,18},{3,19},{4,20},{5,21},{6,22},{7,23},{8,24},{9,... | collective-permute-start | bytes 1671176 | tf_op jit(solution)/shard_map/ppermute | solution.py:396
  79.8 18.1 %collective-permute-start.18 = (bf16[272,1024]{1,0:T(8,128)(2,1)S(1)}, bf16[272,1024]{1,0:T(8,128)(2,1)S(1)}, u32[]{:S(2)}, u32[]{:S(2)}) collective-permute-start(bf16[272,1024]{1,0:T(8,128)(2,1)S(1)} %get-tuple-element.144), channel_id=1, source_target_pairs={{0,2},{1,3},{2,0},{3,1},{4,6},{5,7},{6,4},{7,5},{8,10},{9,11},{10,... | collective-permute-start | bytes 1671176 | tf_op jit(solution)/shard_map/ppermute | solution.py:396
  81.3 16.6 %collective-permute-start.19 = (bf16[128,2048]{1,0:T(8,128)(2,1)S(1)}, bf16[128,2048]{1,0:T(8,128)(2,1)S(1)}, u32[]{:S(2)}, u32[]{:S(2)}) collective-permute-start(bf16[128,2048]{1,0:T(8,128)(2,1)S(1)} %collective-permute-done.12.refs_8_), channel_id=1, source_target_pairs={{0,8},{1,9},{2,10},{3,11},{4,0},{5,1},{6,2},{7,3},{8,12},{9,13},{1... | collective-permute-start | bytes 1572872 | tf_op jit(solution)/shard_map/ppermute | solution.py:396
  83.6 14.3 %collective-permute-start.21 = (bf16[128,2048]{1,0:T(8,128)(2,1)S(1)}, bf16[128,2048]{1,0:T(8,128)(2,1)S(1)}, u32[]{:S(2)}, u32[]{:S(2)}) collective-permute-start(bf16[128,2048]{1,0:T(8,128)(2,1)S(1)} %collective-permute-done.12.refs_8_), channel_id=1, source_target_pairs={{0,1},{1,0},{2,3},{3,2},{4,5},{5,4},{6,7},{7,6},{8,9},{9,8},{10,11... | collective-permute-start | bytes 1572872 | tf_op jit(solution)/shard_map/ppermute | solution.py:396
  83.6 14.3 %collective-permute-start.20 = (bf16[128,1024]{1,0:T(8,128)(2,1)S(1)}, bf16[128,1024]{1,0:T(8,128)(2,1)}, u32[]{:S(2)}, u32[]{:S(2)}) collective-permute-start(bf16[128,1024]{1,0:T(8,128)(2,1)S(1)} %pad_maximum_fusion.1.refs_10_), channel_id=1, source_target_pairs={{0,8},{1,9},{2,10},{3,11},{4,0},{5,1},{6,2},{7,3},{8,12},{9,13},{1... | collective-permute-start | bytes 786440 | tf_op jit(solution)/shard_map/ppermute | solution.py:396
  98.0 11.3 %collective-permute-start.27 = (bf16[128,1024]{1,0:T(8,128)(2,1)S(1)}, bf16[128,1024]{1,0:T(8,128)(2,1)}, u32[]{:S(2)}, u32[]{:S(2)}) collective-permute-start(bf16[128,1024]{1,0:T(8,128)(2,1)S(1)} %pad_maximum_fusion.1.refs_10_), channel_id=1, source_target_pairs={{0,12},{1,13},{2,14},{3,15},{4,8},{5,9},{6,10},{7,11},{8,4},{9,5},... | collective-permute-start | bytes 786440 | tf_op jit(solution)/shard_map/ppermute | solution.py:396
  99.9 18.9 %collective-permute-start.28 = (bf16[128,1024]{1,0:T(8,128)(2,1)S(1)}, bf16[128,1024]{1,0:T(8,128)(2,1)}, u32[]{:S(2)}, u32[]{:S(2)}) collective-permute-start(bf16[128,1024]{1,0:T(8,128)(2,1)S(1)} %pad_maximum_fusion.1.refs_10_), channel_id=1, source_target_pairs={{0,4},{1,5},{2,6},{3,7},{4,12},{5,13},{6,14},{7,15},{8,0},{9,1},{1... | collective-permute-start | bytes 786440 | tf_op jit(solution)/shard_map/ppermute | solution.py:396
  100.8 31.2 %collective-permute-start.22 = (bf16[272,1024]{1,0:T(8,128)(2,1)}, bf16[272,1024]{1,0:T(8,128)(2,1)}, u32[]{:S(2)}, u32[]{:S(2)}) collective-permute-start(bf16[272,1024]{1,0:T(8,128)(2,1)} %get-tuple-element.167._), channel_id=1, source_target_pairs={{0,18},{1,19},{2,16},{3,17},{4,22},{5,23},{6,20},{7,21},{8,26},{9,... | collective-permute-start | bytes 1671176 | tf_op jit(solution)/shard_map/ppermute | solution.py:396
  118.9 13.2 %collective-permute-start.29 = (bf16[128,1024]{1,0:T(8,128)(2,1)}, bf16[128,1024]{1,0:T(8,128)(2,1)S(1)}, u32[]{:S(2)}, u32[]{:S(2)}) collective-permute-start(bf16[128,1024]{1,0:T(8,128)(2,1)} %collective-permute-done.20.refs_11_), channel_id=1, source_target_pairs={{0,1},{1,0},{2,3},{3,2},{4,5},{5,4},{6,7},{7,6},{8,9},{9,8},{10,11... | collective-permute-start | bytes 786440 | tf_op jit(solution)/shard_map/ppermute | solution.py:396
  118.9 13.2 %collective-permute-start.30 = (bf16[128,1024]{1,0:T(8,128)(2,1)}, bf16[128,1024]{1,0:T(8,128)(2,1)}, u32[]{:S(2)}, u32[]{:S(2)}) collective-permute-start(bf16[128,1024]{1,0:T(8,128)(2,1)} %collective-permute-done.27.refs_12_), channel_id=1, source_target_pairs={{0,1},{1,0},{2,3},{3,2},{4,5},{5,4},{6,7},{7,6},{8,9},{9,8},{10,11... | collective-permute-start | bytes 786440 | tf_op jit(solution)/shard_map/ppermute | solution.py:396
  119.4 12.7 %collective-permute-start.31 = (bf16[128,1024]{1,0:T(8,128)(2,1)}, bf16[128,1024]{1,0:T(8,128)(2,1)}, u32[]{:S(2)}, u32[]{:S(2)}) collective-permute-start(bf16[128,1024]{1,0:T(8,128)(2,1)} %collective-permute-done.28.refs_13_), channel_id=1, source_target_pairs={{0,1},{1,0},{2,3},{3,2},{4,5},{5,4},{6,7},{7,6},{8,9},{9,8},{10,11... | collective-permute-start | bytes 786440 | tf_op jit(solution)/shard_map/ppermute | solution.py:396
  (27 other events, 361.7 us)

commit v5 on v4

--- a/solution.py
+++ b/solution.py
@@ -532,8 +532,8 @@
         ups.append(send(ups[0], pairs))
     first = rows + dec
     packed = lowered_products(blocks, pieces, columns, rows, first, rank, last)
-    _, ups = phase(packed, ups)
     packed = [packed[0]] + [send(packed[m], flips[m]) for m in (1, 2, 3)]
+    packed, ups = phase(packed, ups)
     up_parts = ups + up_cores + [send(u, cores) for u in ups[1:]]
     base, packed, up_parts = phase(base, packed, up_parts)
     return tuple(

time: 139 us -> 128 us (0.921)
  waiting for transfers between devices: 56.5 us -> 46.5 us
    ppermute x32, waiting for transfers between devices: 56.5 us -> 46.5 us  [send(): return lax.ppermute(value, BOTH, pairs)]
  transfers between devices with their start and end apart: 32 -> 32, of which waited for: 13 -> 12; matrix products, arithmetic and copies ran while one was open for 6% -> 7% of each run, Pallas kernels for 20% -> 21%
where the time goes in v5:
time: 128 us; the launch traced here: 127 us
  waiting for transfers between devices  46.5 us (36%)
  starting transfers between devices  33.4 us (26%)
  Pallas kernels  32.7 us (26%)
  local copies, waits for them, and re-layouts  7.92 us (6%)
  other arithmetic  3.88 us (3%)
  matrix products  1.97 us (2%)
    ppermute x32, waiting for transfers between devices, send(): return lax.ppermute(value, BOTH, pairs)  46.5 us
    ppermute x32, starting transfers between devices, send(): return lax.ppermute(value, BOTH, pairs)  33.4 us
    pallas_call x2, Pallas kernels, base_products(): pl.pallas_call(kernel, grid_spec=pltpu.PrefetchScalarGridSpec(num_scalar_...  12.7 us
    pallas_call x1, Pallas kernels, lowered_products(): pl.pallas_call(kernel, grid=(1,), in_specs=[pl.BlockSpec(memory_space=pl....  6.43 us
    pallas_call x1, Pallas kernels, finish(): pl.pallas_call(kernel, grid=(out_width // cut,), in_specs=[pl.BlockSpec(p...  5.5 us
    pallas_call x1, Pallas kernels, split_columns(): pl.pallas_call(kernel, grid_spec=pltpu.PrefetchScalarGridSpec(num_scalar_...  5.4 us
    concatenate x2, other arithmetic, paired(): return near if far is None else jnp.concatenate([near, far], axis=0)  2.98 us
    unnamed x38, local copies, waits for them, and re-layouts  2.95 us
  transfers between devices with their start and end apart: 32, of which 12 were waited for; matrix products, arithmetic and copies ran while one was open for 7% of the time, Pallas kernels for 21%

profile of v5, /device:TPU:0, one launch (start us, length us, event | category | flops | bytes accessed | tf_op | source)
XLA Modules:
  0.0 127.4 jit_solution(17762636371904427869)
XLA Ops:
  2.6 4.1 %collective-permute-start = (bf16[256,1024]{1,0:T(8,128)(2,1)S(1)}, bf16[256,1024]{1,0:T(8,128)(2,1)}, u32[]{:S(2)}, u32[]{:S(2)}) collective-permute-start(bf16[256,1024]{1,0:T(8,128)(2,1)S(1)} %constant_dynamic-slice_fusion.refs_2_), channel_id=1, source_target_pairs={{0,8},{1,9},{2,10},{3,11},{4,0},{5,1},{6,2},{7,3},{8,12},{9,13},{1... | collective-permute-start | bytes 1572872 | tf_op jit(solution)/shard_map/ppermute | solution.py:396
  6.7 2.7 %split_down.1 = (bf16[64,2048]{1,0:T(8,128)(2,1)}, bf16[64,2048]{1,0:T(8,128)(2,1)}) custom-call(s32[2]{0:T(128)} %pad_add_fusion.here, bf16[64,8192]{1,0:T(8,128)(2,1)} %bitcast.49), custom_call_target="tpu_custom_call" | custom-call | bytes 2097152 | tf_op jit(solution)/shard_map/split_down/pallas_call | solution.py:49
  9.5 1.5 %collective-permute-start.1 = (bf16[64,2048]{1,0:T(8,128)(2,1)}, bf16[64,2048]{1,0:T(8,128)(2,1)}, u32[]{:S(2)}, u32[]{:S(2)}) collective-permute-start(bf16[64,2048]{1,0:T(8,128)(2,1)} %get-tuple-element.114), channel_id=1, source_target_pairs={{0,2},{1,3},{2,0},{3,1},{4,6},{5,7},{6,4},{7,5},{8,10},{9,11},{10,... | collective-permute-start | bytes 786440 | tf_op jit(solution)/shard_map/ppermute | solution.py:396
  11.5 5.4 %split_columns.1 = (bf16[272,2048]{1,0:T(8,128)(2,1)}, bf16[272,2048]{1,0:T(8,128)(2,1)}, bf16[272,2048]{1,0:T(8,128)(2,1)}, bf16[272,2048]{1,0:T(8,128)(2,1)}) custom-call(s32[2]{0:T(128)} %pad_add_fusion.here, s32[32]{0:T(128)} %own.1, bf16[256,8192]{1,0:T(8,128)(2,1)} %pre.1, bf16[8,8192]{1,0:T(8,128)(2,1)} %dcd.1, s32[1,256]{1,0:T(1,128)} %bitcast.57), custom_call_target="tpu_custom_call" | custom-call | bytes 9437184 | tf_op jit(solution)/shard_map/split_columns/pallas_call | solution.py:102
  16.9 4.4 %collective-permute-done.2 = bf16[64,1024]{1,0:T(8,128)(2,1)} collective-permute-done((bf16[64,1024]{1,0:T(8,128)(2,1)}, bf16[64,1024]{1,0:T(8,128)(2,1)}, u32[]{:S(2)}, u32[]{:S(2)}) %collective-permute-start.2) | collective-permute-done | bytes 131104 | tf_op jit(solution)/shard_map/ppermute | solution.py:396
  22.3 2.0 %pad_maximum_fusion.refs_4_ = bf16[128,2048]{1,0:T(8,128)(2,1)} fusion(bf16[64,2048]{1,0:T(8,128)(2,1)} %collective-permute-done.1, bf16[64,2048]{1,0:T(8,128)(2,1)} %get-tuple-element.113), kind=kLoop, calls=%fused_computation.9 | loop fusion | flops 1048576 | bytes 1048576 | tf_op jit(solution)/shard_map/concatenate | solution.py:415
  24.3 1.6 %collective-permute-start.6 = (bf16[256,1024]{1,0:T(8,128)(2,1)}, bf16[256,1024]{1,0:T(8,128)(2,1)}, u32[]{:S(2)}, u32[]{:S(2)}) collective-permute-start(bf16[256,1024]{1,0:T(8,128)(2,1)} %collective-permute-done.refs_4_), channel_id=1, source_target_pairs={{0,8},{1,9},{2,10},{3,11},{4,0},{5,1},{6,2},{7,3},{8,12},{9,13},{1... | collective-permute-start | bytes 1572872 | tf_op jit(solution)/shard_map/ppermute | solution.py:396
  27.4 1.5 %collective-permute-start.5 = (bf16[272,2048]{1,0:T(8,128)(2,1)}, bf16[272,2048]{1,0:T(8,128)(2,1)}, u32[]{:S(2)}, u32[]{:S(2)}) collective-permute-start(bf16[272,2048]{1,0:T(8,128)(2,1)} %get-tuple-element.122), channel_id=1, source_target_pairs={{0,2},{1,3},{2,0},{3,1},{4,6},{5,7},{6,4},{7,5},{8,10},{9,11},{10,... | collective-permute-start | bytes 3342344 | tf_op jit(solution)/shard_map/ppermute | solution.py:396
  30.0 8.2 %collective-permute-done.6.refs_6_ = bf16[256,1024]{1,0:T(8,128)(2,1)} collective-permute-done((bf16[256,1024]{1,0:T(8,128)(2,1)}, bf16[256,1024]{1,0:T(8,128)(2,1)}, u32[]{:S(2)}, u32[]{:S(2)}) %collective-permute-start.6) | collective-permute-done | bytes 524320 | tf_op jit(solution)/shard_map/ppermute | solution.py:396
  38.2 2.5 %collective-permute-start.7 = (bf16[256,1024]{1,0:T(8,128)(2,1)}, bf16[256,1024]{1,0:T(8,128)(2,1)}, u32[]{:S(2)}, u32[]{:S(2)}) collective-permute-start(bf16[256,1024]{1,0:T(8,128)(2,1)} %collective-permute-done.6.refs_6_), channel_id=1, source_target_pairs={{0,8},{1,9},{2,10},{3,11},{4,0},{5,1},{6,2},{7,3},{8,12},{9,13},{1... | collective-permute-start | bytes 1572872 | tf_op jit(solution)/shard_map/ppermute | solution.py:396
  44.1 7.2 %collective-permute-done.7.refs_8_ = bf16[256,1024]{1,0:T(8,128)(2,1)} collective-permute-done((bf16[256,1024]{1,0:T(8,128)(2,1)}, bf16[256,1024]{1,0:T(8,128)(2,1)}, u32[]{:S(2)}, u32[]{:S(2)}) %collective-permute-start.7) | collective-permute-done | bytes 524320 | tf_op jit(solution)/shard_map/ppermute | solution.py:396
  53.4 1.5 %collective-permute-start.10 = (bf16[272,2048]{1,0:T(8,128)(2,1)}, bf16[272,2048]{1,0:T(8,128)(2,1)S(1)}, u32[]{:S(2)}, u32[]{:S(2)}) collective-permute-start(bf16[272,2048]{1,0:T(8,128)(2,1)} %get-tuple-element.132), channel_id=1, source_target_pairs={{0,18},{1,19},{2,16},{3,17},{4,22},{5,23},{6,20},{7,21},{8,26},{9,... | collective-permute-start | bytes 3342344 | tf_op jit(solution)/shard_map/ppermute | solution.py:396
  54.9 2.3 %collective-permute-start.11 = (bf16[128,2048]{1,0:T(8,128)(2,1)}, bf16[128,2048]{1,0:T(8,128)(2,1)S(1)}, u32[]{:S(2)}, u32[]{:S(2)}) collective-permute-start(bf16[128,2048]{1,0:T(8,128)(2,1)} %pad_maximum_fusion.refs_4_), channel_id=1, source_target_pairs={{0,8},{1,9},{2,10},{3,11},{4,0},{5,1},{6,2},{7,3},{8,12},{9,13},{1... | collective-permute-start | bytes 1572872 | tf_op jit(solution)/shard_map/ppermute | solution.py:396
  57.7 9.5 %collective-permute-done.11.refs_6_ = bf16[128,2048]{1,0:T(8,128)(2,1)S(1)} collective-permute-done((bf16[128,2048]{1,0:T(8,128)(2,1)}, bf16[128,2048]{1,0:T(8,128)(2,1)S(1)}, u32[]{:S(2)}, u32[]{:S(2)}) %collective-permute-start.11) | collective-permute-done | bytes 524320 | tf_op jit(solution)/shard_map/ppermute | solution.py:396
  67.2 2.5 %collective-permute-start.12 = (bf16[128,2048]{1,0:T(8,128)(2,1)S(1)}, bf16[128,2048]{1,0:T(8,128)(2,1)S(1)}, u32[]{:S(2)}, u32[]{:S(2)}) collective-permute-start(bf16[128,2048]{1,0:T(8,128)(2,1)S(1)} %collective-permute-done.11.refs_6_), channel_id=1, source_target_pairs={{0,8},{1,9},{2,10},{3,11},{4,0},{5,1},{6,2},{7,3},{8,12},{9,13},{1... | collective-permute-start | bytes 1572872 | tf_op jit(solution)/shard_map/ppermute | solution.py:396
  71.3 6.4 %base_products.2 = (bf16[272,1024]{1,0:T(8,128)(2,1)S(1)}, bf16[272,1024]{1,0:T(8,128)(2,1)S(1)}) custom-call(s32[8]{0:T(128)S(1)} %fusion.21.spot, bf16[272,2048]{1,0:T(8,128)(2,1)} %collective-permute-done.4.refs_0_.refs_1_, bf16[272,2048]{1,0:T(8,128)(2,1)} %collective-permute-done.5.refs_1_.refs_2_, bf16[256,1024]{1,0:T(8,128)(2,1)S(1)} %copy-done.5, ...), custom_call_target="tpu_custom_call" | custom-call | flops 2281701376 | bytes 6422528 | tf_op jit(solution)/shard_map/base_products/pallas_call | solution.py:146
  79.8 1.5 %collective-permute-start.18 = (bf16[272,1024]{1,0:T(8,128)(2,1)S(1)}, bf16[272,1024]{1,0:T(8,128)(2,1)S(1)}, u32[]{:S(2)}, u32[]{:S(2)}) collective-permute-start(bf16[272,1024]{1,0:T(8,128)(2,1)S(1)} %get-tuple-element.148), channel_id=1, source_target_pairs={{0,2},{1,3},{2,0},{3,1},{4,6},{5,7},{6,4},{7,5},{8,10},{9,11},{10,... | collective-permute-start | bytes 1671176 | tf_op jit(solution)/shard_map/ppermute | solution.py:396
  81.3 2.3 %collective-permute-start.19 = (bf16[128,2048]{1,0:T(8,128)(2,1)S(1)}, bf16[128,2048]{1,0:T(8,128)(2,1)S(1)}, u32[]{:S(2)}, u32[]{:S(2)}) collective-permute-start(bf16[128,2048]{1,0:T(8,128)(2,1)S(1)} %collective-permute-done.12.refs_8_), channel_id=1, source_target_pairs={{0,8},{1,9},{2,10},{3,11},{4,0},{5,1},{6,2},{7,3},{8,12},{9,13},{1... | collective-permute-start | bytes 1572872 | tf_op jit(solution)/shard_map/ppermute | solution.py:396
  83.6 6.2 %base_products.3 = (bf16[272,1024]{1,0:T(8,128)(2,1)}, f32[272,1024]{1,0:T(8,128)S(1)}) custom-call(s32[8]{0:T(128)S(1)} %fusion.21.spot, bf16[272,2048]{1,0:T(8,128)(2,1)S(1)} %collective-permute-done.10.refs_0_.refs_3_, bf16[272,2048]{1,0:T(8,128)(2,1)S(1)} %copy-done.2, bf16[256,1024]{1,0:T(8,128)(2,1)S(1)} %copy-done.6, ...), custom_call_target="tpu_custom_call" | custom-call | flops 2281701376 | bytes 6422528 | tf_op jit(solution)/shard_map/base_products/pallas_call | solution.py:146
  90.9 7.0 %collective-permute-done.20.refs_11_ = bf16[128,1024]{1,0:T(8,128)(2,1)} collective-permute-done((bf16[128,1024]{1,0:T(8,128)(2,1)S(1)}, bf16[128,1024]{1,0:T(8,128)(2,1)}, u32[]{:S(2)}, u32[]{:S(2)}) %collective-permute-start.20) | collective-permute-done | bytes 262176 | tf_op jit(solution)/shard_map/ppermute | solution.py:396
  98.0 1.9 %collective-permute-start.27 = (bf16[128,1024]{1,0:T(8,128)(2,1)S(1)}, bf16[128,1024]{1,0:T(8,128)(2,1)}, u32[]{:S(2)}, u32[]{:S(2)}) collective-permute-start(bf16[128,1024]{1,0:T(8,128)(2,1)S(1)} %pad_maximum_fusion.1.refs_10_), channel_id=1, source_target_pairs={{0,12},{1,13},{2,14},{3,15},{4,8},{5,9},{6,10},{7,11},{8,4},{9,5},... | collective-permute-start | bytes 786440 | tf_op jit(solution)/shard_map/ppermute | solution.py:396
  102.3 6.4 %lowered_products.1 = (f32[64,128]{1,0:T(8,128)S(1)}, f32[64,128]{1,0:T(8,128)S(1)}, f32[64,128]{1,0:T(8,128)S(1)}, f32[64,128]{1,0:T(8,128)S(1)}) custom-call(bf16[272,1024]{1,0:T(8,128)(2,1)} %get-tuple-element.171._, bf16[272,2048]{1,0:T(8,128)(2,1)S(1)} %copy-done.2, bf16[272,2048]{1,0:T(8,128)(2,1)} %collective-permute-done.4.refs_0_.refs_1_, ...), custom_call_target="tpu_custom_call" | custom-call | flops 4294967296 | bytes 8388608 | tf_op jit(solution)/shard_map/lowered_products/pallas_call | solution.py:219
  112.8 6.0 %collective-permute-done.28.refs_13_ = bf16[128,1024]{1,0:T(8,128)(2,1)} collective-permute-done((bf16[128,1024]{1,0:T(8,128)(2,1)S(1)}, bf16[128,1024]{1,0:T(8,128)(2,1)}, u32[]{:S(2)}, u32[]{:S(2)}) %collective-permute-start.28) | collective-permute-done | bytes 262176 | tf_op jit(solution)/shard_map/ppermute | solution.py:396
  121.9 5.5 %finish.1 = (bf16[256,1024]{1,0:T(8,128)(2,1)}, bf16[8,4096]{1,0:T(8,128)(2,1)}) custom-call(f32[64,128]{1,0:T(8,128)} %copy-done.7, f32[64,128]{1,0:T(8,128)} %copy-done.15, f32[64,128]{1,0:T(8,128)} %copy-done.16, f32[64,128]{1,0:T(8,128)} %copy-done.17, bf16[272,2048]{1,0:T(8,128)(2,1)} %get-tuple-element.152.refs_1_.refs_0_.refs_4_, ...), custom_call_target="tpu_custom_call" | custom-call | flops 536870912 | bytes 5242880 | tf_op jit(solution)/shard_map/finish/pallas_call | solution.py:323
  (105 shorter events, 26.1 us)
Async XLA Ops:
  2.6 21.7 %collective-permute-start = (bf16[256,1024]{1,0:T(8,128)(2,1)S(1)}, bf16[256,1024]{1,0:T(8,128)(2,1)}, u32[]{:S(2)}, u32[]{:S(2)}) collective-permute-start(bf16[256,1024]{1,0:T(8,128)(2,1)S(1)} %constant_dynamic-slice_fusion.refs_2_), channel_id=1, source_target_pairs={{0,8},{1,9},{2,10},{3,11},{4,0},{5,1},{6,2},{7,3},{8,12},{9,13},{1... | collective-permute-start | bytes 1572872 | tf_op jit(solution)/shard_map/ppermute | solution.py:396
  6.7 17.6 %collective-permute-start.3 = (bf16[256,1024]{1,0:T(8,128)(2,1)S(1)}, bf16[256,1024]{1,0:T(8,128)(2,1)}, u32[]{:S(2)}, u32[]{:S(2)}) collective-permute-start(bf16[256,1024]{1,0:T(8,128)(2,1)S(1)} %constant_dynamic-slice_fusion.refs_2_), channel_id=1, source_target_pairs={{0,1},{1,0},{2,3},{3,2},{4,5},{5,4},{6,7},{7,6},{8,9},{9,8},{10,11... | collective-permute-start | bytes 1572872 | tf_op jit(solution)/shard_map/ppermute | solution.py:396
  9.5 12.8 %collective-permute-start.1 = (bf16[64,2048]{1,0:T(8,128)(2,1)}, bf16[64,2048]{1,0:T(8,128)(2,1)}, u32[]{:S(2)}, u32[]{:S(2)}) collective-permute-start(bf16[64,2048]{1,0:T(8,128)(2,1)} %get-tuple-element.114), channel_id=1, source_target_pairs={{0,2},{1,3},{2,0},{3,1},{4,6},{5,7},{6,4},{7,5},{8,10},{9,11},{10,... | collective-permute-start | bytes 786440 | tf_op jit(solution)/shard_map/ppermute | solution.py:396
  11.0 10.3 %collective-permute-start.2 = (bf16[64,1024]{1,0:T(8,128)(2,1)}, bf16[64,1024]{1,0:T(8,128)(2,1)}, u32[]{:S(2)}, u32[]{:S(2)}) collective-permute-start(bf16[64,1024]{1,0:T(8,128)(2,1)} %bitcast.54), channel_id=1, source_target_pairs={{0,2},{1,3},{2,0},{3,1},{4,6},{5,7},{6,4},{7,5},{8,10},{9,11},{10,... | collective-permute-start | bytes 393224 | tf_op jit(solution)/shard_map/ppermute | solution.py:396
  24.3 13.9 %collective-permute-start.6 = (bf16[256,1024]{1,0:T(8,128)(2,1)}, bf16[256,1024]{1,0:T(8,128)(2,1)}, u32[]{:S(2)}, u32[]{:S(2)}) collective-permute-start(bf16[256,1024]{1,0:T(8,128)(2,1)} %collective-permute-done.refs_4_), channel_id=1, source_target_pairs={{0,8},{1,9},{2,10},{3,11},{4,0},{5,1},{6,2},{7,3},{8,12},{9,13},{1... | collective-permute-start | bytes 1572872 | tf_op jit(solution)/shard_map/ppermute | solution.py:396
  26.0 26.2 %collective-permute-start.4 = (bf16[272,2048]{1,0:T(8,128)(2,1)}, bf16[272,2048]{1,0:T(8,128)(2,1)}, u32[]{:S(2)}, u32[]{:S(2)}) collective-permute-start(bf16[272,2048]{1,0:T(8,128)(2,1)} %get-tuple-element.121), channel_id=1, source_target_pairs={{0,16},{1,17},{2,18},{3,19},{4,20},{5,21},{6,22},{7,23},{8,24},{9,... | collective-permute-start | bytes 3342344 | tf_op jit(solution)/shard_map/ppermute | solution.py:396
  27.4 25.9 %collective-permute-start.5 = (bf16[272,2048]{1,0:T(8,128)(2,1)}, bf16[272,2048]{1,0:T(8,128)(2,1)}, u32[]{:S(2)}, u32[]{:S(2)}) collective-permute-start(bf16[272,2048]{1,0:T(8,128)(2,1)} %get-tuple-element.122), channel_id=1, source_target_pairs={{0,2},{1,3},{2,0},{3,1},{4,6},{5,7},{6,4},{7,5},{8,10},{9,11},{10,... | collective-permute-start | bytes 3342344 | tf_op jit(solution)/shard_map/ppermute | solution.py:396
  30.0 14.1 %collective-permute-start.9 = (bf16[128,2048]{1,0:T(8,128)(2,1)}, bf16[128,2048]{1,0:T(8,128)(2,1)}, u32[]{:S(2)}, u32[]{:S(2)}) collective-permute-start(bf16[128,2048]{1,0:T(8,128)(2,1)} %pad_maximum_fusion.refs_4_), channel_id=1, source_target_pairs={{0,1},{1,0},{2,3},{3,2},{4,5},{5,4},{6,7},{7,6},{8,9},{9,8},{10,11... | collective-permute-start | bytes 1572872 | tf_op jit(solution)/shard_map/ppermute | solution.py:396
  38.2 13.0 %collective-permute-start.7 = (bf16[256,1024]{1,0:T(8,128)(2,1)}, bf16[256,1024]{1,0:T(8,128)(2,1)}, u32[]{:S(2)}, u32[]{:S(2)}) collective-permute-start(bf16[256,1024]{1,0:T(8,128)(2,1)} %collective-permute-done.6.refs_6_), channel_id=1, source_target_pairs={{0,8},{1,9},{2,10},{3,11},{4,0},{5,1},{6,2},{7,3},{8,12},{9,13},{1... | collective-permute-start | bytes 1572872 | tf_op jit(solution)/shard_map/ppermute | solution.py:396
  40.7 10.5 %collective-permute-start.8 = (bf16[256,1024]{1,0:T(8,128)(2,1)}, bf16[256,1024]{1,0:T(8,128)(2,1)}, u32[]{:S(2)}, u32[]{:S(2)}) collective-permute-start(bf16[256,1024]{1,0:T(8,128)(2,1)} %collective-permute-done.refs_4_), channel_id=1, source_target_pairs={{0,1},{1,0},{2,3},{3,2},{4,5},{5,4},{6,7},{7,6},{8,9},{9,8},{10,11... | collective-permute-start | bytes 1572872 | tf_op jit(solution)/shard_map/ppermute | solution.py:396
  53.4 25.8 %collective-permute-start.10 = (bf16[272,2048]{1,0:T(8,128)(2,1)}, bf16[272,2048]{1,0:T(8,128)(2,1)S(1)}, u32[]{:S(2)}, u32[]{:S(2)}) collective-permute-start(bf16[272,2048]{1,0:T(8,128)(2,1)} %get-tuple-element.132), channel_id=1, source_target_pairs={{0,18},{1,19},{2,16},{3,17},{4,22},{5,23},{6,20},{7,21},{8,26},{9,... | collective-permute-start | bytes 3342344 | tf_op jit(solution)/shard_map/ppermute | solution.py:396
  54.9 12.3 %collective-permute-start.11 = (bf16[128,2048]{1,0:T(8,128)(2,1)}, bf16[128,2048]{1,0:T(8,128)(2,1)S(1)}, u32[]{:S(2)}, u32[]{:S(2)}) collective-permute-start(bf16[128,2048]{1,0:T(8,128)(2,1)} %pad_maximum_fusion.refs_4_), channel_id=1, source_target_pairs={{0,8},{1,9},{2,10},{3,11},{4,0},{5,1},{6,2},{7,3},{8,12},{9,13},{1... | collective-permute-start | bytes 1572872 | tf_op jit(solution)/shard_map/ppermute | solution.py:396
  57.1 12.6 %collective-permute-start.13 = (bf16[256,1024]{1,0:T(8,128)(2,1)}, bf16[256,1024]{1,0:T(8,128)(2,1)S(1)}, u32[]{:S(2)}, u32[]{:S(2)}) collective-permute-start(bf16[256,1024]{1,0:T(8,128)(2,1)} %collective-permute-done.6.refs_6_), channel_id=1, source_target_pairs={{0,1},{1,0},{2,3},{3,2},{4,5},{5,4},{6,7},{7,6},{8,9},{9,8},{10,11... | collective-permute-start | bytes 1572872 | tf_op jit(solution)/shard_map/ppermute | solution.py:396
  57.1 13.1 %collective-permute-start.14 = (bf16[256,1024]{1,0:T(8,128)(2,1)}, bf16[256,1024]{1,0:T(8,128)(2,1)S(1)}, u32[]{:S(2)}, u32[]{:S(2)}) collective-permute-start(bf16[256,1024]{1,0:T(8,128)(2,1)} %collective-permute-done.7.refs_8_), channel_id=1, source_target_pairs={{0,1},{1,0},{2,3},{3,2},{4,5},{5,4},{6,7},{7,6},{8,9},{9,8},{10,11... | collective-permute-start | bytes 1572872 | tf_op jit(solution)/shard_map/ppermute | solution.py:396
  67.2 11.0 %collective-permute-start.12 = (bf16[128,2048]{1,0:T(8,128)(2,1)S(1)}, bf16[128,2048]{1,0:T(8,128)(2,1)S(1)}, u32[]{:S(2)}, u32[]{:S(2)}) collective-permute-start(bf16[128,2048]{1,0:T(8,128)(2,1)S(1)} %collective-permute-done.11.refs_6_), channel_id=1, source_target_pairs={{0,8},{1,9},{2,10},{3,11},{4,0},{5,1},{6,2},{7,3},{8,12},{9,13},{1... | collective-permute-start | bytes 1572872 | tf_op jit(solution)/shard_map/ppermute | solution.py:396
  79.2 18.7 %collective-permute-start.17 = (bf16[272,1024]{1,0:T(8,128)(2,1)S(1)}, bf16[272,1024]{1,0:T(8,128)(2,1)S(1)}, u32[]{:S(2)}, u32[]{:S(2)}) collective-permute-start(bf16[272,1024]{1,0:T(8,128)(2,1)S(1)} %get-tuple-element.147), channel_id=1, source_target_pairs={{0,16},{1,17},{2,18},{3,19},{4,20},{5,21},{6,22},{7,23},{8,24},{9,... | collective-permute-start | bytes 1671176 | tf_op jit(solution)/shard_map/ppermute | solution.py:396
  79.8 18.1 %collective-permute-start.18 = (bf16[272,1024]{1,0:T(8,128)(2,1)S(1)}, bf16[272,1024]{1,0:T(8,128)(2,1)S(1)}, u32[]{:S(2)}, u32[]{:S(2)}) collective-permute-start(bf16[272,1024]{1,0:T(8,128)(2,1)S(1)} %get-tuple-element.148), channel_id=1, source_target_pairs={{0,2},{1,3},{2,0},{3,1},{4,6},{5,7},{6,4},{7,5},{8,10},{9,11},{10,... | collective-permute-start | bytes 1671176 | tf_op jit(solution)/shard_map/ppermute | solution.py:396
  81.3 16.6 %collective-permute-start.19 = (bf16[128,2048]{1,0:T(8,128)(2,1)S(1)}, bf16[128,2048]{1,0:T(8,128)(2,1)S(1)}, u32[]{:S(2)}, u32[]{:S(2)}) collective-permute-start(bf16[128,2048]{1,0:T(8,128)(2,1)S(1)} %collective-permute-done.12.refs_8_), channel_id=1, source_target_pairs={{0,8},{1,9},{2,10},{3,11},{4,0},{5,1},{6,2},{7,3},{8,12},{9,13},{1... | collective-permute-start | bytes 1572872 | tf_op jit(solution)/shard_map/ppermute | solution.py:396
  83.6 14.3 %collective-permute-start.21 = (bf16[128,2048]{1,0:T(8,128)(2,1)S(1)}, bf16[128,2048]{1,0:T(8,128)(2,1)S(1)}, u32[]{:S(2)}, u32[]{:S(2)}) collective-permute-start(bf16[128,2048]{1,0:T(8,128)(2,1)S(1)} %collective-permute-done.12.refs_8_), channel_id=1, source_target_pairs={{0,1},{1,0},{2,3},{3,2},{4,5},{5,4},{6,7},{7,6},{8,9},{9,8},{10,11... | collective-permute-start | bytes 1572872 | tf_op jit(solution)/shard_map/ppermute | solution.py:396
  83.6 14.3 %collective-permute-start.20 = (bf16[128,1024]{1,0:T(8,128)(2,1)S(1)}, bf16[128,1024]{1,0:T(8,128)(2,1)}, u32[]{:S(2)}, u32[]{:S(2)}) collective-permute-start(bf16[128,1024]{1,0:T(8,128)(2,1)S(1)} %pad_maximum_fusion.1.refs_10_), channel_id=1, source_target_pairs={{0,8},{1,9},{2,10},{3,11},{4,0},{5,1},{6,2},{7,3},{8,12},{9,13},{1... | collective-permute-start | bytes 786440 | tf_op jit(solution)/shard_map/ppermute | solution.py:396
  98.0 13.4 %collective-permute-start.27 = (bf16[128,1024]{1,0:T(8,128)(2,1)S(1)}, bf16[128,1024]{1,0:T(8,128)(2,1)}, u32[]{:S(2)}, u32[]{:S(2)}) collective-permute-start(bf16[128,1024]{1,0:T(8,128)(2,1)S(1)} %pad_maximum_fusion.1.refs_10_), channel_id=1, source_target_pairs={{0,12},{1,13},{2,14},{3,15},{4,8},{5,9},{6,10},{7,11},{8,4},{9,5},... | collective-permute-start | bytes 786440 | tf_op jit(solution)/shard_map/ppermute | solution.py:396
  99.9 18.9 %collective-permute-start.28 = (bf16[128,1024]{1,0:T(8,128)(2,1)S(1)}, bf16[128,1024]{1,0:T(8,128)(2,1)}, u32[]{:S(2)}, u32[]{:S(2)}) collective-permute-start(bf16[128,1024]{1,0:T(8,128)(2,1)S(1)} %pad_maximum_fusion.1.refs_10_), channel_id=1, source_target_pairs={{0,4},{1,5},{2,6},{3,7},{4,12},{5,13},{6,14},{7,15},{8,0},{9,1},{1... | collective-permute-start | bytes 786440 | tf_op jit(solution)/shard_map/ppermute | solution.py:396
  100.8 20.3 %collective-permute-start.22 = (bf16[272,1024]{1,0:T(8,128)(2,1)}, bf16[272,1024]{1,0:T(8,128)(2,1)}, u32[]{:S(2)}, u32[]{:S(2)}) collective-permute-start(bf16[272,1024]{1,0:T(8,128)(2,1)} %get-tuple-element.171._), channel_id=1, source_target_pairs={{0,18},{1,19},{2,16},{3,17},{4,22},{5,23},{6,20},{7,21},{8,26},{9,... | collective-permute-start | bytes 1671176 | tf_op jit(solution)/shard_map/ppermute | solution.py:396
  109.3 9.5 %collective-permute-start.24 = (f32[64,128]{1,0:T(8,128)S(1)}, f32[64,128]{1,0:T(8,128)S(1)}, u32[]{:S(2)}, u32[]{:S(2)}) collective-permute-start(f32[64,128]{1,0:T(8,128)S(1)} %get-tuple-element.181), channel_id=1, source_target_pairs={{0,16},{1,17},{2,18},{3,19},{4,20},{5,21},{6,22},{7,23},{8,24},{9,... | collective-permute-start | bytes 98312 | tf_op jit(solution)/shard_map/ppermute | solution.py:396
  (27 other events, 345.1 us)

commit v6 on v5

--- a/solution.py
+++ b/solution.py
@@ -435,10 +435,10 @@
         sides,
         pad,
     )
-    downs = [paired(downs[0], down_far)]
-    ups = [paired(up, up_far)]
     base_parts = both(bases[0])
-    bases, downs, ups, messages, base_parts = phase(bases, downs, ups, messages, base_parts)
+    bases, downs, down_far, up, up_far, messages, base_parts = phase(
+        bases, downs, down_far, up, up_far, messages, base_parts
+    )
     near = [send(messages[m], flips[m]) for m in (1, 2)]
     message = messages[0]
 
@@ -446,6 +446,8 @@
     bases, queries = phase(bases, queries)
     while len(bases) < planes:
         bases.append(send(bases[-1], ring))
+    downs = [paired(downs[0], down_far)]
+    ups = [paired(up, up_far)]
     for held in bases[1:2]:
         base_parts = base_parts + both(held)
 

time: 128 us -> 126 us (0.984)
  waiting for transfers between devices: 46.5 us -> 43.9 us
  local copies, waits for them, and re-layouts: 7.92 us -> 10.5 us
  other arithmetic: 3.88 us -> 2.48 us
    ppermute x32, waiting for transfers between devices: 46.5 us -> 43.9 us  [send(): return lax.ppermute(value, BOTH, pairs)]
    concatenate x2 -> x1, other arithmetic: 2.98 us -> 0.92 us  [paired(): return near if far is None else jnp.concatenate([near, far], axis=0)]
    concatenate x0 -> x1, local copies, waits for them, and re-layouts: none -> 1.67 us  [paired(): return near if far is None else jnp.concatenate([near, far], axis=0)]
    unnamed x38 -> x33, local copies, waits for them, and re-layouts: 2.95 us -> 3.14 us
  transfers between devices with their start and end apart: 32 -> 32, of which waited for: 12 -> 12; matrix products, arithmetic and copies ran while one was open for 7% -> 8% of each run, Pallas kernels for 21% -> 22%
where the time goes in v6:
time: 126 us; the launch traced here: 125 us
  waiting for transfers between devices  43.9 us (35%)
  Pallas kernels  33.1 us (26%)
  starting transfers between devices  32.5 us (26%)
  local copies, waits for them, and re-layouts  10.5 us (8%)
  other arithmetic  2.48 us (2%)
  matrix products  1.98 us (2%)
    ppermute x32, waiting for transfers between devices, send(): return lax.ppermute(value, BOTH, pairs)  43.9 us
    ppermute x32, starting transfers between devices, send(): return lax.ppermute(value, BOTH, pairs)  32.5 us
    pallas_call x2, Pallas kernels, base_products(): pl.pallas_call(kernel, grid_spec=pltpu.PrefetchScalarGridSpec(num_scalar_...  12.7 us
    pallas_call x1, Pallas kernels, lowered_products(): pl.pallas_call(kernel, grid=(1,), in_specs=[pl.BlockSpec(memory_space=pl....  6.59 us
    pallas_call x1, Pallas kernels, split_columns(): pl.pallas_call(kernel, grid_spec=pltpu.PrefetchScalarGridSpec(num_scalar_...  5.5 us
    pallas_call x1, Pallas kernels, finish(): pl.pallas_call(kernel, grid=(out_width // cut,), in_specs=[pl.BlockSpec(p...  5.5 us
    unnamed x33, local copies, waits for them, and re-layouts  3.14 us
    pallas_call x1, Pallas kernels, split_down(): pl.pallas_call(kernel, grid_spec=pltpu.PrefetchScalarGridSpec(num_scalar_...  2.73 us
  transfers between devices with their start and end apart: 32, of which 12 were waited for; matrix products, arithmetic and copies ran while one was open for 8% of the time, Pallas kernels for 22%

profile of v6, /device:TPU:0, one launch (start us, length us, event | category | flops | bytes accessed | tf_op | source)
XLA Modules:
  0.0 125.3 jit_solution(16834331071304694435)
XLA Ops:
  1.2 2.2 %constant_dynamic-slice_fusion.refs_2_ = bf16[256,1024]{1,0:T(8,128)(2,1)} fusion(bf16[512,1024]{1,0:T(8,128)(2,1)} %param.19, s32[]{:T(128)S(6)} %select_n.107), kind=kLoop, calls=%fused_computation.83 | loop fusion | bytes 1048580 | tf_op jit(solution)/shard_map/dynamic_slice | solution.py:417
  3.4 4.0 %collective-permute-start = (bf16[256,1024]{1,0:T(8,128)(2,1)}, bf16[256,1024]{1,0:T(8,128)(2,1)}, u32[]{:S(2)}, u32[]{:S(2)}) collective-permute-start(bf16[256,1024]{1,0:T(8,128)(2,1)} %constant_dynamic-slice_fusion.refs_2_), channel_id=1, source_target_pairs={{0,8},{1,9},{2,10},{3,11},{4,0},{5,1},{6,2},{7,3},{8,12},{9,13},{1... | collective-permute-start | bytes 1572872 | tf_op jit(solution)/shard_map/ppermute | solution.py:396
  7.4 2.7 %split_down.1 = (bf16[64,2048]{1,0:T(8,128)(2,1)}, bf16[64,2048]{1,0:T(8,128)(2,1)}) custom-call(s32[2]{0:T(128)} %pad_add_fusion.here, bf16[64,8192]{1,0:T(8,128)(2,1)} %bitcast.49), custom_call_target="tpu_custom_call" | custom-call | bytes 2097152 | tf_op jit(solution)/shard_map/split_down/pallas_call | solution.py:49
  10.2 1.5 %collective-permute-start.1 = (bf16[64,2048]{1,0:T(8,128)(2,1)}, bf16[64,2048]{1,0:T(8,128)(2,1)}, u32[]{:S(2)}, u32[]{:S(2)}) collective-permute-start(bf16[64,2048]{1,0:T(8,128)(2,1)} %get-tuple-element.116), channel_id=1, source_target_pairs={{0,2},{1,3},{2,0},{3,1},{4,6},{5,7},{6,4},{7,5},{8,10},{9,11},{10,... | collective-permute-start | bytes 786440 | tf_op jit(solution)/shard_map/ppermute | solution.py:396
  13.9 5.5 %split_columns.1 = (bf16[272,2048]{1,0:T(8,128)(2,1)}, bf16[272,2048]{1,0:T(8,128)(2,1)}, bf16[272,2048]{1,0:T(8,128)(2,1)}, bf16[272,2048]{1,0:T(8,128)(2,1)}) custom-call(s32[2]{0:T(128)} %pad_add_fusion.here, s32[32]{0:T(128)} %own.1, bf16[256,8192]{1,0:T(8,128)(2,1)} %pre.1, bf16[8,8192]{1,0:T(8,128)(2,1)} %dcd.1, s32[1,256]{1,0:T(1,128)} %bitcast.57), custom_call_target="tpu_custom_call" | custom-call | bytes 9437184 | tf_op jit(solution)/shard_map/split_columns/pallas_call | solution.py:102
  19.4 2.6 %collective-permute-done.2 = bf16[64,1024]{1,0:T(8,128)(2,1)} collective-permute-done((bf16[64,1024]{1,0:T(8,128)(2,1)}, bf16[64,1024]{1,0:T(8,128)(2,1)}, u32[]{:S(2)}, u32[]{:S(2)}) %collective-permute-start.2) | collective-permute-done | bytes 131104 | tf_op jit(solution)/shard_map/ppermute | solution.py:396
  22.0 1.6 %collective-permute-start.6 = (bf16[256,1024]{1,0:T(8,128)(2,1)}, bf16[256,1024]{1,0:T(8,128)(2,1)}, u32[]{:S(2)}, u32[]{:S(2)}) collective-permute-start(bf16[256,1024]{1,0:T(8,128)(2,1)} %collective-permute-done.refs_4_), channel_id=1, source_target_pairs={{0,8},{1,9},{2,10},{3,11},{4,0},{5,1},{6,2},{7,3},{8,12},{9,13},{1... | collective-permute-start | bytes 1572872 | tf_op jit(solution)/shard_map/ppermute | solution.py:396
  25.1 1.5 %collective-permute-start.5 = (bf16[272,2048]{1,0:T(8,128)(2,1)}, bf16[272,2048]{1,0:T(8,128)(2,1)}, u32[]{:S(2)}, u32[]{:S(2)}) collective-permute-start(bf16[272,2048]{1,0:T(8,128)(2,1)} %get-tuple-element.124), channel_id=1, source_target_pairs={{0,2},{1,3},{2,0},{3,1},{4,6},{5,7},{6,4},{7,5},{8,10},{9,11},{10,... | collective-permute-start | bytes 3342344 | tf_op jit(solution)/shard_map/ppermute | solution.py:396
  27.4 1.7 %constant_dynamic-update-slice_fusion.refs_4_ = bf16[128,2048]{1,0:T(8,128)(2,1)} fusion(bf16[128,2048]{1,0:T(8,128)(2,1)} %constant_dynamic-update-slice_fusion.1, bf16[64,2048]{1,0:T(8,128)(2,1)} %collective-permute-done.1), kind=kLoop, calls=%fused_computation.16 | loop fusion | bytes 524288 | tf_op jit(solution)/shard_map/concatenate | solution.py:415
  30.0 5.9 %collective-permute-done.6.refs_6_ = bf16[256,1024]{1,0:T(8,128)(2,1)} collective-permute-done((bf16[256,1024]{1,0:T(8,128)(2,1)}, bf16[256,1024]{1,0:T(8,128)(2,1)}, u32[]{:S(2)}, u32[]{:S(2)}) %collective-permute-start.6) | collective-permute-done | bytes 524320 | tf_op jit(solution)/shard_map/ppermute | solution.py:396
  35.9 2.5 %collective-permute-start.7 = (bf16[256,1024]{1,0:T(8,128)(2,1)}, bf16[256,1024]{1,0:T(8,128)(2,1)}, u32[]{:S(2)}, u32[]{:S(2)}) collective-permute-start(bf16[256,1024]{1,0:T(8,128)(2,1)} %collective-permute-done.6.refs_6_), channel_id=1, source_target_pairs={{0,8},{1,9},{2,10},{3,11},{4,0},{5,1},{6,2},{7,3},{8,12},{9,13},{1... | collective-permute-start | bytes 1572872 | tf_op jit(solution)/shard_map/ppermute | solution.py:396
  41.7 7.2 %collective-permute-done.7.refs_8_ = bf16[256,1024]{1,0:T(8,128)(2,1)} collective-permute-done((bf16[256,1024]{1,0:T(8,128)(2,1)}, bf16[256,1024]{1,0:T(8,128)(2,1)}, u32[]{:S(2)}, u32[]{:S(2)}) %collective-permute-start.7) | collective-permute-done | bytes 524320 | tf_op jit(solution)/shard_map/ppermute | solution.py:396
  52.6 2.3 %collective-permute-start.11 = (bf16[128,2048]{1,0:T(8,128)(2,1)}, bf16[128,2048]{1,0:T(8,128)(2,1)S(1)}, u32[]{:S(2)}, u32[]{:S(2)}) collective-permute-start(bf16[128,2048]{1,0:T(8,128)(2,1)} %constant_dynamic-update-slice_fusion.refs_4_), channel_id=1, source_target_pairs={{0,8},{1,9},{2,10},{3,11},{4,0},{5,1},{6,2},{7,3},{8,12},{9,13},{1... | collective-permute-start | bytes 1572872 | tf_op jit(solution)/shard_map/ppermute | solution.py:396
  55.4 9.5 %collective-permute-done.11.refs_6_ = bf16[128,2048]{1,0:T(8,128)(2,1)S(1)} collective-permute-done((bf16[128,2048]{1,0:T(8,128)(2,1)}, bf16[128,2048]{1,0:T(8,128)(2,1)S(1)}, u32[]{:S(2)}, u32[]{:S(2)}) %collective-permute-start.11) | collective-permute-done | bytes 524320 | tf_op jit(solution)/shard_map/ppermute | solution.py:396
  64.9 2.5 %collective-permute-start.12 = (bf16[128,2048]{1,0:T(8,128)(2,1)S(1)}, bf16[128,2048]{1,0:T(8,128)(2,1)S(1)}, u32[]{:S(2)}, u32[]{:S(2)}) collective-permute-start(bf16[128,2048]{1,0:T(8,128)(2,1)S(1)} %collective-permute-done.11.refs_6_), channel_id=1, source_target_pairs={{0,8},{1,9},{2,10},{3,11},{4,0},{5,1},{6,2},{7,3},{8,12},{9,13},{1... | collective-permute-start | bytes 1572872 | tf_op jit(solution)/shard_map/ppermute | solution.py:396
  67.9 6.5 %base_products.2 = (bf16[272,1024]{1,0:T(8,128)(2,1)S(1)}, bf16[272,1024]{1,0:T(8,128)(2,1)S(1)}) custom-call(s32[8]{0:T(128)S(1)} %fusion.21.spot, bf16[272,2048]{1,0:T(8,128)(2,1)} %collective-permute-done.4.refs_0_.refs_1_, bf16[272,2048]{1,0:T(8,128)(2,1)} %collective-permute-done.5.refs_1_.refs_2_, ...), custom_call_target="tpu_custom_call" | custom-call | flops 2281701376 | bytes 6422528 | tf_op jit(solution)/shard_map/base_products/pallas_call | solution.py:146
  79.0 2.3 %collective-permute-start.19 = (bf16[128,2048]{1,0:T(8,128)(2,1)S(1)}, bf16[128,2048]{1,0:T(8,128)(2,1)S(1)}, u32[]{:S(2)}, u32[]{:S(2)}) collective-permute-start(bf16[128,2048]{1,0:T(8,128)(2,1)S(1)} %collective-permute-done.12.refs_8_), channel_id=1, source_target_pairs={{0,8},{1,9},{2,10},{3,11},{4,0},{5,1},{6,2},{7,3},{8,12},{9,13},{1... | collective-permute-start | bytes 1572872 | tf_op jit(solution)/shard_map/ppermute | solution.py:396
  81.3 6.3 %base_products.3 = (bf16[272,1024]{1,0:T(8,128)(2,1)}, f32[272,1024]{1,0:T(8,128)S(1)}) custom-call(s32[8]{0:T(128)S(1)} %fusion.21.spot, bf16[272,2048]{1,0:T(8,128)(2,1)S(1)} %collective-permute-done.10.refs_0_.refs_3_, bf16[272,2048]{1,0:T(8,128)(2,1)S(1)} %copy-done.2, bf16[256,1024]{1,0:T(8,128)(2,1)} %constant_dynamic-slice_fusion.refs_2_, ...), custom_call_target="tpu_custom_call" | custom-call | flops 2281701376 | bytes 6422528 | tf_op jit(solution)/shard_map/base_products/pallas_call | solution.py:146
  88.6 6.8 %collective-permute-done.20.refs_11_ = bf16[128,1024]{1,0:T(8,128)(2,1)} collective-permute-done((bf16[128,1024]{1,0:T(8,128)(2,1)S(1)}, bf16[128,1024]{1,0:T(8,128)(2,1)}, u32[]{:S(2)}, u32[]{:S(2)}) %collective-permute-start.20) | collective-permute-done | bytes 262176 | tf_op jit(solution)/shard_map/ppermute | solution.py:396
  96.8 1.7 %collective-permute-start.28 = (bf16[128,1024]{1,0:T(8,128)(2,1)S(1)}, bf16[128,1024]{1,0:T(8,128)(2,1)}, u32[]{:S(2)}, u32[]{:S(2)}) collective-permute-start(bf16[128,1024]{1,0:T(8,128)(2,1)S(1)} %pad_maximum_fusion.refs_10_), channel_id=1, source_target_pairs={{0,4},{1,5},{2,6},{3,7},{4,12},{5,13},{6,14},{7,15},{8,0},{9,1},{1... | collective-permute-start | bytes 786440 | tf_op jit(solution)/shard_map/ppermute | solution.py:396
  99.0 6.6 %lowered_products.1 = (f32[64,128]{1,0:T(8,128)S(1)}, f32[64,128]{1,0:T(8,128)S(1)}, f32[64,128]{1,0:T(8,128)S(1)}, f32[64,128]{1,0:T(8,128)S(1)}) custom-call(bf16[272,1024]{1,0:T(8,128)(2,1)} %get-tuple-element.175._, bf16[272,2048]{1,0:T(8,128)(2,1)S(1)} %copy-done.2, bf16[272,2048]{1,0:T(8,128)(2,1)} %collective-permute-done.4.refs_0_.refs_1_, ...), custom_call_target="tpu_custom_call" | custom-call | flops 4294967296 | bytes 8388608 | tf_op jit(solution)/shard_map/lowered_products/pallas_call | solution.py:219
  107.7 1.5 %collective-permute-start.25 = (f32[64,128]{1,0:T(8,128)S(1)}, f32[64,128]{1,0:T(8,128)S(1)}, u32[]{:S(2)}, u32[]{:S(2)}) collective-permute-start(f32[64,128]{1,0:T(8,128)S(1)} %get-tuple-element.186), channel_id=1, source_target_pairs={{0,2},{1,3},{2,0},{3,1},{4,6},{5,7},{6,4},{7,5},{8,10},{9,11},{10,... | collective-permute-start | bytes 98312 | tf_op jit(solution)/shard_map/ppermute | solution.py:396
  109.7 6.6 %collective-permute-done.28.refs_13_ = bf16[128,1024]{1,0:T(8,128)(2,1)} collective-permute-done((bf16[128,1024]{1,0:T(8,128)(2,1)S(1)}, bf16[128,1024]{1,0:T(8,128)(2,1)}, u32[]{:S(2)}, u32[]{:S(2)}) %collective-permute-start.28) | collective-permute-done | bytes 262176 | tf_op jit(solution)/shard_map/ppermute | solution.py:396
  119.8 5.5 %finish.1 = (bf16[256,1024]{1,0:T(8,128)(2,1)}, bf16[8,4096]{1,0:T(8,128)(2,1)}) custom-call(f32[64,128]{1,0:T(8,128)} %copy-done.3, f32[64,128]{1,0:T(8,128)} %copy-done.13, f32[64,128]{1,0:T(8,128)} %copy-done.14, f32[64,128]{1,0:T(8,128)} %copy-done.15, bf16[272,2048]{1,0:T(8,128)(2,1)} %get-tuple-element.156.refs_1_.refs_0_.refs_4_, ...), custom_call_target="tpu_custom_call" | custom-call | flops 536870912 | bytes 5242880 | tf_op jit(solution)/shard_map/finish/pallas_call | solution.py:323
  (100 shorter events, 27.4 us)
Async XLA Ops:
  3.4 18.6 %collective-permute-start = (bf16[256,1024]{1,0:T(8,128)(2,1)}, bf16[256,1024]{1,0:T(8,128)(2,1)}, u32[]{:S(2)}, u32[]{:S(2)}) collective-permute-start(bf16[256,1024]{1,0:T(8,128)(2,1)} %constant_dynamic-slice_fusion.refs_2_), channel_id=1, source_target_pairs={{0,8},{1,9},{2,10},{3,11},{4,0},{5,1},{6,2},{7,3},{8,12},{9,13},{1... | collective-permute-start | bytes 1572872 | tf_op jit(solution)/shard_map/ppermute | solution.py:396
  7.4 14.6 %collective-permute-start.3 = (bf16[256,1024]{1,0:T(8,128)(2,1)}, bf16[256,1024]{1,0:T(8,128)(2,1)}, u32[]{:S(2)}, u32[]{:S(2)}) collective-permute-start(bf16[256,1024]{1,0:T(8,128)(2,1)} %constant_dynamic-slice_fusion.refs_2_), channel_id=1, source_target_pairs={{0,1},{1,0},{2,3},{3,2},{4,5},{5,4},{6,7},{7,6},{8,9},{9,8},{10,11... | collective-permute-start | bytes 1572872 | tf_op jit(solution)/shard_map/ppermute | solution.py:396
  10.2 11.8 %collective-permute-start.1 = (bf16[64,2048]{1,0:T(8,128)(2,1)}, bf16[64,2048]{1,0:T(8,128)(2,1)}, u32[]{:S(2)}, u32[]{:S(2)}) collective-permute-start(bf16[64,2048]{1,0:T(8,128)(2,1)} %get-tuple-element.116), channel_id=1, source_target_pairs={{0,2},{1,3},{2,0},{3,1},{4,6},{5,7},{6,4},{7,5},{8,10},{9,11},{10,... | collective-permute-start | bytes 786440 | tf_op jit(solution)/shard_map/ppermute | solution.py:396
  11.7 10.3 %collective-permute-start.2 = (bf16[64,1024]{1,0:T(8,128)(2,1)}, bf16[64,1024]{1,0:T(8,128)(2,1)}, u32[]{:S(2)}, u32[]{:S(2)}) collective-permute-start(bf16[64,1024]{1,0:T(8,128)(2,1)} %bitcast.54), channel_id=1, source_target_pairs={{0,2},{1,3},{2,0},{3,1},{4,6},{5,7},{6,4},{7,5},{8,10},{9,11},{10,... | collective-permute-start | bytes 393224 | tf_op jit(solution)/shard_map/ppermute | solution.py:396
  22.0 13.9 %collective-permute-start.6 = (bf16[256,1024]{1,0:T(8,128)(2,1)}, bf16[256,1024]{1,0:T(8,128)(2,1)}, u32[]{:S(2)}, u32[]{:S(2)}) collective-permute-start(bf16[256,1024]{1,0:T(8,128)(2,1)} %collective-permute-done.refs_4_), channel_id=1, source_target_pairs={{0,8},{1,9},{2,10},{3,11},{4,0},{5,1},{6,2},{7,3},{8,12},{9,13},{1... | collective-permute-start | bytes 1572872 | tf_op jit(solution)/shard_map/ppermute | solution.py:396
  23.7 26.2 %collective-permute-start.4 = (bf16[272,2048]{1,0:T(8,128)(2,1)}, bf16[272,2048]{1,0:T(8,128)(2,1)}, u32[]{:S(2)}, u32[]{:S(2)}) collective-permute-start(bf16[272,2048]{1,0:T(8,128)(2,1)} %get-tuple-element.123), channel_id=1, source_target_pairs={{0,16},{1,17},{2,18},{3,19},{4,20},{5,21},{6,22},{7,23},{8,24},{9,... | collective-permute-start | bytes 3342344 | tf_op jit(solution)/shard_map/ppermute | solution.py:396
  25.1 25.9 %collective-permute-start.5 = (bf16[272,2048]{1,0:T(8,128)(2,1)}, bf16[272,2048]{1,0:T(8,128)(2,1)}, u32[]{:S(2)}, u32[]{:S(2)}) collective-permute-start(bf16[272,2048]{1,0:T(8,128)(2,1)} %get-tuple-element.124), channel_id=1, source_target_pairs={{0,2},{1,3},{2,0},{3,1},{4,6},{5,7},{6,4},{7,5},{8,10},{9,11},{10,... | collective-permute-start | bytes 3342344 | tf_op jit(solution)/shard_map/ppermute | solution.py:396
  29.1 12.7 %collective-permute-start.9 = (bf16[128,2048]{1,0:T(8,128)(2,1)}, bf16[128,2048]{1,0:T(8,128)(2,1)}, u32[]{:S(2)}, u32[]{:S(2)}) collective-permute-start(bf16[128,2048]{1,0:T(8,128)(2,1)} %constant_dynamic-update-slice_fusion.refs_4_), channel_id=1, source_target_pairs={{0,1},{1,0},{2,3},{3,2},{4,5},{5,4},{6,7},{7,6},{8,9},{9,8},{10,11... | collective-permute-start | bytes 1572872 | tf_op jit(solution)/shard_map/ppermute | solution.py:396
  35.9 13.0 %collective-permute-start.7 = (bf16[256,1024]{1,0:T(8,128)(2,1)}, bf16[256,1024]{1,0:T(8,128)(2,1)}, u32[]{:S(2)}, u32[]{:S(2)}) collective-permute-start(bf16[256,1024]{1,0:T(8,128)(2,1)} %collective-permute-done.6.refs_6_), channel_id=1, source_target_pairs={{0,8},{1,9},{2,10},{3,11},{4,0},{5,1},{6,2},{7,3},{8,12},{9,13},{1... | collective-permute-start | bytes 1572872 | tf_op jit(solution)/shard_map/ppermute | solution.py:396
  38.4 10.5 %collective-permute-start.8 = (bf16[256,1024]{1,0:T(8,128)(2,1)}, bf16[256,1024]{1,0:T(8,128)(2,1)}, u32[]{:S(2)}, u32[]{:S(2)}) collective-permute-start(bf16[256,1024]{1,0:T(8,128)(2,1)} %collective-permute-done.refs_4_), channel_id=1, source_target_pairs={{0,1},{1,0},{2,3},{3,2},{4,5},{5,4},{6,7},{7,6},{8,9},{9,8},{10,11... | collective-permute-start | bytes 1572872 | tf_op jit(solution)/shard_map/ppermute | solution.py:396
  51.1 25.8 %collective-permute-start.10 = (bf16[272,2048]{1,0:T(8,128)(2,1)}, bf16[272,2048]{1,0:T(8,128)(2,1)S(1)}, u32[]{:S(2)}, u32[]{:S(2)}) collective-permute-start(bf16[272,2048]{1,0:T(8,128)(2,1)} %get-tuple-element.136), channel_id=1, source_target_pairs={{0,18},{1,19},{2,16},{3,17},{4,22},{5,23},{6,20},{7,21},{8,26},{9,... | collective-permute-start | bytes 3342344 | tf_op jit(solution)/shard_map/ppermute | solution.py:396
  52.6 12.3 %collective-permute-start.11 = (bf16[128,2048]{1,0:T(8,128)(2,1)}, bf16[128,2048]{1,0:T(8,128)(2,1)S(1)}, u32[]{:S(2)}, u32[]{:S(2)}) collective-permute-start(bf16[128,2048]{1,0:T(8,128)(2,1)} %constant_dynamic-update-slice_fusion.refs_4_), channel_id=1, source_target_pairs={{0,8},{1,9},{2,10},{3,11},{4,0},{5,1},{6,2},{7,3},{8,12},{9,13},{1... | collective-permute-start | bytes 1572872 | tf_op jit(solution)/shard_map/ppermute | solution.py:396
  54.8 12.6 %collective-permute-start.13 = (bf16[256,1024]{1,0:T(8,128)(2,1)}, bf16[256,1024]{1,0:T(8,128)(2,1)S(1)}, u32[]{:S(2)}, u32[]{:S(2)}) collective-permute-start(bf16[256,1024]{1,0:T(8,128)(2,1)} %collective-permute-done.6.refs_6_), channel_id=1, source_target_pairs={{0,1},{1,0},{2,3},{3,2},{4,5},{5,4},{6,7},{7,6},{8,9},{9,8},{10,11... | collective-permute-start | bytes 1572872 | tf_op jit(solution)/shard_map/ppermute | solution.py:396
  54.8 13.1 %collective-permute-start.14 = (bf16[256,1024]{1,0:T(8,128)(2,1)}, bf16[256,1024]{1,0:T(8,128)(2,1)S(1)}, u32[]{:S(2)}, u32[]{:S(2)}) collective-permute-start(bf16[256,1024]{1,0:T(8,128)(2,1)} %collective-permute-done.7.refs_8_), channel_id=1, source_target_pairs={{0,1},{1,0},{2,3},{3,2},{4,5},{5,4},{6,7},{7,6},{8,9},{9,8},{10,11... | collective-permute-start | bytes 1572872 | tf_op jit(solution)/shard_map/ppermute | solution.py:396
  64.9 11.0 %collective-permute-start.12 = (bf16[128,2048]{1,0:T(8,128)(2,1)S(1)}, bf16[128,2048]{1,0:T(8,128)(2,1)S(1)}, u32[]{:S(2)}, u32[]{:S(2)}) collective-permute-start(bf16[128,2048]{1,0:T(8,128)(2,1)S(1)} %collective-permute-done.11.refs_6_), channel_id=1, source_target_pairs={{0,8},{1,9},{2,10},{3,11},{4,0},{5,1},{6,2},{7,3},{8,12},{9,13},{1... | collective-permute-start | bytes 1572872 | tf_op jit(solution)/shard_map/ppermute | solution.py:396
  76.9 18.4 %collective-permute-start.17 = (bf16[272,1024]{1,0:T(8,128)(2,1)S(1)}, bf16[272,1024]{1,0:T(8,128)(2,1)S(1)}, u32[]{:S(2)}, u32[]{:S(2)}) collective-permute-start(bf16[272,1024]{1,0:T(8,128)(2,1)S(1)} %get-tuple-element.151), channel_id=1, source_target_pairs={{0,16},{1,17},{2,18},{3,19},{4,20},{5,21},{6,22},{7,23},{8,24},{9,... | collective-permute-start | bytes 1671176 | tf_op jit(solution)/shard_map/ppermute | solution.py:396
  77.5 17.9 %collective-permute-start.18 = (bf16[272,1024]{1,0:T(8,128)(2,1)S(1)}, bf16[272,1024]{1,0:T(8,128)(2,1)S(1)}, u32[]{:S(2)}, u32[]{:S(2)}) collective-permute-start(bf16[272,1024]{1,0:T(8,128)(2,1)S(1)} %get-tuple-element.152), channel_id=1, source_target_pairs={{0,2},{1,3},{2,0},{3,1},{4,6},{5,7},{6,4},{7,5},{8,10},{9,11},{10,... | collective-permute-start | bytes 1671176 | tf_op jit(solution)/shard_map/ppermute | solution.py:396
  79.0 16.3 %collective-permute-start.19 = (bf16[128,2048]{1,0:T(8,128)(2,1)S(1)}, bf16[128,2048]{1,0:T(8,128)(2,1)S(1)}, u32[]{:S(2)}, u32[]{:S(2)}) collective-permute-start(bf16[128,2048]{1,0:T(8,128)(2,1)S(1)} %collective-permute-done.12.refs_8_), channel_id=1, source_target_pairs={{0,8},{1,9},{2,10},{3,11},{4,0},{5,1},{6,2},{7,3},{8,12},{9,13},{1... | collective-permute-start | bytes 1572872 | tf_op jit(solution)/shard_map/ppermute | solution.py:396
  81.3 14.1 %collective-permute-start.21 = (bf16[128,2048]{1,0:T(8,128)(2,1)S(1)}, bf16[128,2048]{1,0:T(8,128)(2,1)S(1)}, u32[]{:S(2)}, u32[]{:S(2)}) collective-permute-start(bf16[128,2048]{1,0:T(8,128)(2,1)S(1)} %collective-permute-done.12.refs_8_), channel_id=1, source_target_pairs={{0,1},{1,0},{2,3},{3,2},{4,5},{5,4},{6,7},{7,6},{8,9},{9,8},{10,11... | collective-permute-start | bytes 1572872 | tf_op jit(solution)/shard_map/ppermute | solution.py:396
  81.3 14.0 %collective-permute-start.20 = (bf16[128,1024]{1,0:T(8,128)(2,1)S(1)}, bf16[128,1024]{1,0:T(8,128)(2,1)}, u32[]{:S(2)}, u32[]{:S(2)}) collective-permute-start(bf16[128,1024]{1,0:T(8,128)(2,1)S(1)} %pad_maximum_fusion.refs_10_), channel_id=1, source_target_pairs={{0,8},{1,9},{2,10},{3,11},{4,0},{5,1},{6,2},{7,3},{8,12},{9,13},{1... | collective-permute-start | bytes 786440 | tf_op jit(solution)/shard_map/ppermute | solution.py:396
  95.5 13.8 %collective-permute-start.27 = (bf16[128,1024]{1,0:T(8,128)(2,1)S(1)}, bf16[128,1024]{1,0:T(8,128)(2,1)}, u32[]{:S(2)}, u32[]{:S(2)}) collective-permute-start(bf16[128,1024]{1,0:T(8,128)(2,1)S(1)} %pad_maximum_fusion.refs_10_), channel_id=1, source_target_pairs={{0,12},{1,13},{2,14},{3,15},{4,8},{5,9},{6,10},{7,11},{8,4},{9,5},... | collective-permute-start | bytes 786440 | tf_op jit(solution)/shard_map/ppermute | solution.py:396
  96.8 19.5 %collective-permute-start.28 = (bf16[128,1024]{1,0:T(8,128)(2,1)S(1)}, bf16[128,1024]{1,0:T(8,128)(2,1)}, u32[]{:S(2)}, u32[]{:S(2)}) collective-permute-start(bf16[128,1024]{1,0:T(8,128)(2,1)S(1)} %pad_maximum_fusion.refs_10_), channel_id=1, source_target_pairs={{0,4},{1,5},{2,6},{3,7},{4,12},{5,13},{6,14},{7,15},{8,0},{9,1},{1... | collective-permute-start | bytes 786440 | tf_op jit(solution)/shard_map/ppermute | solution.py:396
  98.5 20.5 %collective-permute-start.22 = (bf16[272,1024]{1,0:T(8,128)(2,1)}, bf16[272,1024]{1,0:T(8,128)(2,1)}, u32[]{:S(2)}, u32[]{:S(2)}) collective-permute-start(bf16[272,1024]{1,0:T(8,128)(2,1)} %get-tuple-element.175._), channel_id=1, source_target_pairs={{0,18},{1,19},{2,16},{3,17},{4,22},{5,23},{6,20},{7,21},{8,26},{9,... | collective-permute-start | bytes 1671176 | tf_op jit(solution)/shard_map/ppermute | solution.py:396
  106.2 10.1 %collective-permute-start.24 = (f32[64,128]{1,0:T(8,128)S(1)}, f32[64,128]{1,0:T(8,128)S(1)}, u32[]{:S(2)}, u32[]{:S(2)}) collective-permute-start(f32[64,128]{1,0:T(8,128)S(1)} %get-tuple-element.185), channel_id=1, source_target_pairs={{0,16},{1,17},{2,18},{3,19},{4,20},{5,21},{6,22},{7,23},{8,24},{9,... | collective-permute-start | bytes 98312 | tf_op jit(solution)/shard_map/ppermute | solution.py:396
  (24 other events, 286.4 us)
